TPU v7x, 32 devices: a whole 2x2x4 slice. The times are simulated.
32 devices in a mesh: dp: 4 (over y, core), space: 8 (over z, x).
Axes of the slice: x: 2, y: 2, z: 4, core: 2. Of those that a mesh axis runs over, the one named last changes fastest.
Arguments:
- features: bfloat16 [4, 8, 48, 512], P('dp', 'space'), may hold values from -6 to 6
- device_block: int32 [4, 8], P('dp'), may hold values from 0 to 15, as said below
- conv_first: bfloat16 [48, 27, 48], replicated, may hold values from -0.15625 to 0.15625
- conv_second: bfloat16 [48, 27, 48], replicated, may hold values from -0.15625 to 0.15625
- head_weight: bfloat16 [3, 48], replicated, may hold values from -0.875 to 0.875
- targets: int32 [4, 8, 3, 512], P('dp', 'space'), may hold values 0 or 1
Outputs:
- affinity_logits: float32 [4, 8, 3, 512], P('dp', 'space')
- grad_first: float32 [48, 27, 48], replicated
- grad_second: float32 [48, 27, 48], replicated
- grad_head: float32 [3, 48], replicated
Inputs may be any that keep to these rules, and one draw needn't show every extreme that they name: `device_block`: row n lists 8 distinct block ids of crop n, one for each device; id = (4 * bx + by) + bz. Blocks that no device lists hold no tissue.
All inputs are finite; a program needn't handle non-finite values. No bound on the sum of `targets` on one device may be relied on, other than what follows from the above.
Results may differ from a plain program's by a relative error of at most 0.0041.
Values may be sent and summed in bfloat16 or wider, within the bound.
No kernel may reach another device: no remote copies, remote signals or barrier semaphores. Data moves between devices by JAX's collectives and lax.ppermute only.
A program may use at most 64 MiB of HBM per device.

v0:
```python
import functools

import jax
import jax.numpy as jnp
from jax import lax
from jax.experimental import pallas as pl
from jax.experimental.pallas import tpu as pltpu
from jax.sharding import PartitionSpec as P

BS = 8


tap_offsets = [
    (tap_index // 9 - 1, tap_index // 3 % 3 - 1, tap_index % 3 - 1) for tap_index in range(27)
]


def elu_pair(values):
    negative = jnp.exp(jnp.minimum(values, 0.0))
    return (jnp.where(values > 0, values, negative - 1.0), jnp.where(values > 0, 1.0, negative))


def neighbor_tables(device_block):
    space_count = lax.axis_size("space")
    depth_z = space_count // 8
    self_index = lax.axis_index("space")
    blocks = device_block[0]
    coords = jnp.stack([blocks // (4 * depth_z), blocks // depth_z % 4, blocks % depth_z])
    own_coords = lax.dynamic_index_in_dim(coords, self_index, 1, keepdims=False)
    offsets = jnp.array(tap_offsets, jnp.int32)
    limits = jnp.array([4, 4, depth_z], jnp.int32)
    wanted = own_coords[None, :] + offsets
    inside = jnp.all((wanted >= 0) & (wanted < limits[None, :]), axis=1) & (jnp.arange(27) != 13)
    wanted_id = (wanted[:, 0] * 4 + wanted[:, 1]) * depth_z + wanted[:, 2]
    matches = (blocks[None, :] == wanted_id[:, None]) & inside[:, None]
    devices = jnp.arange(space_count, dtype=jnp.int32)
    owner_row = jnp.sum(jnp.where(matches, devices[None, :], 0), axis=1)
    present = jnp.any(matches, axis=1)
    relative = coords - own_coords[:, None]
    adjacent = jnp.all(jnp.abs(relative) <= 1, axis=0) & (devices != self_index)
    send_tap = jnp.where(
        adjacent, (relative[0] + 1) * 9 + (relative[1] + 1) * 3 + relative[2] + 1, 13
    )
    return (owner_row, present, send_tap)


def region_slice(block_data, offset, depth_cells):
    span_list = []
    for step_value in offset:
        if step_value == 1:
            span_list.append(slice(BS - depth_cells, BS))
        elif step_value == -1:
            span_list.append(slice(0, depth_cells))
        else:
            span_list.append(slice(0, BS))
    return block_data[:, span_list[0], span_list[1], span_list[2]]


def surround(block_data, depth_cells, tables):
    owner_row, present, send_tap = tables
    channels = block_data.shape[0]
    length = depth_cells * BS * BS
    pieces = []
    for tap_index in range(27):
        if tap_index == 13:
            pieces.append(jnp.zeros((channels, length), block_data.dtype))
        else:
            region = region_slice(block_data, tap_offsets[tap_index], depth_cells).reshape(
                channels, -1
            )
            pieces.append(jnp.pad(region, ((0, 0), (0, length - region.shape[1]))))
    outgoing = jnp.stack(pieces)
    sending = outgoing[send_tap]
    by_source = lax.all_to_all(sending, "space", split_axis=0, concat_axis=0, tiled=True)
    incoming = jnp.where(
        present[:, None, None], by_source[owner_row], jnp.zeros((), block_data.dtype)
    )
    rows_x = []
    for step_x in range(3):
        rows_y = []
        for step_y in range(3):
            rows_z = []
            for step_z in range(3):
                tap_index = step_x * 9 + step_y * 3 + step_z
                if tap_index == 13:
                    rows_z.append(block_data)
                else:
                    extent_list = [
                        BS if step_value == 1 else depth_cells
                        for step_value in (step_x, step_y, step_z)
                    ]
                    count_cells = extent_list[0] * extent_list[1] * extent_list[2]
                    rows_z.append(
                        incoming[tap_index][:, :count_cells].reshape(
                            channels, extent_list[0], extent_list[1], extent_list[2]
                        )
                    )
            rows_y.append(jnp.concatenate(rows_z, axis=3))
        rows_x.append(jnp.concatenate(rows_y, axis=2))
    return jnp.concatenate(rows_x, axis=1)


def conv_padded(padded, kernel, dilation):
    result = lax.conv_general_dilated(
        padded[None],
        kernel,
        (1, 1, 1),
        "VALID",
        rhs_dilation=(dilation, dilation, dilation),
        dimension_numbers=("NCDHW", "OIDHW", "NCDHW"),
        preferred_element_type=jnp.float32,
    )
    return result[0].reshape(kernel.shape[0], BS * BS * BS)


def kernel_grad(padded, grad_rows, dilation):
    channels = padded.shape[0]
    outputs = grad_rows.shape[0]
    grad_block = grad_rows.reshape(outputs, 1, BS, BS, BS)
    result = lax.conv_general_dilated(
        padded[None],
        grad_block,
        (dilation, dilation, dilation),
        "VALID",
        dimension_numbers=("CNDHW", "OIDHW", "NCDHW"),
        preferred_element_type=jnp.float32,
    )
    return result.reshape(channels, outputs, 27).transpose(1, 2, 0)


def on_device_deep(features, device_block, conv_first, conv_second, head_weight, targets):
    channels = features.shape[2]
    tables = neighbor_tables(device_block)
    kernel_first = conv_first.reshape(channels, 3, 3, 3, channels).transpose(0, 4, 1, 2, 3)
    kernel_second = conv_second.reshape(channels, 3, 3, 3, channels).transpose(0, 4, 1, 2, 3)
    block_in = features[0, 0].reshape(channels, BS, BS, BS)
    padded_in = surround(block_in, 1, tables)
    pre_first = conv_padded(padded_in, kernel_first, 1)
    act_first, slope_first = elu_pair(pre_first)
    hid_first = act_first.astype(jnp.bfloat16)
    padded_first = surround(hid_first.reshape(channels, BS, BS, BS), 2, tables)
    pre_second = conv_padded(padded_first, kernel_second, 2)
    act_second, slope_second = elu_pair(pre_second)
    hid_second = act_second.astype(jnp.bfloat16)
    logits = jnp.dot(head_weight, hid_second, preferred_element_type=jnp.float32)
    scale = (lax.axis_size("dp") * lax.axis_size("space") * 3 * BS * BS * BS) ** (-0.5)
    grad_logit = ((jax.nn.sigmoid(logits) - targets[0, 0].astype(jnp.float32)) * scale).astype(
        jnp.bfloat16
    )
    grad_head = lax.dot_general(
        grad_logit, hid_second, (((1,), (1,)), ((), ())), preferred_element_type=jnp.float32
    )
    back_second = lax.dot_general(
        head_weight, grad_logit, (((0,), (0,)), ((), ())), preferred_element_type=jnp.float32
    )
    grad_pre_second = (back_second * slope_second).astype(jnp.bfloat16)
    grad_second = kernel_grad(padded_first, grad_pre_second, 2)
    padded_grad = surround(grad_pre_second.reshape(channels, BS, BS, BS), 2, tables)
    kernel_back = jnp.transpose(kernel_second[:, :, ::-1, ::-1, ::-1], (1, 0, 2, 3, 4))
    back_first = conv_padded(padded_grad, kernel_back, 2)
    grad_pre_first = (back_first * slope_first).astype(jnp.bfloat16)
    grad_first = kernel_grad(padded_in, grad_pre_first, 1)
    grad_first, grad_second, grad_head = lax.psum(
        (grad_first, grad_second, grad_head), ("dp", "space")
    )
    return (logits[None, None], grad_first, grad_second, grad_head)


C = 48
CELLS = 512
HALF = 512
LANES = 128


def lanes(rows=1):
    return lax.broadcasted_iota(jnp.int32, (rows, LANES), 1)


def roll(values, shift):
    return pltpu.roll(values, shift % LANES, 1) if shift % LANES else values


def listed_blocks(block_ref, me):
    ids = block_ref[...].astype(jnp.float32)
    index = lax.broadcasted_iota(jnp.int32, ids.shape, 1)
    return [
        jnp.sum(jnp.where(index == (me ^ k), ids, 0.0)).astype(jnp.int32)
        for k in range(ids.shape[1])
    ]


def apart(source, target):
    return (target >> 2) - (source >> 2), (target & 3) - (source & 3)


PARTNERS = (6, 4, 2)


def block_tiles(features_ref, targets_ref):
    tiles = [
        [features_ref[16 * ct : 16 * (ct + 1), LANES * q : LANES * (q + 1)] for q in range(4)]
        for ct in range(3)
    ]
    targets = targets_ref[:, 0, :].astype(jnp.float32)
    targets = jnp.concatenate([targets, jnp.zeros((1, CELLS), jnp.float32)], axis=0)
    return tiles, [targets[:, LANES * q : LANES * (q + 1)] for q in range(4)]


def write_cases(tiles, rows, cases_ref):
    lane = lanes(16)
    left = lane < 64
    cell = lane & 63
    target_tile = jnp.concatenate(rows, axis=0)

    def write(case, pairs, halves, wanted):
        for ct in range(3):
            cases_ref[case, 2 * ct] = pairs[ct][0]
            cases_ref[case, 2 * ct + 1] = pairs[ct][1]
        cases_ref[case, 6] = jnp.where(left, halves[0], halves[1])
        cases_ref[case, 7] = jnp.where(left, halves[2], wanted.astype(jnp.bfloat16))

    for case, pair, single, q in ((0, (2, 3), 1, 3), (1, (0, 1), 2, 0)):
        turns = (64, 0, 64) if case == 0 else (0, 64, 0)
        halves = [roll(tiles[ct][single], turns[ct]) for ct in range(3)]
        both = [roll(rows[q], 64), rows[q], jnp.zeros((8, LANES), jnp.float32)]
        wanted = jnp.concatenate(both, axis=0)
        write(case, [(t[pair[0]], t[pair[1]]) for t in tiles], halves, wanted)
    for case, spare, turn, turns, target_turns in (
        (2, cell < 24, -24, (-48, -96, -16, -64), (16, -32)),
        (3, cell >= 40, 40, (-24, -72, 8, -40), (64, 16)),
    ):
        pairs, halves = [], []
        for ct, t in enumerate(tiles):
            pairs.append([jnp.where(spare, roll(t[q + 2], turn), t[q]) for q in range(2)])
            moved = [roll(t[2 + n // 2], turns[n] + (64 if ct == 1 else 0)) for n in range(4)]
            half = jnp.where(cell < 16, moved[0], jnp.where(cell < 32, moved[1], moved[2]))
            halves.append(jnp.where(cell < 48, half, moved[3]))
        wanted = [roll(target_tile, n) for n in target_turns]
        write(case, pairs, halves, jnp.where(lane < 80, wanted[0], wanted[1]))


def case_of(source, target):
    dx, dy = apart(source, target)
    return jnp.where(dx > 0, 0, jnp.where(dx < 0, 1, jnp.where(dy > 0, 2, 3)))


def pack_own_kernel(block_ref, features_ref, targets_ref, own_ref, slabs_ref, cases_ref):
    blocks = listed_blocks(block_ref, lax.axis_index("space"))
    tiles, rows = block_tiles(features_ref, targets_ref)
    for ct in range(3):
        for q in range(4):
            own_ref[4 * ct + q] = tiles[ct][q]
    own_ref[12] = jnp.concatenate(rows, axis=0).astype(jnp.bfloat16)
    write_cases(tiles, rows, cases_ref)
    for n, k in enumerate(PARTNERS):
        slabs_ref[n] = cases_ref[case_of(blocks[0], blocks[k])]


def pack_mate_kernel(block_ref, features_ref, targets_ref, slabs_ref, mate_ref, *refs):
    *pair_refs, cases_ref = refs
    blocks = listed_blocks(block_ref, lax.axis_index("space"))
    write_cases(*block_tiles(features_ref, targets_ref), cases_ref)
    mate_ref[...] = cases_ref[case_of(blocks[1], blocks[0])]
    for n, (k, ref) in enumerate(zip(PARTNERS, pair_refs)):
        ref[0] = slabs_ref[n]
        ref[1] = cases_ref[case_of(blocks[1], blocks[k])]


def stacked_taps(ref):
    rows = []
    for a in range(3):
        taps = [ref[9 * a + t] for t in range(9)]
        rows.append(jnp.concatenate(taps, axis=1))
    return jnp.concatenate(rows, axis=0)


def prepare_kernel(
    block_ref,
    first_ref,
    second_ref,
    head_ref,
    w1_ref,
    w2_ref,
    w2t_ref,
    h_ref,
    ht_ref,
    owners_ref,
    masks_ref,
    table_ref,
):
    w1_ref[...] = stacked_taps(first_ref)
    whole = stacked_taps(second_ref)
    w2_ref[...] = whole
    w2t_ref[...] = whole.T
    head = head_ref[...].astype(jnp.float32)
    head = jnp.concatenate([head, jnp.zeros((13, C), jnp.float32)], axis=0)
    h_ref[...] = head.astype(jnp.bfloat16)
    ht_ref[...] = head.T.astype(jnp.bfloat16)

    blocks = listed_blocks(block_ref, lax.axis_index("space"))
    for slot in range(10):
        table_ref[0, slot] = 1
        table_ref[1, slot] = 0
    table_ref[1, 4] = 1
    for k in range(1, len(blocks)):
        dx, dy = apart(blocks[0], blocks[k])
        near = (dx >= -1) & (dx <= 1) & (dy >= -1) & (dy <= 1)
        slot = jnp.where(near, dx * 3 + dy + 4, 9)
        table_ref[0, slot] = k
        table_ref[1, slot] = 1
    lane = lanes()
    there = [table_ref[1, q].astype(jnp.float32) for q in range(9)]
    owners = jnp.zeros((1, LANES), jnp.int32)
    for q in range(9):
        owners = jnp.where(lane == q, table_ref[0, q], owners)
    owners_ref[...] = owners
    for bx in range(3):
        before, middle, after = there[3 * bx : 3 * bx + 3]
        masks_ref[bx : bx + 1, :] = jnp.where(
            lane < 32, before, jnp.where(lane < 96, middle, after)
        )
        masks_ref[bx + 3 : bx + 4, :] = jnp.where(lane < 64, after, before)


def matmul(left, right):
    return lax.dot_general(
        left, right, (((1,), (0,)), ((), ())), preferred_element_type=jnp.float32
    )


def matmul_lanes(left, right):
    return lax.dot_general(
        left, right, (((1,), (1,)), ((), ())), preferred_element_type=jnp.float32
    )


def crop_kernel(scale, owners_ref, masks_ref, own_ref, mate_ref, *refs):
    crop_body(scale, owners_ref, masks_ref, own_ref, mate_ref, refs[:3], *refs[3:])


def crop_body(
    scale,
    owners_ref,
    masks_ref,
    own_ref,
    mate_ref,
    pairs,
    w1_ref,
    w2_ref,
    w2t_ref,
    h_ref,
    ht_ref,
    logits_ref,
    keep_ref,
    send_ref,
    gathered_ref,
    sides_ref,
    ends_ref,
    x9_ref,
    h9_ref,
    product_ref,
    slope1_ref,
    slope2_ref,
    hid2_ref,
    grad2_ref,
    shifted_ref,
    back_ref,
):
    gathered_ref[1] = mate_ref[...]
    for k, pair in zip(PARTNERS, pairs):
        for j in range(2):
            gathered_ref[k + j] = pair[j]
    owners = owners_ref[...]
    owner = [owners[0, q] for q in range(9)]

    bf16 = jnp.bfloat16
    lane = lanes(16)
    depth = lane & 7
    depth48 = lanes(C) & 7
    low, mid, left_half = lane < 32, lane < 96, lane < 64
    masks = [masks_ref[bx : bx + 1, :] for bx in range(3)]
    main_masks = [jnp.broadcast_to(mask, (16, LANES)).astype(bf16) for mask in masks]
    edge_masks = [
        jnp.broadcast_to(masks_ref[bx + 3 : bx + 4, :], (16, LANES)).astype(bf16)
        for bx in range(3)
    ]
    own_row = jnp.where((lane >= 32) & mid, 1.0, 0.0)[0:1]

    cell = lane & 63
    for side, by, in_place, turn, turns in (
        (0, 0, cell < 48, 24, (48, 96, 16, 64)),
        (1, 2, cell < 24, -40, (24, 72, -8, 40)),
    ):
        slab = owner[3 + by]
        for ct in range(3):
            half = gathered_ref[slab, 6 + ct // 2]
            for q in range(2):
                sides_ref[side, 4 * ct + q] = gathered_ref[slab, 2 * ct + q]
                moved = [roll(half, turns[2 * q + n] - (64 if ct == 1 else 0)) for n in range(2)]
                sides_ref[side, 4 * ct + q + 2] = jnp.where(
                    in_place,
                    roll(gathered_ref[slab, 2 * ct + q], turn),
                    jnp.where(left_half, moved[0], moved[1]),
                )

    for bx in (0, 2):
        for by in range(3):
            for ct in range(3):
                tile = gathered_ref[owner[3 * bx + by], 6 + ct // 2]
                ends_ref[3 * bx // 2 + by, ct] = roll(tile, -64 * (ct % 2))

    def placed(ct, bx, i):
        if bx == 1:
            tile, half = 4 * ct + i // 2, i % 2
            parts = [sides_ref[0, tile], own_ref[tile], sides_ref[1, tile]]
        elif i == (3 if bx == 0 else 4):
            half = 0
            parts = [ends_ref[3 * bx // 2 + by, ct] for by in range(3)]
        else:
            tile, half = 2 * ct + (i // 2 - 2 if bx == 0 else i // 2), i % 2
            parts = [gathered_ref[owner[3 * bx + by], tile] for by in range(3)]
        outer = 96 - 64 * half
        return roll(parts[0], outer), roll(parts[1], 32 - 64 * half), roll(parts[2], outer)

    zero = jnp.zeros((16, LANES), bf16)

    for plane in range(18):
        bx, i = (plane + 3) // 8, (plane + 3) % 8
        for ct in range(3):
            before, middle, after = placed(ct, bx, i)
            main = jnp.where(low, before, jnp.where(mid, middle, after)) * main_masks[bx]
            edge = jnp.where(left_half, after, before) * edge_masks[bx]
            for c in (-1, 0, 1):
                if c == 0:
                    main_c, edge_c = main, edge
                else:
                    keep = depth >= 1 if c == 1 else depth <= 6
                    main_c, edge_c = jnp.where(keep, main, zero), jnp.where(keep, edge, zero)
                for b in (-1, 0, 1):
                    step = 8 * b + c
                    if b == 1:
                        source = jnp.where(lane < step, edge_c, main_c)
                    elif b == -1:
                        source = jnp.where(lane >= LANES + step, edge_c, main_c)
                    else:
                        source = main_c
                    row = (3 * (b + 1) + c + 1) * C + 16 * ct
                    x9_ref[row : row + 16, LANES * plane : LANES * (plane + 1)] = (
                        roll(source, -step) if step else source
                    )

    def plane_cols(plane):
        return slice(LANES * plane, LANES * (plane + 1))

    def summed(plane, stride):
        return (
            product_ref[0:C, plane_cols(plane)]
            + product_ref[C : 2 * C, plane_cols(plane + stride)]
            + product_ref[2 * C : 3 * C, plane_cols(plane + 2 * stride)]
        )

    for n in range(9):
        cols = slice(256 * n, 256 * (n + 1))
        product_ref[:, cols] = matmul(w1_ref[...], x9_ref[:, cols])

    for plane in range(16):
        bx = (plane + 4) // 8
        pre = summed(plane, 1)
        negative = jnp.exp(jnp.minimum(pre, 0.0))
        if 4 <= plane < 12:
            slope1_ref[:, plane_cols(plane - 4)] = jnp.where(pre > 0, 1.0, negative)
        hidden = jnp.where(pre > 0, pre, negative - 1.0) * masks[bx]
        hidden = hidden.astype(bf16)
        for c in (-1, 0, 1):
            if c == 0:
                source = hidden
            else:
                keep = depth48 >= 2 if c == 1 else depth48 <= 5
                source = jnp.where(keep, hidden, jnp.zeros((C, LANES), bf16))
            for b in (-1, 0, 1):
                step = 16 * b + 2 * c
                row = (3 * (b + 1) + c + 1) * C
                h9_ref[row : row + C, plane_cols(plane)] = roll(source, -step) if step else source

    for n in range(8):
        cols = slice(256 * n, 256 * (n + 1))
        product_ref[:, cols] = matmul(w2_ref[...], h9_ref[:, cols])

    for plane in range(12):
        bx = (plane + 6) // 8
        pre = summed(plane, 2)
        negative = jnp.exp(jnp.minimum(pre, 0.0))
        slope2_ref[:, plane_cols(plane)] = jnp.where(pre > 0, 1.0, negative) * masks[bx]
        hidden = jnp.where(pre > 0, pre, negative - 1.0) * masks[bx]
        hid2_ref[:, plane_cols(plane)] = hidden.astype(jnp.bfloat16)

    logits = matmul(h_ref[...], hid2_ref[...])
    targets = []
    for bx, half in ((0, 1), (1, 0), (1, 1), (2, 1)):
        if bx == 1:
            before = roll(gathered_ref[owner[3], 7], -48 - 16 * half)
            middle = roll(own_ref[12], 32 - 64 * half)
            after = roll(gathered_ref[owner[5], 7], 32 - 16 * half)
        else:
            parts = [gathered_ref[owner[3 * bx + by], 7] for by in range(3)]
            before, middle, after = roll(parts[0], 32), roll(parts[1], -32), roll(parts[2], 32)
        cells = jnp.where(low, before, jnp.where(mid, middle, after))
        targets.append(cells.astype(jnp.float32))
    grads = []
    for plane in range(12):
        bx, i = (plane + 6) // 8, (plane + 6) % 8
        value = logits[:, plane_cols(plane)]
        if bx == 1:
            wanted = targets[1 + i % 2][4 * (i // 2) : 4 * (i // 2) + 4]
        else:
            wanted = targets[0 if bx == 0 else 3][4 * (i % 2) : 4 * (i % 2) + 4]
        wanted = jnp.concatenate([wanted, jnp.zeros((12, LANES), jnp.float32)], axis=0)
        sigmoid = 1.0 / (1.0 + jnp.exp(-value))
        grads.append((sigmoid - wanted) * masks[bx] * scale)
    for q in range(4):
        first = roll(logits[:, plane_cols(2 + 2 * q)], -32)
        second = roll(logits[:, plane_cols(3 + 2 * q)], 32)
        logits_ref[:, plane_cols(q)] = jnp.where(left_half, first, second)[0:8]

    grad_logit = jnp.concatenate(grads, axis=1).astype(jnp.bfloat16)
    back = matmul(ht_ref[...], grad_logit)
    grad2_ref[...] = (back * slope2_ref[...]).astype(jnp.bfloat16)
    own_grads = jnp.concatenate([grads[2 + x] * own_row for x in range(8)], axis=1)
    head_part = matmul_lanes(hid2_ref[:, 2 * LANES : 10 * LANES], own_grads.astype(jnp.bfloat16))

    own_bf16 = jnp.broadcast_to(own_row, (C, LANES)).astype(bf16)
    shifted_ref[...] = jnp.zeros_like(shifted_ref)
    for a in range(3):
        for x in range(8):
            shifted_ref[C * a : C * (a + 1), plane_cols(x + 2 * a)] = (
                grad2_ref[:, plane_cols(x + 2)] * own_bf16
            )
    second_part = matmul_lanes(shifted_ref[...], h9_ref[:, 2 * LANES : 14 * LANES])

    for a in range(3):
        for x in range(8):
            shifted_ref[C * a : C * (a + 1), plane_cols(x)] = grad2_ref[:, plane_cols(x + 4 - 2 * a)]
    for n in range(4):
        cols = slice(256 * n, 256 * (n + 1))
        back_ref[:, cols] = matmul(w2t_ref[...], shifted_ref[:, cols])
    grad1 = []
    for x in range(8):
        total = jnp.zeros((C, LANES), jnp.float32)
        for c in (-1, 0, 1):
            part = jnp.zeros((C, LANES), jnp.float32)
            for b in (-1, 0, 1):
                row = (3 * (b + 1) + c + 1) * C
                step = 16 * b + 2 * c
                piece = back_ref[row : row + C, plane_cols(x)]
                part += roll(piece, step) if step else piece
            if c:
                part = jnp.where(depth48 >= 2 if c == 1 else depth48 <= 5, part, 0.0)
            total += part
        grad1.append((total * slope1_ref[:, plane_cols(x)] * own_row).astype(jnp.bfloat16))

    shifted_ref[...] = jnp.zeros_like(shifted_ref)
    for a in range(3):
        for x in range(8):
            shifted_ref[C * a : C * (a + 1), plane_cols(x + a)] = grad1[x]
    first_part = matmul_lanes(
        shifted_ref[:, 0 : 10 * LANES], x9_ref[:, 4 * LANES : 14 * LANES]
    )

    first_core = (lax.axis_index("dp") & 1) == 0
    head_part = jnp.concatenate([head_part, jnp.zeros((24, 16), jnp.float32)], axis=0)
    nothing = jnp.zeros((72, 16), jnp.float32)
    ends = []
    for part, extra in ((first_part, nothing), (second_part, head_part)):
        tail = jnp.concatenate([part[0:72, 384:], part[72:144, 384:], extra, nothing], axis=1)
        ends.append(jnp.concatenate([tail, jnp.zeros((8, LANES), jnp.float32)], axis=0))
    pieces = [(first_part[:, plane_cols(q)], second_part[:, plane_cols(q)]) for q in range(3)]
    row = 0
    for first, second in pieces + [tuple(ends)]:
        rows = slice(row, row + first.shape[0])
        keep_ref[rows, :] = jnp.where(first_core, first, second)
        send_ref[rows, :] = jnp.where(first_core, second, first)
        row += first.shape[0]


def add_kernel(mine_ref, other_ref, out_ref):
    out_ref[...] = (mine_ref[...] + other_ref[...]).astype(jnp.bfloat16)


def sum_kernel(parts_ref, out_ref):
    total = parts_ref[0].astype(jnp.float32)
    for s in range(1, parts_ref.shape[0]):
        total += parts_ref[s].astype(jnp.float32)
    total = total.astype(jnp.bfloat16)
    for s in range(out_ref.shape[0]):
        out_ref[s] = total


def unpack_kernel(mine_ref, other_ref, logits_ref, first_ref, second_ref, head_ref, out_ref):
    out_ref[:, 0, :] = logits_ref[0:3, :]
    first_core = (lax.axis_index("dp") & 1) == 0
    mine, other = mine_ref[...], other_ref[...]
    for k, out in ((0, first_ref), (1, second_ref)):
        half = jnp.where(first_core, other if k else mine, mine if k else other)
        half = half.astype(jnp.float32)
        tail = jnp.concatenate([half[432:504, 0:C], half[432:504, C : 2 * C]], axis=0)
        tiles = [half[144 * q : 144 * (q + 1), :] for q in range(3)]
        whole = jnp.concatenate(tiles + [tail], axis=1)
        for a in range(3):
            for t in range(9):
                out[9 * a + t] = whole[C * a : C * (a + 1), C * t : C * (t + 1)]
        if k:
            head_ref[...] = half[432 : 432 + C, 96:112].T[0:3]


def on_device_flat(features, device_block, conv_first, conv_second, head_weight, targets):
    space_count = lax.axis_size("space")
    device_count = lax.axis_size("dp") * space_count
    bf16, f32 = jnp.bfloat16, jnp.float32
    small = pltpu.CompilerParams(vmem_limit_bytes=8 * 1024 * 1024)
    shape = jax.ShapeDtypeStruct
    vmem = pl.BlockSpec(memory_space=pltpu.VMEM)

    def swap(values, mask):
        return lax.ppermute(values, "space", [(s, s ^ mask) for s in range(space_count)])

    mate_targets, mate_features = swap(targets, 1), swap(features, 1)
    own, own_slabs = pl.pallas_call(
        pack_own_kernel,
        out_shape=(shape((13, 16, LANES), bf16), shape((3, 8, 16, LANES), bf16)),
        in_specs=[vmem] * 3,
        out_specs=(vmem,) * 2,
        scratch_shapes=[pltpu.VMEM((4, 8, 16, LANES), bf16)],
        compiler_params=small,
        cost_estimate=pl.CostEstimate(flops=1_000_000, bytes_accessed=2_000_000, transcendentals=0),
        name="pack_own",
    )(device_block, features[0, 0], targets[0].transpose(1, 0, 2))
    mate_slab, *pairs = pl.pallas_call(
        pack_mate_kernel,
        out_shape=(
            shape((8, 16, LANES), bf16),
            *[shape((2, 8, 16, LANES), bf16) for _ in PARTNERS],
        ),
        in_specs=[vmem] * 4,
        out_specs=(vmem,) * 4,
        scratch_shapes=[pltpu.VMEM((4, 8, 16, LANES), bf16)],
        compiler_params=small,
        name="pack_mate",
    )(device_block, mate_features[0, 0], mate_targets[0].transpose(1, 0, 2), own_slabs)
    pairs = [swap(pair, mask) for pair, mask in zip(pairs, PARTNERS)]

    w1, w2, w2t, head, head_t, owners, masks = pl.pallas_call(
        prepare_kernel,
        out_shape=(
            shape((3 * C, 9 * C), bf16),
            shape((3 * C, 9 * C), bf16),
            shape((9 * C, 3 * C), bf16),
            shape((16, C), bf16),
            shape((C, 16), bf16),
            shape((1, LANES), jnp.int32),
            shape((8, LANES), f32),
        ),
        in_specs=[vmem] * 4,
        out_specs=(vmem,) * 7,
        scratch_shapes=[pltpu.SMEM((2, 16), jnp.int32)],
        compiler_params=small,
        cost_estimate=pl.CostEstimate(flops=2_000_000, bytes_accessed=4_000_000, transcendentals=0),
        name="prepare",
    )(device_block, conv_first.transpose(1, 0, 2), conv_second.transpose(1, 0, 2), head_weight)

    scale = (device_count * 3 * CELLS) ** (-0.5)
    logits, keep, send = pl.pallas_call(
        functools.partial(crop_kernel, scale),
        out_shape=(shape((8, CELLS), f32), shape((HALF, LANES), f32), shape((HALF, LANES), f32)),
        in_specs=[vmem] * 12,
        out_specs=(vmem,) * 3,
        scratch_shapes=[
            pltpu.VMEM((space_count, 8, 16, LANES), bf16),
            pltpu.VMEM((2, 12, 16, LANES), bf16),
            pltpu.VMEM((6, 3, 16, LANES), bf16),
            pltpu.VMEM((9 * C, 18 * LANES), bf16),
            pltpu.VMEM((9 * C, 16 * LANES), bf16),
            pltpu.VMEM((3 * C, 18 * LANES), f32),
            pltpu.VMEM((C, 8 * LANES), f32),
            pltpu.VMEM((C, 12 * LANES), f32),
            pltpu.VMEM((C, 12 * LANES), bf16),
            pltpu.VMEM((C, 12 * LANES), bf16),
            pltpu.VMEM((3 * C, 12 * LANES), bf16),
            pltpu.VMEM((9 * C, 8 * LANES), f32),
        ],
        compiler_params=pltpu.CompilerParams(vmem_limit_bytes=20 * 1024 * 1024),
        name="forward_backward",
    )(owners, masks, own, mate_slab, *pairs, w1, w2, w2t, head, head_t)

    dp_count = lax.axis_size("dp")

    def swap_cores(values):
        return lax.ppermute(values, "dp", [(d, d ^ 1) for d in range(dp_count)])

    peers = device_count // 2
    groups = [
        [d * space_count + s for d in range(core, dp_count, 2) for s in range(space_count)]
        for core in range(2)
    ]

    def exchange(values):
        return lax.all_to_all(
            values, ("dp", "space"), 0, 0, axis_index_groups=groups, tiled=True
        )

    def step(kernel, out, *operands):
        return pl.pallas_call(
            kernel,
            out_shape=out,
            in_specs=[vmem] * len(operands),
            out_specs=vmem,
            compiler_params=small,
            name="gradient_sum",
        )(*operands)

    term = step(add_kernel, shape((HALF, LANES), bf16), keep, swap_cores(send))
    pieces = shape((peers, HALF // peers, LANES), bf16)
    total = exchange(step(sum_kernel, pieces, exchange(term.reshape(pieces.shape))))
    total = total.reshape(HALF, LANES)
    grad_first, grad_second, grad_head, logits = pl.pallas_call(
        unpack_kernel,
        out_shape=(
            shape((27, C, C), f32),
            shape((27, C, C), f32),
            shape((3, C), f32),
            shape((3, 1, CELLS), f32),
        ),
        in_specs=[vmem] * 3,
        out_specs=(vmem,) * 4,
        compiler_params=small,
        name="unpack_gradients",
    )(total, swap_cores(total), logits)
    return (
        logits.transpose(1, 0, 2)[None],
        grad_first.transpose(1, 0, 2),
        grad_second.transpose(1, 0, 2),
        grad_head,
    )


def solution(mesh):
    in_specs = (
        P("dp", "space", None, None),
        P("dp", None),
        P(),
        P(),
        P(),
        P("dp", "space", None, None),
    )
    out_specs = (P("dp", "space", None, None), P(), P(), P())
    flat = mesh.shape["space"] == 8 and mesh.shape["dp"] in (2, 4)
    return jax.shard_map(
        on_device_flat if flat else on_device_deep,
        mesh=mesh,
        in_specs=in_specs,
        out_specs=out_specs,
        check_vma=False,
    )
```

profile of v0, /device:TPU:0, one launch (start us, length us, event | category | flops | bytes accessed | tf_op | source)
XLA Modules:
  0.0 47.6 jit_solution(17470956950679824283)
XLA Ops:
  0.6 3.0 %collective-permute-start = (bf16[1,1,48,512]{3,2,1,0:T(8,128)(2,1)}, bf16[1,1,48,512]{3,2,1,0:T(8,128)(2,1)S(1)}, u32[]{:S(2)}, u32[]{:S(2)}) collective-permute-start(bf16[1,1,48,512]{3,2,1,0:T(8,128)(2,1)} %param.6), channel_id=1, source_target_pairs={{0,1},{1,0},{2,3},{3,2},{4,5},{5,4},{6,7},{7,6},{8,9},{9,8},{10,11... | collective-permute-start | bytes 147464 | tf_op jit(solution)/shard_map/ppermute | solution.py:624
  3.6 0.1 collective-permute-start.1
  3.7 0.0 copy-start.4
  3.7 0.7 %copy-done.4 = s32[1,8]{1,0:T(1,128)S(1)} copy-done((s32[1,8]{1,0:T(1,128)S(1)}, s32[1,8]{1,0:T(1,128)}, u32[]{:S(2)}) %copy-start.4) | copy-done | bytes 56
  4.4 0.0 copy-start.2
  4.4 0.8 %copy-done.2 = bf16[1,1,48,512]{3,2,1,0:T(8,128)(2,1)S(1)} copy-done((bf16[1,1,48,512]{3,2,1,0:T(8,128)(2,1)S(1)}, bf16[1,1,48,512]{3,2,1,0:T(8,128)(2,1)}, u32[]{:S(2)}) %copy-start.2) | copy-done | bytes 49176
  5.2 0.0 copy-start.3
  5.2 0.7 %copy-done.3 = s32[1,1,3,512]{3,1,2,0:T(1,128)S(1)} copy-done((s32[1,1,3,512]{3,1,2,0:T(1,128)S(1)}, s32[1,1,3,512]{3,1,2,0:T(1,128)}, u32[]{:S(2)}) %copy-start.3) | copy-done | bytes 6168
  5.9 0.2 pack_own.1
  6.0 1.5 %collective-permute-done.1 = s32[1,1,3,512]{3,0,2,1:T(1,128)S(1)} collective-permute-done((s32[1,1,3,512]{3,0,2,1:T(1,128)}, s32[1,1,3,512]{3,0,2,1:T(1,128)S(1)}, u32[]{:S(2)}, u32[]{:S(2)}) %collective-permute-start.1) | collective-permute-done | bytes 6176 | tf_op jit(solution)/shard_map/ppermute | solution.py:624
  7.5 0.0 collective-permute-done
  7.5 0.2 pack_mate.1
  7.6 3.7 %collective-permute-start.2 = (bf16[2,8,16,128]{3,2,1,0:T(8,128)(2,1)S(1)}, bf16[2,8,16,128]{3,2,1,0:T(8,128)(2,1)S(1)}, u32[]{:S(2)}, u32[]{:S(2)}) collective-permute-start(bf16[2,8,16,128]{3,2,1,0:T(8,128)(2,1)S(1)} %get-tuple-element.29), channel_id=1, source_target_pairs={{0,6},{1,7},{2,4},{3,5},{4,2},{5,3},{6,0},{7,1},{8,14},{9,15},{10,... | collective-permute-start | bytes 196616 | tf_op jit(solution)/shard_map/ppermute | solution.py:624
  11.3 0.0 collective-permute-start.3
  11.3 0.8 %collective-permute-start.4 = (bf16[2,8,16,128]{3,2,1,0:T(8,128)(2,1)S(1)}, bf16[2,8,16,128]{3,2,1,0:T(8,128)(2,1)S(1)}, u32[]{:S(2)}, u32[]{:S(2)}) collective-permute-start(bf16[2,8,16,128]{3,2,1,0:T(8,128)(2,1)S(1)} %get-tuple-element.31), channel_id=1, source_target_pairs={{0,2},{1,3},{2,0},{3,1},{4,6},{5,7},{6,4},{7,5},{8,10},{9,11},{10,... | collective-permute-start | bytes 196616 | tf_op jit(solution)/shard_map/ppermute | solution.py:624
  12.1 0.0 copy-start.5
  12.1 0.7 %copy-done.5 = bf16[3,48]{1,0:T(4,128)(2,1)S(1)} copy-done((bf16[3,48]{1,0:T(4,128)(2,1)S(1)}, bf16[3,48]{1,0:T(4,128)(2,1)}, u32[]{:S(2)}) %copy-start.5) | copy-done | bytes 312
  12.8 0.0 copy-start
  12.8 1.0 %copy-done = bf16[48,27,48]{2,0,1:T(8,128)(2,1)S(1)} copy-done((bf16[48,27,48]{2,0,1:T(8,128)(2,1)S(1)}, bf16[48,27,48]{2,0,1:T(8,128)(2,1)}, u32[]{:S(2)}) %copy-start) | copy-done | bytes 124440
  13.8 0.0 copy-start.1
  13.8 1.0 %copy-done.1 = bf16[48,27,48]{2,0,1:T(8,128)(2,1)S(1)} copy-done((bf16[48,27,48]{2,0,1:T(8,128)(2,1)S(1)}, bf16[48,27,48]{2,0,1:T(8,128)(2,1)}, u32[]{:S(2)}) %copy-start.1) | copy-done | bytes 124440
  14.7 0.3 prepare.1
  15.1 0.0 collective-permute-done.2.refs_0_
  15.1 1.5 %collective-permute-done.3.refs_1_ = bf16[2,8,16,128]{3,2,1,0:T(8,128)(2,1)S(1)} collective-permute-done((bf16[2,8,16,128]{3,2,1,0:T(8,128)(2,1)S(1)}, bf16[2,8,16,128]{3,2,1,0:T(8,128)(2,1)S(1)}, u32[]{:S(2)}, u32[]{:S(2)}) %collective-permute-start.3) | collective-permute-done | bytes 65568 | tf_op jit(solution)/shard_map/ppermute | solution.py:624
  16.6 0.0 collective-permute-done.4.refs_2_
  16.6 3.7 %forward_backward.1 = (f32[8,512]{1,0:T(8,128)S(1)}, f32[512,128]{1,0:T(8,128)S(1)}, f32[512,128]{1,0:T(8,128)S(1)}) custom-call(s32[1,128]{1,0:T(1,128)S(1)} %get-tuple-element.24.owners_ref, f32[8,128]{1,0:T(8,128)S(1)} %get-tuple-element.25.masks_ref, bf16[13,16,128]{2,1,0:T(8,128)(2,1)S(1)} %get-tuple-element.26.own_ref, ...), custom_call_target="tpu_custom_call" | custom-call | tf_op jit(solution)/shard_map/forward_backward/pallas_call | solution.py:671
  20.3 0.1 collective-permute-start.5
  20.4 1.5 %collective-permute-done.5.other_ref = f32[512,128]{1,0:T(8,128)S(1)} collective-permute-done((f32[512,128]{1,0:T(8,128)S(1)}, f32[512,128]{1,0:T(8,128)S(1)}, u32[]{:S(2)}, u32[]{:S(2)}) %collective-permute-start.5) | collective-permute-done | bytes 262176 | tf_op jit(solution)/shard_map/ppermute | solution.py:697
  21.9 12.4 %all_to_all.10.parts_ref = bf16[16,32,128]{2,1,0:T(8,128)(2,1)S(1)} all-to-all(bf16[16,32,128]{2,1,0:T(8,128)(2,1)S(1)} %bitcast.14), channel_id=1, replica_groups={{0,1,2,3,4,5,6,7,16,17,18,19,20,21,22,23},{8,9,10,11,12,13,14,15,24,25,..., dimensions={0} | all-to-all | bytes 262144 | tf_op jit(solution)/shard_map/all_to_all | solution.py:706
  34.4 10.6 %all_to_all.11 = bf16[16,32,128]{2,1,0:T(8,128)(2,1)S(1)} all-to-all(bf16[16,32,128]{2,1,0:T(8,128)(2,1)S(1)} %gradient_sum.3), channel_id=1, replica_groups={{0,1,2,3,4,5,6,7,16,17,18,19,20,21,22,23},{8,9,10,11,12,13,14,15,24,25,..., dimensions={0} | all-to-all | bytes 262144 | tf_op jit(solution)/shard_map/all_to_all | solution.py:706
  45.0 0.0 collective-permute-start.6
  45.0 1.3 %collective-permute-done.6.other_ref = bf16[512,128]{1,0:T(8,128)(2,1)S(1)} collective-permute-done((bf16[512,128]{1,0:T(8,128)(2,1)S(1)}, bf16[512,128]{1,0:T(8,128)(2,1)S(1)}, u32[]{:S(2)}, u32[]{:S(2)}) %collective-permute-start.6) | collective-permute-done | bytes 131104 | tf_op jit(solution)/shard_map/ppermute | solution.py:697
  46.3 1.3 %unpack_gradients.1 = (f32[27,48,48]{2,1,0:T(8,128)}, f32[27,48,48]{2,1,0:T(8,128)}, f32[3,48]{1,0:T(4,128)}, f32[3,1,512]{2,1,0:T(1,128)}) custom-call(bf16[512,128]{1,0:T(8,128)(2,1)S(1)} %bitcast.16, bf16[512,128]{1,0:T(8,128)(2,1)S(1)} %collective-permute-done.6.other_ref, f32[8,512]{1,0:T(8,128)S(1)} %get-tuple-element.39.logits_ref), custom_call_target="tpu_custom_call" | custom-call | tf_op jit(solution)/shard_map/unpack_gradients/pallas_call | solution.py:724
  (2 shorter events, 0.1 us)
Async XLA Ops:
  0.6 6.8 %collective-permute-start = (bf16[1,1,48,512]{3,2,1,0:T(8,128)(2,1)}, bf16[1,1,48,512]{3,2,1,0:T(8,128)(2,1)S(1)}, u32[]{:S(2)}, u32[]{:S(2)}) collective-permute-start(bf16[1,1,48,512]{3,2,1,0:T(8,128)(2,1)} %param.6), channel_id=1, source_target_pairs={{0,1},{1,0},{2,3},{3,2},{4,5},{5,4},{6,7},{7,6},{8,9},{9,8},{10,11... | collective-permute-start | bytes 147464 | tf_op jit(solution)/shard_map/ppermute | solution.py:624
  3.6 3.8 %collective-permute-start.1 = (s32[1,1,3,512]{3,0,2,1:T(1,128)}, s32[1,1,3,512]{3,0,2,1:T(1,128)S(1)}, u32[]{:S(2)}, u32[]{:S(2)}) collective-permute-start(s32[1,1,3,512]{3,0,2,1:T(1,128)} %bitcast.22), channel_id=1, source_target_pairs={{0,1},{1,0},{2,3},{3,2},{4,5},{5,4},{6,7},{7,6},{8,9},{9,8},{10,11... | collective-permute-start | bytes 18440 | tf_op jit(solution)/shard_map/ppermute | solution.py:624
  3.7 0.7 %copy-start.4 = (s32[1,8]{1,0:T(1,128)S(1)}, s32[1,8]{1,0:T(1,128)}, u32[]{:S(2)}) copy-start(s32[1,8]{1,0:T(1,128)} %block_ref.5) | copy-start | bytes 100
  4.4 0.8 %copy-start.2 = (bf16[1,1,48,512]{3,2,1,0:T(8,128)(2,1)S(1)}, bf16[1,1,48,512]{3,2,1,0:T(8,128)(2,1)}, u32[]{:S(2)}) copy-start(bf16[1,1,48,512]{3,2,1,0:T(8,128)(2,1)} %param.6) | copy-start | bytes 147460
  5.2 0.7 %copy-start.3 = (s32[1,1,3,512]{3,1,2,0:T(1,128)S(1)}, s32[1,1,3,512]{3,1,2,0:T(1,128)}, u32[]{:S(2)}) copy-start(s32[1,1,3,512]{3,1,2,0:T(1,128)} %param.11) | copy-start | bytes 18436
  7.6 7.4 %collective-permute-start.2 = (bf16[2,8,16,128]{3,2,1,0:T(8,128)(2,1)S(1)}, bf16[2,8,16,128]{3,2,1,0:T(8,128)(2,1)S(1)}, u32[]{:S(2)}, u32[]{:S(2)}) collective-permute-start(bf16[2,8,16,128]{3,2,1,0:T(8,128)(2,1)S(1)} %get-tuple-element.29), channel_id=1, source_target_pairs={{0,6},{1,7},{2,4},{3,5},{4,2},{5,3},{6,0},{7,1},{8,14},{9,15},{10,... | collective-permute-start | bytes 196616 | tf_op jit(solution)/shard_map/ppermute | solution.py:624
  11.3 5.3 %collective-permute-start.3 = (bf16[2,8,16,128]{3,2,1,0:T(8,128)(2,1)S(1)}, bf16[2,8,16,128]{3,2,1,0:T(8,128)(2,1)S(1)}, u32[]{:S(2)}, u32[]{:S(2)}) collective-permute-start(bf16[2,8,16,128]{3,2,1,0:T(8,128)(2,1)S(1)} %get-tuple-element.30), channel_id=1, source_target_pairs={{0,4},{1,5},{2,6},{3,7},{4,0},{5,1},{6,2},{7,3},{8,12},{9,13},{10,... | collective-permute-start | bytes 196616 | tf_op jit(solution)/shard_map/ppermute | solution.py:624
  11.3 5.3 %collective-permute-start.4 = (bf16[2,8,16,128]{3,2,1,0:T(8,128)(2,1)S(1)}, bf16[2,8,16,128]{3,2,1,0:T(8,128)(2,1)S(1)}, u32[]{:S(2)}, u32[]{:S(2)}) collective-permute-start(bf16[2,8,16,128]{3,2,1,0:T(8,128)(2,1)S(1)} %get-tuple-element.31), channel_id=1, source_target_pairs={{0,2},{1,3},{2,0},{3,1},{4,6},{5,7},{6,4},{7,5},{8,10},{9,11},{10,... | collective-permute-start | bytes 196616 | tf_op jit(solution)/shard_map/ppermute | solution.py:624
  12.1 0.7 %copy-start.5 = (bf16[3,48]{1,0:T(4,128)(2,1)S(1)}, bf16[3,48]{1,0:T(4,128)(2,1)}, u32[]{:S(2)}) copy-start(bf16[3,48]{1,0:T(4,128)(2,1)} %head_ref.1) | copy-start | bytes 868
  12.8 1.0 %copy-start = (bf16[48,27,48]{2,0,1:T(8,128)(2,1)S(1)}, bf16[48,27,48]{2,0,1:T(8,128)(2,1)}, u32[]{:S(2)}) copy-start(bf16[48,27,48]{2,0,1:T(8,128)(2,1)} %param.8) | copy-start | bytes 373252
  13.8 1.0 %copy-start.1 = (bf16[48,27,48]{2,0,1:T(8,128)(2,1)S(1)}, bf16[48,27,48]{2,0,1:T(8,128)(2,1)}, u32[]{:S(2)}) copy-start(bf16[48,27,48]{2,0,1:T(8,128)(2,1)} %param.9) | copy-start | bytes 373252
  20.3 1.6 %collective-permute-start.5 = (f32[512,128]{1,0:T(8,128)S(1)}, f32[512,128]{1,0:T(8,128)S(1)}, u32[]{:S(2)}, u32[]{:S(2)}) collective-permute-start(f32[512,128]{1,0:T(8,128)S(1)} %get-tuple-element.38), channel_id=1, source_target_pairs={{0,8},{8,0},{16,24},{24,16},{1,9},{9,1},{17,25},{25,17},{2,10},{10... | collective-permute-start | bytes 786440 | tf_op jit(solution)/shard_map/ppermute | solution.py:697
  45.0 1.3 %collective-permute-start.6 = (bf16[512,128]{1,0:T(8,128)(2,1)S(1)}, bf16[512,128]{1,0:T(8,128)(2,1)S(1)}, u32[]{:S(2)}, u32[]{:S(2)}) collective-permute-start(bf16[512,128]{1,0:T(8,128)(2,1)S(1)} %bitcast.15), channel_id=1, source_target_pairs={{0,8},{8,0},{16,24},{24,16},{1,9},{9,1},{17,25},{25,17},{2,10},{10... | collective-permute-start | bytes 393224 | tf_op jit(solution)/shard_map/ppermute | solution.py:697
where the time goes:
time: 48 us; the launch traced here: 47.6 us
  blocking collectives  23 us (48%)
  starting transfers between devices  7.61 us (16%)
  waiting for transfers between devices  5.82 us (12%)
  Pallas kernels  5.72 us (12%)
  local copies, waits for them, and re-layouts  4.77 us (10%)
  between operations  0.7 us (1%)
    all_to_all x2, blocking collectives, exchange(): lax.all_to_all(values, ('dp', 'space'), 0, 0, axis_index_groups=groups, t...  23 us
    ppermute x5, starting transfers between devices, swap(): lax.ppermute(values, 'space', [(s, s ^ mask) for s in range(space_count)])  7.53 us
    unnamed x12, local copies, waits for them, and re-layouts  4.77 us
    pallas_call x1, Pallas kernels, on_device_flat(): pl.pallas_call(functools.partial(crop_kernel, scale), out_shape=(shape((8...  3.73 us
    ppermute x5, waiting for transfers between devices, swap(): lax.ppermute(values, 'space', [(s, s ^ mask) for s in range(space_count)])  2.95 us
    ppermute x2, waiting for transfers between devices, swap_cores(): return lax.ppermute(values, 'dp', [(d, d ^ 1) for d in range(dp_count)])  2.87 us
    pallas_call x1, Pallas kernels, on_device_flat(): pl.pallas_call(unpack_kernel, out_shape=(shape((27, C, C), f32), shape((2...  1.28 us
  transfers between devices with their start and end apart: 7, of which 4 were waited for; matrix products, arithmetic and copies ran while one was open for 0% of the time, Pallas kernels for 1%

commit v1 on v0

--- a/solution.py
+++ b/solution.py
@@ -360,10 +360,10 @@
     h9_ref,
     product_ref,
     slope1_ref,
-    slope2_ref,
     hid2_ref,
     grad2_ref,
     shifted_ref,
+    spread_ref,
     back_ref,
 ):
     gathered_ref[1] = mate_ref[...]
@@ -486,15 +486,6 @@
         cols = slice(256 * n, 256 * (n + 1))
         product_ref[:, cols] = matmul(w2_ref[...], h9_ref[:, cols])
 
-    for plane in range(12):
-        bx = (plane + 6) // 8
-        pre = summed(plane, 2)
-        negative = jnp.exp(jnp.minimum(pre, 0.0))
-        slope2_ref[:, plane_cols(plane)] = jnp.where(pre > 0, 1.0, negative) * masks[bx]
-        hidden = jnp.where(pre > 0, pre, negative - 1.0) * masks[bx]
-        hid2_ref[:, plane_cols(plane)] = hidden.astype(jnp.bfloat16)
-
-    logits = matmul(h_ref[...], hid2_ref[...])
     targets = []
     for bx, half in ((0, 1), (1, 0), (1, 1), (2, 1)):
         if bx == 1:
@@ -506,36 +497,43 @@
             before, middle, after = roll(parts[0], 32), roll(parts[1], -32), roll(parts[2], 32)
         cells = jnp.where(low, before, jnp.where(mid, middle, after))
         targets.append(cells.astype(jnp.float32))
-    grads = []
-    for plane in range(12):
-        bx, i = (plane + 6) // 8, (plane + 6) % 8
-        value = logits[:, plane_cols(plane)]
-        if bx == 1:
-            wanted = targets[1 + i % 2][4 * (i // 2) : 4 * (i // 2) + 4]
-        else:
-            wanted = targets[0 if bx == 0 else 3][4 * (i % 2) : 4 * (i % 2) + 4]
-        wanted = jnp.concatenate([wanted, jnp.zeros((12, LANES), jnp.float32)], axis=0)
-        sigmoid = 1.0 / (1.0 + jnp.exp(-value))
-        grads.append((sigmoid - wanted) * masks[bx] * scale)
-    for q in range(4):
-        first = roll(logits[:, plane_cols(2 + 2 * q)], -32)
-        second = roll(logits[:, plane_cols(3 + 2 * q)], 32)
-        logits_ref[:, plane_cols(q)] = jnp.where(left_half, first, second)[0:8]
-
-    grad_logit = jnp.concatenate(grads, axis=1).astype(jnp.bfloat16)
-    back = matmul(ht_ref[...], grad_logit)
-    grad2_ref[...] = (back * slope2_ref[...]).astype(jnp.bfloat16)
-    own_grads = jnp.concatenate([grads[2 + x] * own_row for x in range(8)], axis=1)
-    head_part = matmul_lanes(hid2_ref[:, 2 * LANES : 10 * LANES], own_grads.astype(jnp.bfloat16))
-
-    own_bf16 = jnp.broadcast_to(own_row, (C, LANES)).astype(bf16)
-    shifted_ref[...] = jnp.zeros_like(shifted_ref)
-    for a in range(3):
-        for x in range(8):
-            shifted_ref[C * a : C * (a + 1), plane_cols(x + 2 * a)] = (
-                grad2_ref[:, plane_cols(x + 2)] * own_bf16
-            )
-    second_part = matmul_lanes(shifted_ref[...], h9_ref[:, 2 * LANES : 14 * LANES])
+    own_grads = []
+    for pair in range(6):
+        cols = slice(256 * pair, 256 * (pair + 1))
+        slopes = []
+        for plane in (2 * pair, 2 * pair + 1):
+            bx = (plane + 6) // 8
+            pre = summed(plane, 2)
+            negative = jnp.exp(jnp.minimum(pre, 0.0))
+            slopes.append(jnp.where(pre > 0, 1.0, negative) * masks[bx])
+            hidden = jnp.where(pre > 0, pre, negative - 1.0) * masks[bx]
+            hid2_ref[:, plane_cols(plane)] = hidden.astype(bf16)
+        logits = matmul(h_ref[...], hid2_ref[:, cols])
+        grads = []
+        for side in range(2):
+            plane = 2 * pair + side
+            bx, i = (plane + 6) // 8, (plane + 6) % 8
+            value = logits[:, plane_cols(side)]
+            if bx == 1:
+                wanted = targets[1 + i % 2][4 * (i // 2) : 4 * (i // 2) + 4]
+            else:
+                wanted = targets[0 if bx == 0 else 3][4 * (i % 2) : 4 * (i % 2) + 4]
+            wanted = jnp.concatenate([wanted, jnp.zeros((12, LANES), jnp.float32)], axis=0)
+            sigmoid = 1.0 / (1.0 + jnp.exp(-value))
+            grads.append((sigmoid - wanted) * masks[bx] * scale)
+        if 1 <= pair <= 4:
+            first = roll(logits[:, plane_cols(0)], -32)
+            second = roll(logits[:, plane_cols(1)], 32)
+            logits_ref[:, plane_cols(pair - 1)] = jnp.where(left_half, first, second)[0:8]
+            own_grads += [(grad * own_row).astype(bf16) for grad in grads]
+        back = matmul(ht_ref[...], jnp.concatenate(grads, axis=1).astype(bf16))
+        for side in range(2):
+            grad2_ref[:, plane_cols(2 * pair + side)] = (
+                back[:, plane_cols(side)] * slopes[side]
+            ).astype(bf16)
+    head_part = matmul_lanes(
+        hid2_ref[:, 2 * LANES : 10 * LANES], jnp.concatenate(own_grads, axis=1)
+    )
 
     for a in range(3):
         for x in range(8):
@@ -543,6 +541,17 @@
     for n in range(4):
         cols = slice(256 * n, 256 * (n + 1))
         back_ref[:, cols] = matmul(w2t_ref[...], shifted_ref[:, cols])
+    own_bf16 = jnp.broadcast_to(own_row, (C, LANES)).astype(bf16)
+    empty = jnp.zeros((C, LANES), bf16)
+    for a in range(3):
+        for x in [*range(2 * a), *range(2 * a + 8, 12)]:
+            spread_ref[C * a : C * (a + 1), plane_cols(x)] = empty
+        for x in range(8):
+            spread_ref[C * a : C * (a + 1), plane_cols(x + 2 * a)] = (
+                grad2_ref[:, plane_cols(x + 2)] * own_bf16
+            )
+    second_part = matmul_lanes(spread_ref[...], h9_ref[:, 2 * LANES : 14 * LANES])
+
     grad1 = []
     for x in range(8):
         total = jnp.zeros((C, LANES), jnp.float32)
@@ -558,8 +567,9 @@
             total += part
         grad1.append((total * slope1_ref[:, plane_cols(x)] * own_row).astype(jnp.bfloat16))
 
-    shifted_ref[...] = jnp.zeros_like(shifted_ref)
     for a in range(3):
+        for x in [*range(a), *range(a + 8, 10)]:
+            shifted_ref[C * a : C * (a + 1), plane_cols(x)] = empty
         for x in range(8):
             shifted_ref[C * a : C * (a + 1), plane_cols(x + a)] = grad1[x]
     first_part = matmul_lanes(
@@ -681,9 +691,9 @@
             pltpu.VMEM((9 * C, 16 * LANES), bf16),
             pltpu.VMEM((3 * C, 18 * LANES), f32),
             pltpu.VMEM((C, 8 * LANES), f32),
-            pltpu.VMEM((C, 12 * LANES), f32),
             pltpu.VMEM((C, 12 * LANES), bf16),
             pltpu.VMEM((C, 12 * LANES), bf16),
+            pltpu.VMEM((3 * C, 12 * LANES), bf16),
             pltpu.VMEM((3 * C, 12 * LANES), bf16),
             pltpu.VMEM((9 * C, 8 * LANES), f32),
         ],

time: 48 us -> 48.1 us (level)
  no operation moved by 1% of the time
where the time goes in v1:
time: 48.1 us; the launch traced here: 47.7 us
  blocking collectives  23 us (48%)
  starting transfers between devices  7.61 us (16%)
  waiting for transfers between devices  5.82 us (12%)
  Pallas kernels  5.79 us (12%)
  local copies, waits for them, and re-layouts  4.77 us (10%)
  between operations  0.7 us (1%)
    all_to_all x2, blocking collectives, exchange(): lax.all_to_all(values, ('dp', 'space'), 0, 0, axis_index_groups=groups, t...  23 us
    ppermute x5, starting transfers between devices, swap(): lax.ppermute(values, 'space', [(s, s ^ mask) for s in range(space_count)])  7.53 us
    unnamed x12, local copies, waits for them, and re-layouts  4.77 us
    pallas_call x1, Pallas kernels, on_device_flat(): pl.pallas_call(functools.partial(crop_kernel, scale), out_shape=(shape((8...  3.8 us
    ppermute x5, waiting for transfers between devices, swap(): lax.ppermute(values, 'space', [(s, s ^ mask) for s in range(space_count)])  2.95 us
    ppermute x2, waiting for transfers between devices, swap_cores(): return lax.ppermute(values, 'dp', [(d, d ^ 1) for d in range(dp_count)])  2.87 us
    pallas_call x1, Pallas kernels, on_device_flat(): pl.pallas_call(unpack_kernel, out_shape=(shape((27, C, C), f32), shape((2...  1.28 us
  transfers between devices with their start and end apart: 7, of which 4 were waited for; matrix products, arithmetic and copies ran while one was open for 0% of the time, Pallas kernels for 1%

profile of v1, /device:TPU:0, one launch (start us, length us, event | category | flops | bytes accessed | tf_op | source)
XLA Modules:
  0.0 47.7 jit_solution(12152501346327614048)
XLA Ops:
  0.6 3.0 %collective-permute-start = (bf16[1,1,48,512]{3,2,1,0:T(8,128)(2,1)}, bf16[1,1,48,512]{3,2,1,0:T(8,128)(2,1)S(1)}, u32[]{:S(2)}, u32[]{:S(2)}) collective-permute-start(bf16[1,1,48,512]{3,2,1,0:T(8,128)(2,1)} %param.6), channel_id=1, source_target_pairs={{0,1},{1,0},{2,3},{3,2},{4,5},{5,4},{6,7},{7,6},{8,9},{9,8},{10,11... | collective-permute-start | bytes 147464 | tf_op jit(solution)/shard_map/ppermute | solution.py:634
  3.6 0.1 collective-permute-start.1
  3.7 0.0 copy-start.4
  3.7 0.7 %copy-done.4 = s32[1,8]{1,0:T(1,128)S(1)} copy-done((s32[1,8]{1,0:T(1,128)S(1)}, s32[1,8]{1,0:T(1,128)}, u32[]{:S(2)}) %copy-start.4) | copy-done | bytes 56
  4.4 0.0 copy-start.2
  4.4 0.8 %copy-done.2 = bf16[1,1,48,512]{3,2,1,0:T(8,128)(2,1)S(1)} copy-done((bf16[1,1,48,512]{3,2,1,0:T(8,128)(2,1)S(1)}, bf16[1,1,48,512]{3,2,1,0:T(8,128)(2,1)}, u32[]{:S(2)}) %copy-start.2) | copy-done | bytes 49176
  5.2 0.0 copy-start.3
  5.2 0.7 %copy-done.3 = s32[1,1,3,512]{3,1,2,0:T(1,128)S(1)} copy-done((s32[1,1,3,512]{3,1,2,0:T(1,128)S(1)}, s32[1,1,3,512]{3,1,2,0:T(1,128)}, u32[]{:S(2)}) %copy-start.3) | copy-done | bytes 6168
  5.9 0.2 pack_own.1
  6.0 1.5 %collective-permute-done.1 = s32[1,1,3,512]{3,0,2,1:T(1,128)S(1)} collective-permute-done((s32[1,1,3,512]{3,0,2,1:T(1,128)}, s32[1,1,3,512]{3,0,2,1:T(1,128)S(1)}, u32[]{:S(2)}, u32[]{:S(2)}) %collective-permute-start.1) | collective-permute-done | bytes 6176 | tf_op jit(solution)/shard_map/ppermute | solution.py:634
  7.5 0.0 collective-permute-done
  7.5 0.2 pack_mate.1
  7.6 3.7 %collective-permute-start.2 = (bf16[2,8,16,128]{3,2,1,0:T(8,128)(2,1)S(1)}, bf16[2,8,16,128]{3,2,1,0:T(8,128)(2,1)S(1)}, u32[]{:S(2)}, u32[]{:S(2)}) collective-permute-start(bf16[2,8,16,128]{3,2,1,0:T(8,128)(2,1)S(1)} %get-tuple-element.29), channel_id=1, source_target_pairs={{0,6},{1,7},{2,4},{3,5},{4,2},{5,3},{6,0},{7,1},{8,14},{9,15},{10,... | collective-permute-start | bytes 196616 | tf_op jit(solution)/shard_map/ppermute | solution.py:634
  11.3 0.0 collective-permute-start.3
  11.3 0.8 %collective-permute-start.4 = (bf16[2,8,16,128]{3,2,1,0:T(8,128)(2,1)S(1)}, bf16[2,8,16,128]{3,2,1,0:T(8,128)(2,1)S(1)}, u32[]{:S(2)}, u32[]{:S(2)}) collective-permute-start(bf16[2,8,16,128]{3,2,1,0:T(8,128)(2,1)S(1)} %get-tuple-element.31), channel_id=1, source_target_pairs={{0,2},{1,3},{2,0},{3,1},{4,6},{5,7},{6,4},{7,5},{8,10},{9,11},{10,... | collective-permute-start | bytes 196616 | tf_op jit(solution)/shard_map/ppermute | solution.py:634
  12.1 0.0 copy-start.5
  12.1 0.7 %copy-done.5 = bf16[3,48]{1,0:T(4,128)(2,1)S(1)} copy-done((bf16[3,48]{1,0:T(4,128)(2,1)S(1)}, bf16[3,48]{1,0:T(4,128)(2,1)}, u32[]{:S(2)}) %copy-start.5) | copy-done | bytes 312
  12.8 0.0 copy-start
  12.8 1.0 %copy-done = bf16[48,27,48]{2,0,1:T(8,128)(2,1)S(1)} copy-done((bf16[48,27,48]{2,0,1:T(8,128)(2,1)S(1)}, bf16[48,27,48]{2,0,1:T(8,128)(2,1)}, u32[]{:S(2)}) %copy-start) | copy-done | bytes 124440
  13.8 0.0 copy-start.1
  13.8 1.0 %copy-done.1 = bf16[48,27,48]{2,0,1:T(8,128)(2,1)S(1)} copy-done((bf16[48,27,48]{2,0,1:T(8,128)(2,1)S(1)}, bf16[48,27,48]{2,0,1:T(8,128)(2,1)}, u32[]{:S(2)}) %copy-start.1) | copy-done | bytes 124440
  14.7 0.3 prepare.1
  15.1 0.0 collective-permute-done.2.refs_0_
  15.1 1.5 %collective-permute-done.3.refs_1_ = bf16[2,8,16,128]{3,2,1,0:T(8,128)(2,1)S(1)} collective-permute-done((bf16[2,8,16,128]{3,2,1,0:T(8,128)(2,1)S(1)}, bf16[2,8,16,128]{3,2,1,0:T(8,128)(2,1)S(1)}, u32[]{:S(2)}, u32[]{:S(2)}) %collective-permute-start.3) | collective-permute-done | bytes 65568 | tf_op jit(solution)/shard_map/ppermute | solution.py:634
  16.6 0.0 collective-permute-done.4.refs_2_
  16.6 3.8 %forward_backward.1 = (f32[8,512]{1,0:T(8,128)S(1)}, f32[512,128]{1,0:T(8,128)S(1)}, f32[512,128]{1,0:T(8,128)S(1)}) custom-call(s32[1,128]{1,0:T(1,128)S(1)} %get-tuple-element.24.owners_ref, f32[8,128]{1,0:T(8,128)S(1)} %get-tuple-element.25.masks_ref, bf16[13,16,128]{2,1,0:T(8,128)(2,1)S(1)} %get-tuple-element.26.own_ref, ...), custom_call_target="tpu_custom_call" | custom-call | tf_op jit(solution)/shard_map/forward_backward/pallas_call | solution.py:681
  20.4 0.1 collective-permute-start.5
  20.5 1.5 %collective-permute-done.5.other_ref = f32[512,128]{1,0:T(8,128)S(1)} collective-permute-done((f32[512,128]{1,0:T(8,128)S(1)}, f32[512,128]{1,0:T(8,128)S(1)}, u32[]{:S(2)}, u32[]{:S(2)}) %collective-permute-start.5) | collective-permute-done | bytes 262176 | tf_op jit(solution)/shard_map/ppermute | solution.py:707
  22.0 12.4 %all_to_all.10.parts_ref = bf16[16,32,128]{2,1,0:T(8,128)(2,1)S(1)} all-to-all(bf16[16,32,128]{2,1,0:T(8,128)(2,1)S(1)} %bitcast.14), channel_id=1, replica_groups={{0,1,2,3,4,5,6,7,16,17,18,19,20,21,22,23},{8,9,10,11,12,13,14,15,24,25,..., dimensions={0} | all-to-all | bytes 262144 | tf_op jit(solution)/shard_map/all_to_all | solution.py:716
  34.4 10.6 %all_to_all.11 = bf16[16,32,128]{2,1,0:T(8,128)(2,1)S(1)} all-to-all(bf16[16,32,128]{2,1,0:T(8,128)(2,1)S(1)} %gradient_sum.3), channel_id=1, replica_groups={{0,1,2,3,4,5,6,7,16,17,18,19,20,21,22,23},{8,9,10,11,12,13,14,15,24,25,..., dimensions={0} | all-to-all | bytes 262144 | tf_op jit(solution)/shard_map/all_to_all | solution.py:716
  45.1 0.0 collective-permute-start.6
  45.1 1.3 %collective-permute-done.6.other_ref = bf16[512,128]{1,0:T(8,128)(2,1)S(1)} collective-permute-done((bf16[512,128]{1,0:T(8,128)(2,1)S(1)}, bf16[512,128]{1,0:T(8,128)(2,1)S(1)}, u32[]{:S(2)}, u32[]{:S(2)}) %collective-permute-start.6) | collective-permute-done | bytes 131104 | tf_op jit(solution)/shard_map/ppermute | solution.py:707
  46.4 1.3 %unpack_gradients.1 = (f32[27,48,48]{2,1,0:T(8,128)}, f32[27,48,48]{2,1,0:T(8,128)}, f32[3,48]{1,0:T(4,128)}, f32[3,1,512]{2,1,0:T(1,128)}) custom-call(bf16[512,128]{1,0:T(8,128)(2,1)S(1)} %bitcast.16, bf16[512,128]{1,0:T(8,128)(2,1)S(1)} %collective-permute-done.6.other_ref, f32[8,512]{1,0:T(8,128)S(1)} %get-tuple-element.39.logits_ref), custom_call_target="tpu_custom_call" | custom-call | tf_op jit(solution)/shard_map/unpack_gradients/pallas_call | solution.py:734
  (2 shorter events, 0.1 us)
Async XLA Ops:
  0.6 6.8 %collective-permute-start = (bf16[1,1,48,512]{3,2,1,0:T(8,128)(2,1)}, bf16[1,1,48,512]{3,2,1,0:T(8,128)(2,1)S(1)}, u32[]{:S(2)}, u32[]{:S(2)}) collective-permute-start(bf16[1,1,48,512]{3,2,1,0:T(8,128)(2,1)} %param.6), channel_id=1, source_target_pairs={{0,1},{1,0},{2,3},{3,2},{4,5},{5,4},{6,7},{7,6},{8,9},{9,8},{10,11... | collective-permute-start | bytes 147464 | tf_op jit(solution)/shard_map/ppermute | solution.py:634
  3.6 3.8 %collective-permute-start.1 = (s32[1,1,3,512]{3,0,2,1:T(1,128)}, s32[1,1,3,512]{3,0,2,1:T(1,128)S(1)}, u32[]{:S(2)}, u32[]{:S(2)}) collective-permute-start(s32[1,1,3,512]{3,0,2,1:T(1,128)} %bitcast.22), channel_id=1, source_target_pairs={{0,1},{1,0},{2,3},{3,2},{4,5},{5,4},{6,7},{7,6},{8,9},{9,8},{10,11... | collective-permute-start | bytes 18440 | tf_op jit(solution)/shard_map/ppermute | solution.py:634
  3.7 0.7 %copy-start.4 = (s32[1,8]{1,0:T(1,128)S(1)}, s32[1,8]{1,0:T(1,128)}, u32[]{:S(2)}) copy-start(s32[1,8]{1,0:T(1,128)} %block_ref.5) | copy-start | bytes 100
  4.4 0.8 %copy-start.2 = (bf16[1,1,48,512]{3,2,1,0:T(8,128)(2,1)S(1)}, bf16[1,1,48,512]{3,2,1,0:T(8,128)(2,1)}, u32[]{:S(2)}) copy-start(bf16[1,1,48,512]{3,2,1,0:T(8,128)(2,1)} %param.6) | copy-start | bytes 147460
  5.2 0.7 %copy-start.3 = (s32[1,1,3,512]{3,1,2,0:T(1,128)S(1)}, s32[1,1,3,512]{3,1,2,0:T(1,128)}, u32[]{:S(2)}) copy-start(s32[1,1,3,512]{3,1,2,0:T(1,128)} %param.11) | copy-start | bytes 18436
  7.6 7.4 %collective-permute-start.2 = (bf16[2,8,16,128]{3,2,1,0:T(8,128)(2,1)S(1)}, bf16[2,8,16,128]{3,2,1,0:T(8,128)(2,1)S(1)}, u32[]{:S(2)}, u32[]{:S(2)}) collective-permute-start(bf16[2,8,16,128]{3,2,1,0:T(8,128)(2,1)S(1)} %get-tuple-element.29), channel_id=1, source_target_pairs={{0,6},{1,7},{2,4},{3,5},{4,2},{5,3},{6,0},{7,1},{8,14},{9,15},{10,... | collective-permute-start | bytes 196616 | tf_op jit(solution)/shard_map/ppermute | solution.py:634
  11.3 5.3 %collective-permute-start.3 = (bf16[2,8,16,128]{3,2,1,0:T(8,128)(2,1)S(1)}, bf16[2,8,16,128]{3,2,1,0:T(8,128)(2,1)S(1)}, u32[]{:S(2)}, u32[]{:S(2)}) collective-permute-start(bf16[2,8,16,128]{3,2,1,0:T(8,128)(2,1)S(1)} %get-tuple-element.30), channel_id=1, source_target_pairs={{0,4},{1,5},{2,6},{3,7},{4,0},{5,1},{6,2},{7,3},{8,12},{9,13},{10,... | collective-permute-start | bytes 196616 | tf_op jit(solution)/shard_map/ppermute | solution.py:634
  11.3 5.3 %collective-permute-start.4 = (bf16[2,8,16,128]{3,2,1,0:T(8,128)(2,1)S(1)}, bf16[2,8,16,128]{3,2,1,0:T(8,128)(2,1)S(1)}, u32[]{:S(2)}, u32[]{:S(2)}) collective-permute-start(bf16[2,8,16,128]{3,2,1,0:T(8,128)(2,1)S(1)} %get-tuple-element.31), channel_id=1, source_target_pairs={{0,2},{1,3},{2,0},{3,1},{4,6},{5,7},{6,4},{7,5},{8,10},{9,11},{10,... | collective-permute-start | bytes 196616 | tf_op jit(solution)/shard_map/ppermute | solution.py:634
  12.1 0.7 %copy-start.5 = (bf16[3,48]{1,0:T(4,128)(2,1)S(1)}, bf16[3,48]{1,0:T(4,128)(2,1)}, u32[]{:S(2)}) copy-start(bf16[3,48]{1,0:T(4,128)(2,1)} %head_ref.1) | copy-start | bytes 868
  12.8 1.0 %copy-start = (bf16[48,27,48]{2,0,1:T(8,128)(2,1)S(1)}, bf16[48,27,48]{2,0,1:T(8,128)(2,1)}, u32[]{:S(2)}) copy-start(bf16[48,27,48]{2,0,1:T(8,128)(2,1)} %param.8) | copy-start | bytes 373252
  13.8 1.0 %copy-start.1 = (bf16[48,27,48]{2,0,1:T(8,128)(2,1)S(1)}, bf16[48,27,48]{2,0,1:T(8,128)(2,1)}, u32[]{:S(2)}) copy-start(bf16[48,27,48]{2,0,1:T(8,128)(2,1)} %param.9) | copy-start | bytes 373252
  20.4 1.6 %collective-permute-start.5 = (f32[512,128]{1,0:T(8,128)S(1)}, f32[512,128]{1,0:T(8,128)S(1)}, u32[]{:S(2)}, u32[]{:S(2)}) collective-permute-start(f32[512,128]{1,0:T(8,128)S(1)} %get-tuple-element.38), channel_id=1, source_target_pairs={{0,8},{8,0},{16,24},{24,16},{1,9},{9,1},{17,25},{25,17},{2,10},{10... | collective-permute-start | bytes 786440 | tf_op jit(solution)/shard_map/ppermute | solution.py:707
  45.1 1.3 %collective-permute-start.6 = (bf16[512,128]{1,0:T(8,128)(2,1)S(1)}, bf16[512,128]{1,0:T(8,128)(2,1)S(1)}, u32[]{:S(2)}, u32[]{:S(2)}) collective-permute-start(bf16[512,128]{1,0:T(8,128)(2,1)S(1)} %bitcast.15), channel_id=1, source_target_pairs={{0,8},{8,0},{16,24},{24,16},{1,9},{9,1},{17,25},{25,17},{2,10},{10... | collective-permute-start | bytes 393224 | tf_op jit(solution)/shard_map/ppermute | solution.py:707

commit v2 on v0

--- a/solution.py
+++ b/solution.py
@@ -193,7 +193,7 @@
     return (target >> 2) - (source >> 2), (target & 3) - (source & 3)
 
 
-PARTNERS = (6, 4, 2)
+PARTNERS = (6, 2, 4)
 
 
 def block_tiles(features_ref, targets_ref):
@@ -244,7 +244,9 @@
     return jnp.where(dx > 0, 0, jnp.where(dx < 0, 1, jnp.where(dy > 0, 2, 3)))
 
 
-def pack_own_kernel(block_ref, features_ref, targets_ref, own_ref, slabs_ref, cases_ref):
+def pack_own_kernel(
+    block_ref, features_ref, targets_ref, head_ref, own_ref, slabs_ref, h_ref, ht_ref, cases_ref
+):
     blocks = listed_blocks(block_ref, lax.axis_index("space"))
     tiles, rows = block_tiles(features_ref, targets_ref)
     for ct in range(3):
@@ -254,6 +256,10 @@
     write_cases(tiles, rows, cases_ref)
     for n, k in enumerate(PARTNERS):
         slabs_ref[n] = cases_ref[case_of(blocks[0], blocks[k])]
+    head = head_ref[...].astype(jnp.float32)
+    head = jnp.concatenate([head, jnp.zeros((13, C), jnp.float32)], axis=0)
+    h_ref[...] = head.astype(jnp.bfloat16)
+    ht_ref[...] = head.T.astype(jnp.bfloat16)
 
 
 def pack_mate_kernel(block_ref, features_ref, targets_ref, slabs_ref, mate_ref, *refs):
@@ -278,12 +284,9 @@
     block_ref,
     first_ref,
     second_ref,
-    head_ref,
     w1_ref,
     w2_ref,
     w2t_ref,
-    h_ref,
-    ht_ref,
     owners_ref,
     masks_ref,
     table_ref,
@@ -292,10 +295,6 @@
     whole = stacked_taps(second_ref)
     w2_ref[...] = whole
     w2t_ref[...] = whole.T
-    head = head_ref[...].astype(jnp.float32)
-    head = jnp.concatenate([head, jnp.zeros((13, C), jnp.float32)], axis=0)
-    h_ref[...] = head.astype(jnp.bfloat16)
-    ht_ref[...] = head.T.astype(jnp.bfloat16)
 
     blocks = listed_blocks(block_ref, lax.axis_index("space"))
     for slot in range(10):
@@ -624,16 +623,21 @@
         return lax.ppermute(values, "space", [(s, s ^ mask) for s in range(space_count)])
 
     mate_targets, mate_features = swap(targets, 1), swap(features, 1)
-    own, own_slabs = pl.pallas_call(
+    own, own_slabs, head, head_t = pl.pallas_call(
         pack_own_kernel,
-        out_shape=(shape((13, 16, LANES), bf16), shape((3, 8, 16, LANES), bf16)),
-        in_specs=[vmem] * 3,
-        out_specs=(vmem,) * 2,
+        out_shape=(
+            shape((13, 16, LANES), bf16),
+            shape((3, 8, 16, LANES), bf16),
+            shape((16, C), bf16),
+            shape((C, 16), bf16),
+        ),
+        in_specs=[vmem] * 4,
+        out_specs=(vmem,) * 4,
         scratch_shapes=[pltpu.VMEM((4, 8, 16, LANES), bf16)],
         compiler_params=small,
         cost_estimate=pl.CostEstimate(flops=1_000_000, bytes_accessed=2_000_000, transcendentals=0),
         name="pack_own",
-    )(device_block, features[0, 0], targets[0].transpose(1, 0, 2))
+    )(device_block, features[0, 0], targets[0].transpose(1, 0, 2), head_weight)
     mate_slab, *pairs = pl.pallas_call(
         pack_mate_kernel,
         out_shape=(
@@ -648,24 +652,22 @@
     )(device_block, mate_features[0, 0], mate_targets[0].transpose(1, 0, 2), own_slabs)
     pairs = [swap(pair, mask) for pair, mask in zip(pairs, PARTNERS)]
 
-    w1, w2, w2t, head, head_t, owners, masks = pl.pallas_call(
+    w1, w2, w2t, owners, masks = pl.pallas_call(
         prepare_kernel,
         out_shape=(
             shape((3 * C, 9 * C), bf16),
             shape((3 * C, 9 * C), bf16),
             shape((9 * C, 3 * C), bf16),
-            shape((16, C), bf16),
-            shape((C, 16), bf16),
             shape((1, LANES), jnp.int32),
             shape((8, LANES), f32),
         ),
-        in_specs=[vmem] * 4,
-        out_specs=(vmem,) * 7,
+        in_specs=[vmem] * 3,
+        out_specs=(vmem,) * 5,
         scratch_shapes=[pltpu.SMEM((2, 16), jnp.int32)],
         compiler_params=small,
         cost_estimate=pl.CostEstimate(flops=2_000_000, bytes_accessed=4_000_000, transcendentals=0),
         name="prepare",
-    )(device_block, conv_first.transpose(1, 0, 2), conv_second.transpose(1, 0, 2), head_weight)
+    )(device_block, conv_first.transpose(1, 0, 2), conv_second.transpose(1, 0, 2))
 
     scale = (device_count * 3 * CELLS) ** (-0.5)
     logits, keep, send = pl.pallas_call(

time: 48 us -> 48.6 us (1.012)
  blocking collectives: 23 us -> 23.7 us
  local copies, waits for them, and re-layouts: 4.77 us -> 4.13 us
  waiting for transfers between devices: 5.82 us -> 6.36 us
    all_to_all x2, blocking collectives: 23 us -> 23.7 us  [exchange(): lax.all_to_all(values, ('dp', 'space'), 0, 0, axis_index_groups=groups, t...]
    unnamed x12, local copies, waits for them, and re-layouts: 4.77 us -> 4.13 us
    ppermute x5, waiting for transfers between devices: 2.95 us -> 3.5 us  [swap(): lax.ppermute(values, 'space', [(s, s ^ mask) for s in range(space_count)])]
  transfers between devices with their start and end apart: 7 -> 7, of which waited for: 4 -> 5; matrix products, arithmetic and copies ran while one was open for 0% -> 0% of each run, Pallas kernels for 1% -> 1%
where the time goes in v2:
time: 48.6 us; the launch traced here: 48.3 us
  blocking collectives  23.7 us (49%)
  starting transfers between devices  7.61 us (16%)
  waiting for transfers between devices  6.36 us (13%)
  Pallas kernels  5.73 us (12%)
  local copies, waits for them, and re-layouts  4.13 us (8%)
  between operations  0.69 us (1%)
    all_to_all x2, blocking collectives, exchange(): lax.all_to_all(values, ('dp', 'space'), 0, 0, axis_index_groups=groups, t...  23.7 us
    ppermute x5, starting transfers between devices, swap(): lax.ppermute(values, 'space', [(s, s ^ mask) for s in range(space_count)])  7.53 us
    unnamed x12, local copies, waits for them, and re-layouts  4.13 us
    pallas_call x1, Pallas kernels, on_device_flat(): pl.pallas_call(functools.partial(crop_kernel, scale), out_shape=(shape((8...  3.74 us
    ppermute x5, waiting for transfers between devices, swap(): lax.ppermute(values, 'space', [(s, s ^ mask) for s in range(space_count)])  3.5 us
    ppermute x2, waiting for transfers between devices, swap_cores(): return lax.ppermute(values, 'dp', [(d, d ^ 1) for d in range(dp_count)])  2.87 us
    pallas_call x1, Pallas kernels, on_device_flat(): pl.pallas_call(unpack_kernel, out_shape=(shape((27, C, C), f32), shape((2...  1.28 us
  transfers between devices with their start and end apart: 7, of which 5 were waited for; matrix products, arithmetic and copies ran while one was open for 0% of the time, Pallas kernels for 1%

profile of v2, /device:TPU:0, one launch (start us, length us, event | category | flops | bytes accessed | tf_op | source)
XLA Modules:
  0.0 48.3 jit_solution(6483546403146457590)
XLA Ops:
  0.6 3.0 %collective-permute-start = (bf16[1,1,48,512]{3,2,1,0:T(8,128)(2,1)}, bf16[1,1,48,512]{3,2,1,0:T(8,128)(2,1)S(1)}, u32[]{:S(2)}, u32[]{:S(2)}) collective-permute-start(bf16[1,1,48,512]{3,2,1,0:T(8,128)(2,1)} %param.6), channel_id=1, source_target_pairs={{0,1},{1,0},{2,3},{3,2},{4,5},{5,4},{6,7},{7,6},{8,9},{9,8},{10,11... | collective-permute-start | bytes 147464 | tf_op jit(solution)/shard_map/ppermute | solution.py:623
  3.6 0.1 collective-permute-start.1
  3.7 0.0 copy-start.4
  3.7 0.0 copy-start.5
  3.7 0.7 %copy-done.4 = s32[1,8]{1,0:T(1,128)S(1)} copy-done((s32[1,8]{1,0:T(1,128)S(1)}, s32[1,8]{1,0:T(1,128)}, u32[]{:S(2)}) %copy-start.4) | copy-done | bytes 56
  4.4 0.0 copy-done.5
  4.4 0.0 copy-start.2
  4.4 0.8 %copy-done.2 = bf16[1,1,48,512]{3,2,1,0:T(8,128)(2,1)S(1)} copy-done((bf16[1,1,48,512]{3,2,1,0:T(8,128)(2,1)S(1)}, bf16[1,1,48,512]{3,2,1,0:T(8,128)(2,1)}, u32[]{:S(2)}) %copy-start.2) | copy-done | bytes 49176
  5.2 0.0 copy-start.3
  5.2 0.7 %copy-done.3 = s32[1,1,3,512]{3,1,2,0:T(1,128)S(1)} copy-done((s32[1,1,3,512]{3,1,2,0:T(1,128)S(1)}, s32[1,1,3,512]{3,1,2,0:T(1,128)}, u32[]{:S(2)}) %copy-start.3) | copy-done | bytes 6168
  5.9 0.2 pack_own.1
  6.1 1.4 %collective-permute-done.1 = s32[1,1,3,512]{3,0,2,1:T(1,128)S(1)} collective-permute-done((s32[1,1,3,512]{3,0,2,1:T(1,128)}, s32[1,1,3,512]{3,0,2,1:T(1,128)S(1)}, u32[]{:S(2)}, u32[]{:S(2)}) %collective-permute-start.1) | collective-permute-done | bytes 6176 | tf_op jit(solution)/shard_map/ppermute | solution.py:623
  7.5 0.0 collective-permute-done
  7.5 0.2 pack_mate.1
  7.6 3.7 %collective-permute-start.2 = (bf16[2,8,16,128]{3,2,1,0:T(8,128)(2,1)S(1)}, bf16[2,8,16,128]{3,2,1,0:T(8,128)(2,1)S(1)}, u32[]{:S(2)}, u32[]{:S(2)}) collective-permute-start(bf16[2,8,16,128]{3,2,1,0:T(8,128)(2,1)S(1)} %get-tuple-element.29), channel_id=1, source_target_pairs={{0,6},{1,7},{2,4},{3,5},{4,2},{5,3},{6,0},{7,1},{8,14},{9,15},{10,... | collective-permute-start | bytes 196616 | tf_op jit(solution)/shard_map/ppermute | solution.py:623
  11.3 0.0 collective-permute-start.3
  11.3 0.8 %collective-permute-start.4 = (bf16[2,8,16,128]{3,2,1,0:T(8,128)(2,1)S(1)}, bf16[2,8,16,128]{3,2,1,0:T(8,128)(2,1)S(1)}, u32[]{:S(2)}, u32[]{:S(2)}) collective-permute-start(bf16[2,8,16,128]{3,2,1,0:T(8,128)(2,1)S(1)} %get-tuple-element.31), channel_id=1, source_target_pairs={{0,4},{1,5},{2,6},{3,7},{4,0},{5,1},{6,2},{7,3},{8,12},{9,13},{10,... | collective-permute-start | bytes 196616 | tf_op jit(solution)/shard_map/ppermute | solution.py:623
  12.1 0.0 copy-start
  12.1 1.0 %copy-done = bf16[48,27,48]{2,0,1:T(8,128)(2,1)S(1)} copy-done((bf16[48,27,48]{2,0,1:T(8,128)(2,1)S(1)}, bf16[48,27,48]{2,0,1:T(8,128)(2,1)}, u32[]{:S(2)}) %copy-start) | copy-done | bytes 124440
  13.1 0.0 copy-start.1
  13.1 1.0 %copy-done.1 = bf16[48,27,48]{2,0,1:T(8,128)(2,1)S(1)} copy-done((bf16[48,27,48]{2,0,1:T(8,128)(2,1)S(1)}, bf16[48,27,48]{2,0,1:T(8,128)(2,1)}, u32[]{:S(2)}) %copy-start.1) | copy-done | bytes 124440
  14.0 0.3 prepare.1
  14.4 0.0 collective-permute-done.2.refs_0_
  14.4 1.2 %collective-permute-done.3.refs_1_ = bf16[2,8,16,128]{3,2,1,0:T(8,128)(2,1)S(1)} collective-permute-done((bf16[2,8,16,128]{3,2,1,0:T(8,128)(2,1)S(1)}, bf16[2,8,16,128]{3,2,1,0:T(8,128)(2,1)S(1)}, u32[]{:S(2)}, u32[]{:S(2)}) %collective-permute-start.3) | collective-permute-done | bytes 65568 | tf_op jit(solution)/shard_map/ppermute | solution.py:623
  15.6 0.9 %collective-permute-done.4.refs_2_ = bf16[2,8,16,128]{3,2,1,0:T(8,128)(2,1)S(1)} collective-permute-done((bf16[2,8,16,128]{3,2,1,0:T(8,128)(2,1)S(1)}, bf16[2,8,16,128]{3,2,1,0:T(8,128)(2,1)S(1)}, u32[]{:S(2)}, u32[]{:S(2)}) %collective-permute-start.4) | collective-permute-done | bytes 65568 | tf_op jit(solution)/shard_map/ppermute | solution.py:623
  16.5 3.7 %forward_backward.1 = (f32[8,512]{1,0:T(8,128)S(1)}, f32[512,128]{1,0:T(8,128)S(1)}, f32[512,128]{1,0:T(8,128)S(1)}) custom-call(s32[1,128]{1,0:T(1,128)S(1)} %get-tuple-element.24.owners_ref, f32[8,128]{1,0:T(8,128)S(1)} %get-tuple-element.25.masks_ref, bf16[13,16,128]{2,1,0:T(8,128)(2,1)S(1)} %get-tuple-element.26.own_ref, ...), custom_call_target="tpu_custom_call" | custom-call | tf_op jit(solution)/shard_map/forward_backward/pallas_call | solution.py:673
  20.2 0.1 collective-permute-start.5
  20.3 1.5 %collective-permute-done.5.other_ref = f32[512,128]{1,0:T(8,128)S(1)} collective-permute-done((f32[512,128]{1,0:T(8,128)S(1)}, f32[512,128]{1,0:T(8,128)S(1)}, u32[]{:S(2)}, u32[]{:S(2)}) %collective-permute-start.5) | collective-permute-done | bytes 262176 | tf_op jit(solution)/shard_map/ppermute | solution.py:699
  21.9 13.1 %all_to_all.10.parts_ref = bf16[16,32,128]{2,1,0:T(8,128)(2,1)S(1)} all-to-all(bf16[16,32,128]{2,1,0:T(8,128)(2,1)S(1)} %bitcast.14), channel_id=1, replica_groups={{0,1,2,3,4,5,6,7,16,17,18,19,20,21,22,23},{8,9,10,11,12,13,14,15,24,25,..., dimensions={0} | all-to-all | bytes 262144 | tf_op jit(solution)/shard_map/all_to_all | solution.py:708
  35.0 10.6 %all_to_all.11 = bf16[16,32,128]{2,1,0:T(8,128)(2,1)S(1)} all-to-all(bf16[16,32,128]{2,1,0:T(8,128)(2,1)S(1)} %gradient_sum.3), channel_id=1, replica_groups={{0,1,2,3,4,5,6,7,16,17,18,19,20,21,22,23},{8,9,10,11,12,13,14,15,24,25,..., dimensions={0} | all-to-all | bytes 262144 | tf_op jit(solution)/shard_map/all_to_all | solution.py:708
  45.6 0.0 collective-permute-start.6
  45.6 1.3 %collective-permute-done.6.other_ref = bf16[512,128]{1,0:T(8,128)(2,1)S(1)} collective-permute-done((bf16[512,128]{1,0:T(8,128)(2,1)S(1)}, bf16[512,128]{1,0:T(8,128)(2,1)S(1)}, u32[]{:S(2)}, u32[]{:S(2)}) %collective-permute-start.6) | collective-permute-done | bytes 131104 | tf_op jit(solution)/shard_map/ppermute | solution.py:699
  47.0 1.3 %unpack_gradients.1 = (f32[27,48,48]{2,1,0:T(8,128)}, f32[27,48,48]{2,1,0:T(8,128)}, f32[3,48]{1,0:T(4,128)}, f32[3,1,512]{2,1,0:T(1,128)}) custom-call(bf16[512,128]{1,0:T(8,128)(2,1)S(1)} %bitcast.16, bf16[512,128]{1,0:T(8,128)(2,1)S(1)} %collective-permute-done.6.other_ref, f32[8,512]{1,0:T(8,128)S(1)} %get-tuple-element.39.logits_ref), custom_call_target="tpu_custom_call" | custom-call | tf_op jit(solution)/shard_map/unpack_gradients/pallas_call | solution.py:726
  (2 shorter events, 0.1 us)
Async XLA Ops:
  0.6 6.8 %collective-permute-start = (bf16[1,1,48,512]{3,2,1,0:T(8,128)(2,1)}, bf16[1,1,48,512]{3,2,1,0:T(8,128)(2,1)S(1)}, u32[]{:S(2)}, u32[]{:S(2)}) collective-permute-start(bf16[1,1,48,512]{3,2,1,0:T(8,128)(2,1)} %param.6), channel_id=1, source_target_pairs={{0,1},{1,0},{2,3},{3,2},{4,5},{5,4},{6,7},{7,6},{8,9},{9,8},{10,11... | collective-permute-start | bytes 147464 | tf_op jit(solution)/shard_map/ppermute | solution.py:623
  3.6 3.8 %collective-permute-start.1 = (s32[1,1,3,512]{3,0,2,1:T(1,128)}, s32[1,1,3,512]{3,0,2,1:T(1,128)S(1)}, u32[]{:S(2)}, u32[]{:S(2)}) collective-permute-start(s32[1,1,3,512]{3,0,2,1:T(1,128)} %bitcast.22), channel_id=1, source_target_pairs={{0,1},{1,0},{2,3},{3,2},{4,5},{5,4},{6,7},{7,6},{8,9},{9,8},{10,11... | collective-permute-start | bytes 18440 | tf_op jit(solution)/shard_map/ppermute | solution.py:623
  3.7 0.7 %copy-start.4 = (s32[1,8]{1,0:T(1,128)S(1)}, s32[1,8]{1,0:T(1,128)}, u32[]{:S(2)}) copy-start(s32[1,8]{1,0:T(1,128)} %block_ref.5) | copy-start | bytes 100
  3.7 0.7 %copy-start.5 = (bf16[3,48]{1,0:T(4,128)(2,1)S(1)}, bf16[3,48]{1,0:T(4,128)(2,1)}, u32[]{:S(2)}) copy-start(bf16[3,48]{1,0:T(4,128)(2,1)} %head_ref.1) | copy-start | bytes 868
  4.4 0.8 %copy-start.2 = (bf16[1,1,48,512]{3,2,1,0:T(8,128)(2,1)S(1)}, bf16[1,1,48,512]{3,2,1,0:T(8,128)(2,1)}, u32[]{:S(2)}) copy-start(bf16[1,1,48,512]{3,2,1,0:T(8,128)(2,1)} %param.6) | copy-start | bytes 147460
  5.2 0.7 %copy-start.3 = (s32[1,1,3,512]{3,1,2,0:T(1,128)S(1)}, s32[1,1,3,512]{3,1,2,0:T(1,128)}, u32[]{:S(2)}) copy-start(s32[1,1,3,512]{3,1,2,0:T(1,128)} %param.11) | copy-start | bytes 18436
  7.6 6.7 %collective-permute-start.2 = (bf16[2,8,16,128]{3,2,1,0:T(8,128)(2,1)S(1)}, bf16[2,8,16,128]{3,2,1,0:T(8,128)(2,1)S(1)}, u32[]{:S(2)}, u32[]{:S(2)}) collective-permute-start(bf16[2,8,16,128]{3,2,1,0:T(8,128)(2,1)S(1)} %get-tuple-element.29), channel_id=1, source_target_pairs={{0,6},{1,7},{2,4},{3,5},{4,2},{5,3},{6,0},{7,1},{8,14},{9,15},{10,... | collective-permute-start | bytes 196616 | tf_op jit(solution)/shard_map/ppermute | solution.py:623
  11.3 4.3 %collective-permute-start.3 = (bf16[2,8,16,128]{3,2,1,0:T(8,128)(2,1)S(1)}, bf16[2,8,16,128]{3,2,1,0:T(8,128)(2,1)S(1)}, u32[]{:S(2)}, u32[]{:S(2)}) collective-permute-start(bf16[2,8,16,128]{3,2,1,0:T(8,128)(2,1)S(1)} %get-tuple-element.30), channel_id=1, source_target_pairs={{0,2},{1,3},{2,0},{3,1},{4,6},{5,7},{6,4},{7,5},{8,10},{9,11},{10,... | collective-permute-start | bytes 196616 | tf_op jit(solution)/shard_map/ppermute | solution.py:623
  11.3 5.2 %collective-permute-start.4 = (bf16[2,8,16,128]{3,2,1,0:T(8,128)(2,1)S(1)}, bf16[2,8,16,128]{3,2,1,0:T(8,128)(2,1)S(1)}, u32[]{:S(2)}, u32[]{:S(2)}) collective-permute-start(bf16[2,8,16,128]{3,2,1,0:T(8,128)(2,1)S(1)} %get-tuple-element.31), channel_id=1, source_target_pairs={{0,4},{1,5},{2,6},{3,7},{4,0},{5,1},{6,2},{7,3},{8,12},{9,13},{10,... | collective-permute-start | bytes 196616 | tf_op jit(solution)/shard_map/ppermute | solution.py:623
  12.1 1.0 %copy-start = (bf16[48,27,48]{2,0,1:T(8,128)(2,1)S(1)}, bf16[48,27,48]{2,0,1:T(8,128)(2,1)}, u32[]{:S(2)}) copy-start(bf16[48,27,48]{2,0,1:T(8,128)(2,1)} %param.8) | copy-start | bytes 373252
  13.1 1.0 %copy-start.1 = (bf16[48,27,48]{2,0,1:T(8,128)(2,1)S(1)}, bf16[48,27,48]{2,0,1:T(8,128)(2,1)}, u32[]{:S(2)}) copy-start(bf16[48,27,48]{2,0,1:T(8,128)(2,1)} %param.9) | copy-start | bytes 373252
  20.2 1.6 %collective-permute-start.5 = (f32[512,128]{1,0:T(8,128)S(1)}, f32[512,128]{1,0:T(8,128)S(1)}, u32[]{:S(2)}, u32[]{:S(2)}) collective-permute-start(f32[512,128]{1,0:T(8,128)S(1)} %get-tuple-element.38), channel_id=1, source_target_pairs={{0,8},{8,0},{16,24},{24,16},{1,9},{9,1},{17,25},{25,17},{2,10},{10... | collective-permute-start | bytes 786440 | tf_op jit(solution)/shard_map/ppermute | solution.py:699
  45.6 1.3 %collective-permute-start.6 = (bf16[512,128]{1,0:T(8,128)(2,1)S(1)}, bf16[512,128]{1,0:T(8,128)(2,1)S(1)}, u32[]{:S(2)}, u32[]{:S(2)}) collective-permute-start(bf16[512,128]{1,0:T(8,128)(2,1)S(1)} %bitcast.15), channel_id=1, source_target_pairs={{0,8},{8,0},{16,24},{24,16},{1,9},{9,1},{17,25},{25,17},{2,10},{10... | collective-permute-start | bytes 393224 | tf_op jit(solution)/shard_map/ppermute | solution.py:699

commit v3 on v0

--- a/solution.py
+++ b/solution.py
@@ -193,7 +193,7 @@
     return (target >> 2) - (source >> 2), (target & 3) - (source & 3)
 
 
-PARTNERS = (6, 4, 2)
+PARTNERS = (4, 6, 2)
 
 
 def block_tiles(features_ref, targets_ref):
@@ -244,6 +244,13 @@
     return jnp.where(dx > 0, 0, jnp.where(dx < 0, 1, jnp.where(dy > 0, 2, 3)))
 
 
+def head_kernel(head_ref, h_ref, ht_ref):
+    head = head_ref[...].astype(jnp.float32)
+    head = jnp.concatenate([head, jnp.zeros((13, C), jnp.float32)], axis=0)
+    h_ref[...] = head.astype(jnp.bfloat16)
+    ht_ref[...] = head.T.astype(jnp.bfloat16)
+
+
 def pack_own_kernel(block_ref, features_ref, targets_ref, own_ref, slabs_ref, cases_ref):
     blocks = listed_blocks(block_ref, lax.axis_index("space"))
     tiles, rows = block_tiles(features_ref, targets_ref)
@@ -274,28 +281,14 @@
     return jnp.concatenate(rows, axis=0)
 
 
-def prepare_kernel(
-    block_ref,
-    first_ref,
-    second_ref,
-    head_ref,
-    w1_ref,
-    w2_ref,
-    w2t_ref,
-    h_ref,
-    ht_ref,
-    owners_ref,
-    masks_ref,
-    table_ref,
-):
-    w1_ref[...] = stacked_taps(first_ref)
+def second_kernel(second_ref, w2_ref, w2t_ref):
     whole = stacked_taps(second_ref)
     w2_ref[...] = whole
     w2t_ref[...] = whole.T
-    head = head_ref[...].astype(jnp.float32)
-    head = jnp.concatenate([head, jnp.zeros((13, C), jnp.float32)], axis=0)
-    h_ref[...] = head.astype(jnp.bfloat16)
-    ht_ref[...] = head.T.astype(jnp.bfloat16)
+
+
+def prepare_kernel(block_ref, first_ref, w1_ref, owners_ref, masks_ref, table_ref):
+    w1_ref[...] = stacked_taps(first_ref)
 
     blocks = listed_blocks(block_ref, lax.axis_index("space"))
     for slot in range(10):
@@ -624,6 +617,15 @@
         return lax.ppermute(values, "space", [(s, s ^ mask) for s in range(space_count)])
 
     mate_targets, mate_features = swap(targets, 1), swap(features, 1)
+    head, head_t = pl.pallas_call(
+        head_kernel,
+        out_shape=(shape((16, C), bf16), shape((C, 16), bf16)),
+        in_specs=[vmem],
+        out_specs=(vmem,) * 2,
+        compiler_params=small,
+        cost_estimate=pl.CostEstimate(flops=1_000_000, bytes_accessed=2_000_000, transcendentals=0),
+        name="lay_out_head",
+    )(head_weight)
     own, own_slabs = pl.pallas_call(
         pack_own_kernel,
         out_shape=(shape((13, 16, LANES), bf16), shape((3, 8, 16, LANES), bf16)),
@@ -644,28 +646,34 @@
         out_specs=(vmem,) * 4,
         scratch_shapes=[pltpu.VMEM((4, 8, 16, LANES), bf16)],
         compiler_params=small,
+        cost_estimate=pl.CostEstimate(flops=1_000_000, bytes_accessed=2_000_000, transcendentals=0),
         name="pack_mate",
     )(device_block, mate_features[0, 0], mate_targets[0].transpose(1, 0, 2), own_slabs)
     pairs = [swap(pair, mask) for pair, mask in zip(pairs, PARTNERS)]
 
-    w1, w2, w2t, head, head_t, owners, masks = pl.pallas_call(
+    w1, owners, masks = pl.pallas_call(
         prepare_kernel,
         out_shape=(
             shape((3 * C, 9 * C), bf16),
-            shape((3 * C, 9 * C), bf16),
-            shape((9 * C, 3 * C), bf16),
-            shape((16, C), bf16),
-            shape((C, 16), bf16),
             shape((1, LANES), jnp.int32),
             shape((8, LANES), f32),
         ),
-        in_specs=[vmem] * 4,
-        out_specs=(vmem,) * 7,
+        in_specs=[vmem] * 2,
+        out_specs=(vmem,) * 3,
         scratch_shapes=[pltpu.SMEM((2, 16), jnp.int32)],
         compiler_params=small,
         cost_estimate=pl.CostEstimate(flops=2_000_000, bytes_accessed=4_000_000, transcendentals=0),
         name="prepare",
-    )(device_block, conv_first.transpose(1, 0, 2), conv_second.transpose(1, 0, 2), head_weight)
+    )(device_block, conv_first.transpose(1, 0, 2))
+    w2, w2t = pl.pallas_call(
+        second_kernel,
+        out_shape=(shape((3 * C, 9 * C), bf16), shape((9 * C, 3 * C), bf16)),
+        in_specs=[vmem],
+        out_specs=(vmem,) * 2,
+        compiler_params=small,
+        cost_estimate=pl.CostEstimate(flops=2_000_000, bytes_accessed=4_000_000, transcendentals=0),
+        name="second_weights",
+    )(conv_second.transpose(1, 0, 2))
 
     scale = (device_count * 3 * CELLS) ** (-0.5)
     logits, keep, send = pl.pallas_call(

time: 48 us -> 47.9 us (level)
  waiting for transfers between devices: 5.82 us -> 6.79 us
  local copies, waits for them, and re-layouts: 4.77 us -> 3.88 us
    ppermute x5, waiting for transfers between devices: 2.95 us -> 3.92 us  [swap(): lax.ppermute(values, 'space', [(s, s ^ mask) for s in range(space_count)])]
    unnamed x12, local copies, waits for them, and re-layouts: 4.77 us -> 3.88 us
  transfers between devices with their start and end apart: 7 -> 7, of which waited for: 4 -> 6; matrix products, arithmetic and copies ran while one was open for 0% -> 0% of each run, Pallas kernels for 1% -> 1%
where the time goes in v3:
time: 47.9 us; the launch traced here: 47.5 us
  blocking collectives  22.9 us (48%)
  starting transfers between devices  7.39 us (15%)
  waiting for transfers between devices  6.79 us (14%)
  Pallas kernels  5.91 us (12%)
  local copies, waits for them, and re-layouts  3.88 us (8%)
  between operations  0.7 us (1%)
    all_to_all x2, blocking collectives, exchange(): lax.all_to_all(values, ('dp', 'space'), 0, 0, axis_index_groups=groups, t...  22.9 us
    ppermute x5, starting transfers between devices, swap(): lax.ppermute(values, 'space', [(s, s ^ mask) for s in range(space_count)])  7.31 us
    ppermute x5, waiting for transfers between devices, swap(): lax.ppermute(values, 'space', [(s, s ^ mask) for s in range(space_count)])  3.92 us
    unnamed x12, local copies, waits for them, and re-layouts  3.88 us
    pallas_call x1, Pallas kernels, on_device_flat(): pl.pallas_call(functools.partial(crop_kernel, scale), out_shape=(shape((8...  3.74 us
    ppermute x2, waiting for transfers between devices, swap_cores(): return lax.ppermute(values, 'dp', [(d, d ^ 1) for d in range(dp_count)])  2.87 us
    pallas_call x1, Pallas kernels, on_device_flat(): pl.pallas_call(unpack_kernel, out_shape=(shape((27, C, C), f32), shape((2...  1.28 us
  transfers between devices with their start and end apart: 7, of which 6 were waited for; matrix products, arithmetic and copies ran while one was open for 0% of the time, Pallas kernels for 1%

profile of v3, /device:TPU:0, one launch (start us, length us, event | category | flops | bytes accessed | tf_op | source)
XLA Modules:
  0.0 47.5 jit_solution(604174973443370464)
XLA Ops:
  0.6 3.0 %collective-permute-start = (bf16[1,1,48,512]{3,2,1,0:T(8,128)(2,1)}, bf16[1,1,48,512]{3,2,1,0:T(8,128)(2,1)S(1)}, u32[]{:S(2)}, u32[]{:S(2)}) collective-permute-start(bf16[1,1,48,512]{3,2,1,0:T(8,128)(2,1)} %param.6), channel_id=1, source_target_pairs={{0,1},{1,0},{2,3},{3,2},{4,5},{5,4},{6,7},{7,6},{8,9},{9,8},{10,11... | collective-permute-start | bytes 147464 | tf_op jit(solution)/shard_map/ppermute | solution.py:617
  3.6 0.1 collective-permute-start.1
  3.7 0.0 copy-start.4
  3.7 0.7 %copy-done.4 = s32[1,8]{1,0:T(1,128)S(1)} copy-done((s32[1,8]{1,0:T(1,128)S(1)}, s32[1,8]{1,0:T(1,128)}, u32[]{:S(2)}) %copy-start.4) | copy-done | bytes 56
  4.4 0.0 copy-start.2
  4.4 0.8 %copy-done.2 = bf16[1,1,48,512]{3,2,1,0:T(8,128)(2,1)S(1)} copy-done((bf16[1,1,48,512]{3,2,1,0:T(8,128)(2,1)S(1)}, bf16[1,1,48,512]{3,2,1,0:T(8,128)(2,1)}, u32[]{:S(2)}) %copy-start.2) | copy-done | bytes 49176
  5.2 0.0 copy-start.3
  5.2 0.7 %copy-done.3 = s32[1,1,3,512]{3,1,2,0:T(1,128)S(1)} copy-done((s32[1,1,3,512]{3,1,2,0:T(1,128)S(1)}, s32[1,1,3,512]{3,1,2,0:T(1,128)}, u32[]{:S(2)}) %copy-start.3) | copy-done | bytes 6168
  5.9 0.2 pack_own.1
  6.0 1.5 %collective-permute-done.1 = s32[1,1,3,512]{3,0,2,1:T(1,128)S(1)} collective-permute-done((s32[1,1,3,512]{3,0,2,1:T(1,128)}, s32[1,1,3,512]{3,0,2,1:T(1,128)S(1)}, u32[]{:S(2)}, u32[]{:S(2)}) %collective-permute-start.1) | collective-permute-done | bytes 6176 | tf_op jit(solution)/shard_map/ppermute | solution.py:617
  7.5 0.0 collective-permute-done
  7.5 0.2 pack_mate.1
  7.6 2.7 %collective-permute-start.2 = (bf16[2,8,16,128]{3,2,1,0:T(8,128)(2,1)S(1)}, bf16[2,8,16,128]{3,2,1,0:T(8,128)(2,1)S(1)}, u32[]{:S(2)}, u32[]{:S(2)}) collective-permute-start(bf16[2,8,16,128]{3,2,1,0:T(8,128)(2,1)S(1)} %get-tuple-element.29), channel_id=1, source_target_pairs={{0,4},{1,5},{2,6},{3,7},{4,0},{5,1},{6,2},{7,3},{8,12},{9,13},{10,... | collective-permute-start | bytes 196616 | tf_op jit(solution)/shard_map/ppermute | solution.py:617
  10.3 0.0 copy-start.5
  10.3 1.3 %collective-permute-start.3 = (bf16[2,8,16,128]{3,2,1,0:T(8,128)(2,1)S(1)}, bf16[2,8,16,128]{3,2,1,0:T(8,128)(2,1)S(1)}, u32[]{:S(2)}, u32[]{:S(2)}) collective-permute-start(bf16[2,8,16,128]{3,2,1,0:T(8,128)(2,1)S(1)} %get-tuple-element.30), channel_id=1, source_target_pairs={{0,6},{1,7},{2,4},{3,5},{4,2},{5,3},{6,0},{7,1},{8,14},{9,15},{10,... | collective-permute-start | bytes 196616 | tf_op jit(solution)/shard_map/ppermute | solution.py:617
  11.7 0.2 collective-permute-start.4
  11.9 0.0 copy-done.5
  11.9 0.1 lay_out_head.1
  12.0 0.0 copy-start
  12.0 1.0 %copy-done = bf16[48,27,48]{2,0,1:T(8,128)(2,1)S(1)} copy-done((bf16[48,27,48]{2,0,1:T(8,128)(2,1)S(1)}, bf16[48,27,48]{2,0,1:T(8,128)(2,1)}, u32[]{:S(2)}) %copy-start) | copy-done | bytes 124440
  12.9 0.0 copy-start.1
  12.9 0.2 prepare.1
  13.2 0.8 %copy-done.1 = bf16[48,27,48]{2,0,1:T(8,128)(2,1)S(1)} copy-done((bf16[48,27,48]{2,0,1:T(8,128)(2,1)S(1)}, bf16[48,27,48]{2,0,1:T(8,128)(2,1)}, u32[]{:S(2)}) %copy-start.1) | copy-done | bytes 124440
  13.9 0.2 second_weights.1
  14.2 0.6 %collective-permute-done.2.refs_0_ = bf16[2,8,16,128]{3,2,1,0:T(8,128)(2,1)S(1)} collective-permute-done((bf16[2,8,16,128]{3,2,1,0:T(8,128)(2,1)S(1)}, bf16[2,8,16,128]{3,2,1,0:T(8,128)(2,1)S(1)}, u32[]{:S(2)}, u32[]{:S(2)}) %collective-permute-start.2) | collective-permute-done | bytes 65568 | tf_op jit(solution)/shard_map/ppermute | solution.py:617
  14.8 1.7 %collective-permute-done.3.refs_1_ = bf16[2,8,16,128]{3,2,1,0:T(8,128)(2,1)S(1)} collective-permute-done((bf16[2,8,16,128]{3,2,1,0:T(8,128)(2,1)S(1)}, bf16[2,8,16,128]{3,2,1,0:T(8,128)(2,1)S(1)}, u32[]{:S(2)}, u32[]{:S(2)}) %collective-permute-start.3) | collective-permute-done | bytes 65568 | tf_op jit(solution)/shard_map/ppermute | solution.py:617
  16.5 0.1 collective-permute-done.4.refs_2_
  16.6 3.7 %forward_backward.1 = (f32[8,512]{1,0:T(8,128)S(1)}, f32[512,128]{1,0:T(8,128)S(1)}, f32[512,128]{1,0:T(8,128)S(1)}) custom-call(s32[1,128]{1,0:T(1,128)S(1)} %get-tuple-element.24.owners_ref, f32[8,128]{1,0:T(8,128)S(1)} %get-tuple-element.25.masks_ref, bf16[13,16,128]{2,1,0:T(8,128)(2,1)S(1)} %get-tuple-element.26.own_ref, ...), custom_call_target="tpu_custom_call" | custom-call | tf_op jit(solution)/shard_map/forward_backward/pallas_call | solution.py:679
  20.4 0.1 collective-permute-start.5
  20.5 1.5 %collective-permute-done.5.other_ref = f32[512,128]{1,0:T(8,128)S(1)} collective-permute-done((f32[512,128]{1,0:T(8,128)S(1)}, f32[512,128]{1,0:T(8,128)S(1)}, u32[]{:S(2)}, u32[]{:S(2)}) %collective-permute-start.5) | collective-permute-done | bytes 262176 | tf_op jit(solution)/shard_map/ppermute | solution.py:705
  22.0 12.2 %all_to_all.10.parts_ref = bf16[16,32,128]{2,1,0:T(8,128)(2,1)S(1)} all-to-all(bf16[16,32,128]{2,1,0:T(8,128)(2,1)S(1)} %bitcast.14), channel_id=1, replica_groups={{0,1,2,3,4,5,6,7,16,17,18,19,20,21,22,23},{8,9,10,11,12,13,14,15,24,25,..., dimensions={0} | all-to-all | bytes 262144 | tf_op jit(solution)/shard_map/all_to_all | solution.py:714
  34.3 10.6 %all_to_all.11 = bf16[16,32,128]{2,1,0:T(8,128)(2,1)S(1)} all-to-all(bf16[16,32,128]{2,1,0:T(8,128)(2,1)S(1)} %gradient_sum.3), channel_id=1, replica_groups={{0,1,2,3,4,5,6,7,16,17,18,19,20,21,22,23},{8,9,10,11,12,13,14,15,24,25,..., dimensions={0} | all-to-all | bytes 262144 | tf_op jit(solution)/shard_map/all_to_all | solution.py:714
  44.9 0.0 collective-permute-start.6
  44.9 1.3 %collective-permute-done.6.other_ref = bf16[512,128]{1,0:T(8,128)(2,1)S(1)} collective-permute-done((bf16[512,128]{1,0:T(8,128)(2,1)S(1)}, bf16[512,128]{1,0:T(8,128)(2,1)S(1)}, u32[]{:S(2)}, u32[]{:S(2)}) %collective-permute-start.6) | collective-permute-done | bytes 131104 | tf_op jit(solution)/shard_map/ppermute | solution.py:705
  46.2 1.3 %unpack_gradients.1 = (f32[27,48,48]{2,1,0:T(8,128)}, f32[27,48,48]{2,1,0:T(8,128)}, f32[3,48]{1,0:T(4,128)}, f32[3,1,512]{2,1,0:T(1,128)}) custom-call(bf16[512,128]{1,0:T(8,128)(2,1)S(1)} %bitcast.16, bf16[512,128]{1,0:T(8,128)(2,1)S(1)} %collective-permute-done.6.other_ref, f32[8,512]{1,0:T(8,128)S(1)} %get-tuple-element.39.logits_ref), custom_call_target="tpu_custom_call" | custom-call | tf_op jit(solution)/shard_map/unpack_gradients/pallas_call | solution.py:732
  (2 shorter events, 0.1 us)
Async XLA Ops:
  0.6 6.8 %collective-permute-start = (bf16[1,1,48,512]{3,2,1,0:T(8,128)(2,1)}, bf16[1,1,48,512]{3,2,1,0:T(8,128)(2,1)S(1)}, u32[]{:S(2)}, u32[]{:S(2)}) collective-permute-start(bf16[1,1,48,512]{3,2,1,0:T(8,128)(2,1)} %param.6), channel_id=1, source_target_pairs={{0,1},{1,0},{2,3},{3,2},{4,5},{5,4},{6,7},{7,6},{8,9},{9,8},{10,11... | collective-permute-start | bytes 147464 | tf_op jit(solution)/shard_map/ppermute | solution.py:617
  3.6 3.8 %collective-permute-start.1 = (s32[1,1,3,512]{3,0,2,1:T(1,128)}, s32[1,1,3,512]{3,0,2,1:T(1,128)S(1)}, u32[]{:S(2)}, u32[]{:S(2)}) collective-permute-start(s32[1,1,3,512]{3,0,2,1:T(1,128)} %bitcast.22), channel_id=1, source_target_pairs={{0,1},{1,0},{2,3},{3,2},{4,5},{5,4},{6,7},{7,6},{8,9},{9,8},{10,11... | collective-permute-start | bytes 18440 | tf_op jit(solution)/shard_map/ppermute | solution.py:617
  3.7 0.7 %copy-start.4 = (s32[1,8]{1,0:T(1,128)S(1)}, s32[1,8]{1,0:T(1,128)}, u32[]{:S(2)}) copy-start(s32[1,8]{1,0:T(1,128)} %block_ref.5) | copy-start | bytes 100
  4.4 0.8 %copy-start.2 = (bf16[1,1,48,512]{3,2,1,0:T(8,128)(2,1)S(1)}, bf16[1,1,48,512]{3,2,1,0:T(8,128)(2,1)}, u32[]{:S(2)}) copy-start(bf16[1,1,48,512]{3,2,1,0:T(8,128)(2,1)} %param.6) | copy-start | bytes 147460
  5.2 0.7 %copy-start.3 = (s32[1,1,3,512]{3,1,2,0:T(1,128)S(1)}, s32[1,1,3,512]{3,1,2,0:T(1,128)}, u32[]{:S(2)}) copy-start(s32[1,1,3,512]{3,1,2,0:T(1,128)} %param.11) | copy-start | bytes 18436
  7.6 7.1 %collective-permute-start.2 = (bf16[2,8,16,128]{3,2,1,0:T(8,128)(2,1)S(1)}, bf16[2,8,16,128]{3,2,1,0:T(8,128)(2,1)S(1)}, u32[]{:S(2)}, u32[]{:S(2)}) collective-permute-start(bf16[2,8,16,128]{3,2,1,0:T(8,128)(2,1)S(1)} %get-tuple-element.29), channel_id=1, source_target_pairs={{0,4},{1,5},{2,6},{3,7},{4,0},{5,1},{6,2},{7,3},{8,12},{9,13},{10,... | collective-permute-start | bytes 196616 | tf_op jit(solution)/shard_map/ppermute | solution.py:617
  10.3 1.6 %copy-start.5 = (bf16[3,48]{1,0:T(4,128)(2,1)S(1)}, bf16[3,48]{1,0:T(4,128)(2,1)}, u32[]{:S(2)}) copy-start(bf16[3,48]{1,0:T(4,128)(2,1)} %head_ref.1) | copy-start | bytes 868
  10.3 6.2 %collective-permute-start.3 = (bf16[2,8,16,128]{3,2,1,0:T(8,128)(2,1)S(1)}, bf16[2,8,16,128]{3,2,1,0:T(8,128)(2,1)S(1)}, u32[]{:S(2)}, u32[]{:S(2)}) collective-permute-start(bf16[2,8,16,128]{3,2,1,0:T(8,128)(2,1)S(1)} %get-tuple-element.30), channel_id=1, source_target_pairs={{0,6},{1,7},{2,4},{3,5},{4,2},{5,3},{6,0},{7,1},{8,14},{9,15},{10,... | collective-permute-start | bytes 196616 | tf_op jit(solution)/shard_map/ppermute | solution.py:617
  11.7 5.0 %collective-permute-start.4 = (bf16[2,8,16,128]{3,2,1,0:T(8,128)(2,1)S(1)}, bf16[2,8,16,128]{3,2,1,0:T(8,128)(2,1)S(1)}, u32[]{:S(2)}, u32[]{:S(2)}) collective-permute-start(bf16[2,8,16,128]{3,2,1,0:T(8,128)(2,1)S(1)} %get-tuple-element.31), channel_id=1, source_target_pairs={{0,2},{1,3},{2,0},{3,1},{4,6},{5,7},{6,4},{7,5},{8,10},{9,11},{10,... | collective-permute-start | bytes 196616 | tf_op jit(solution)/shard_map/ppermute | solution.py:617
  12.0 1.0 %copy-start = (bf16[48,27,48]{2,0,1:T(8,128)(2,1)S(1)}, bf16[48,27,48]{2,0,1:T(8,128)(2,1)}, u32[]{:S(2)}) copy-start(bf16[48,27,48]{2,0,1:T(8,128)(2,1)} %param.8) | copy-start | bytes 373252
  12.9 1.0 %copy-start.1 = (bf16[48,27,48]{2,0,1:T(8,128)(2,1)S(1)}, bf16[48,27,48]{2,0,1:T(8,128)(2,1)}, u32[]{:S(2)}) copy-start(bf16[48,27,48]{2,0,1:T(8,128)(2,1)} %param.9) | copy-start | bytes 373252
  20.4 1.6 %collective-permute-start.5 = (f32[512,128]{1,0:T(8,128)S(1)}, f32[512,128]{1,0:T(8,128)S(1)}, u32[]{:S(2)}, u32[]{:S(2)}) collective-permute-start(f32[512,128]{1,0:T(8,128)S(1)} %get-tuple-element.38), channel_id=1, source_target_pairs={{0,8},{8,0},{16,24},{24,16},{1,9},{9,1},{17,25},{25,17},{2,10},{10... | collective-permute-start | bytes 786440 | tf_op jit(solution)/shard_map/ppermute | solution.py:705
  44.9 1.3 %collective-permute-start.6 = (bf16[512,128]{1,0:T(8,128)(2,1)S(1)}, bf16[512,128]{1,0:T(8,128)(2,1)S(1)}, u32[]{:S(2)}, u32[]{:S(2)}) collective-permute-start(bf16[512,128]{1,0:T(8,128)(2,1)S(1)} %bitcast.15), channel_id=1, source_target_pairs={{0,8},{8,0},{16,24},{24,16},{1,9},{9,1},{17,25},{25,17},{2,10},{10... | collective-permute-start | bytes 393224 | tf_op jit(solution)/shard_map/ppermute | solution.py:705

commit v4 on v3

--- a/solution.py
+++ b/solution.py
@@ -206,8 +206,7 @@
     return tiles, [targets[:, LANES * q : LANES * (q + 1)] for q in range(4)]
 
 
-def write_cases(tiles, rows, cases_ref):
-    lane = lanes(16)
+def write_cases(tiles, rows, cases_ref, lane):
     left = lane < 64
     cell = lane & 63
     target_tile = jnp.concatenate(rows, axis=0)
@@ -251,14 +250,20 @@
     ht_ref[...] = head.T.astype(jnp.bfloat16)
 
 
-def pack_own_kernel(block_ref, features_ref, targets_ref, own_ref, slabs_ref, cases_ref):
+def lanes_kernel(out_ref):
+    out_ref[...] = lanes(16)
+
+
+def pack_own_kernel(
+    block_ref, features_ref, targets_ref, lane_ref, own_ref, slabs_ref, cases_ref
+):
     blocks = listed_blocks(block_ref, lax.axis_index("space"))
     tiles, rows = block_tiles(features_ref, targets_ref)
     for ct in range(3):
         for q in range(4):
             own_ref[4 * ct + q] = tiles[ct][q]
     own_ref[12] = jnp.concatenate(rows, axis=0).astype(jnp.bfloat16)
-    write_cases(tiles, rows, cases_ref)
+    write_cases(tiles, rows, cases_ref, lane_ref[...])
     for n, k in enumerate(PARTNERS):
         slabs_ref[n] = cases_ref[case_of(blocks[0], blocks[k])]
 
@@ -266,7 +271,7 @@
 def pack_mate_kernel(block_ref, features_ref, targets_ref, slabs_ref, mate_ref, *refs):
     *pair_refs, cases_ref = refs
     blocks = listed_blocks(block_ref, lax.axis_index("space"))
-    write_cases(*block_tiles(features_ref, targets_ref), cases_ref)
+    write_cases(*block_tiles(features_ref, targets_ref), cases_ref, lanes(16))
     mate_ref[...] = cases_ref[case_of(blocks[1], blocks[0])]
     for n, (k, ref) in enumerate(zip(PARTNERS, pair_refs)):
         ref[0] = slabs_ref[n]
@@ -626,16 +631,24 @@
         cost_estimate=pl.CostEstimate(flops=1_000_000, bytes_accessed=2_000_000, transcendentals=0),
         name="lay_out_head",
     )(head_weight)
+    lane = pl.pallas_call(
+        lanes_kernel,
+        out_shape=shape((16, LANES), jnp.int32),
+        out_specs=vmem,
+        compiler_params=small,
+        cost_estimate=pl.CostEstimate(flops=0, bytes_accessed=2_000_000, transcendentals=0),
+        name="lane_indices",
+    )()
     own, own_slabs = pl.pallas_call(
         pack_own_kernel,
         out_shape=(shape((13, 16, LANES), bf16), shape((3, 8, 16, LANES), bf16)),
-        in_specs=[vmem] * 3,
+        in_specs=[vmem] * 4,
         out_specs=(vmem,) * 2,
         scratch_shapes=[pltpu.VMEM((4, 8, 16, LANES), bf16)],
         compiler_params=small,
         cost_estimate=pl.CostEstimate(flops=1_000_000, bytes_accessed=2_000_000, transcendentals=0),
         name="pack_own",
-    )(device_block, features[0, 0], targets[0].transpose(1, 0, 2))
+    )(device_block, features[0, 0], targets[0].transpose(1, 0, 2), lane)
     mate_slab, *pairs = pl.pallas_call(
         pack_mate_kernel,
         out_shape=(

time: 47.9 us -> 47.8 us (level)
  local copies, waits for them, and re-layouts: 3.88 us -> 3.19 us
  waiting for transfers between devices: 6.79 us -> 7.46 us
    unnamed x12, local copies, waits for them, and re-layouts: 3.88 us -> 3.19 us
    ppermute x5, waiting for transfers between devices: 3.92 us -> 4.6 us  [swap(): lax.ppermute(values, 'space', [(s, s ^ mask) for s in range(space_count)])]
where the time goes in v4:
time: 47.8 us; the launch traced here: 47.5 us
  blocking collectives  22.8 us (48%)
  waiting for transfers between devices  7.46 us (16%)
  starting transfers between devices  7.4 us (15%)
  Pallas kernels  5.92 us (12%)
  local copies, waits for them, and re-layouts  3.19 us (7%)
  between operations  0.7 us (1%)
    all_to_all x2, blocking collectives, exchange(): lax.all_to_all(values, ('dp', 'space'), 0, 0, axis_index_groups=groups, t...  22.8 us
    ppermute x5, starting transfers between devices, swap(): lax.ppermute(values, 'space', [(s, s ^ mask) for s in range(space_count)])  7.33 us
    ppermute x5, waiting for transfers between devices, swap(): lax.ppermute(values, 'space', [(s, s ^ mask) for s in range(space_count)])  4.6 us
    pallas_call x1, Pallas kernels, on_device_flat(): pl.pallas_call(functools.partial(crop_kernel, scale), out_shape=(shape((8...  3.75 us
    unnamed x12, local copies, waits for them, and re-layouts  3.19 us
    ppermute x2, waiting for transfers between devices, swap_cores(): return lax.ppermute(values, 'dp', [(d, d ^ 1) for d in range(dp_count)])  2.87 us
    pallas_call x1, Pallas kernels, on_device_flat(): pl.pallas_call(unpack_kernel, out_shape=(shape((27, C, C), f32), shape((2...  1.28 us
  transfers between devices with their start and end apart: 7, of which 6 were waited for; matrix products, arithmetic and copies ran while one was open for 0% of the time, Pallas kernels for 1%

profile of v4, /device:TPU:0, one launch (start us, length us, event | category | flops | bytes accessed | tf_op | source)
XLA Modules:
  0.0 47.5 jit_solution(9033210594861863101)
XLA Ops:
  0.6 3.0 %collective-permute-start = (bf16[1,1,48,512]{3,2,1,0:T(8,128)(2,1)}, bf16[1,1,48,512]{3,2,1,0:T(8,128)(2,1)S(1)}, u32[]{:S(2)}, u32[]{:S(2)}) collective-permute-start(bf16[1,1,48,512]{3,2,1,0:T(8,128)(2,1)} %param.6), channel_id=1, source_target_pairs={{0,1},{1,0},{2,3},{3,2},{4,5},{5,4},{6,7},{7,6},{8,9},{9,8},{10,11... | collective-permute-start | bytes 147464 | tf_op jit(solution)/shard_map/ppermute | solution.py:622
  3.6 0.0 copy-start.3
  3.6 0.1 collective-permute-start.1
  3.7 0.0 copy-start.4
  3.7 0.6 %copy-done.3 = s32[1,1,3,512]{3,1,2,0:T(1,128)S(1)} copy-done((s32[1,1,3,512]{3,1,2,0:T(1,128)S(1)}, s32[1,1,3,512]{3,1,2,0:T(1,128)}, u32[]{:S(2)}) %copy-start.3) | copy-done | bytes 6168
  4.3 0.1 copy-done.4
  4.4 0.0 copy-start.2
  4.4 0.8 %copy-done.2 = bf16[1,1,48,512]{3,2,1,0:T(8,128)(2,1)S(1)} copy-done((bf16[1,1,48,512]{3,2,1,0:T(8,128)(2,1)S(1)}, bf16[1,1,48,512]{3,2,1,0:T(8,128)(2,1)}, u32[]{:S(2)}) %copy-start.2) | copy-done | bytes 49176
  5.2 0.2 pack_own.1
  5.3 2.1 %collective-permute-done.1 = s32[1,1,3,512]{3,0,2,1:T(1,128)S(1)} collective-permute-done((s32[1,1,3,512]{3,0,2,1:T(1,128)}, s32[1,1,3,512]{3,0,2,1:T(1,128)S(1)}, u32[]{:S(2)}, u32[]{:S(2)}) %collective-permute-start.1) | collective-permute-done | bytes 6176 | tf_op jit(solution)/shard_map/ppermute | solution.py:622
  7.5 0.0 collective-permute-done
  7.5 0.2 pack_mate.1
  7.6 2.7 %collective-permute-start.2 = (bf16[2,8,16,128]{3,2,1,0:T(8,128)(2,1)S(1)}, bf16[2,8,16,128]{3,2,1,0:T(8,128)(2,1)S(1)}, u32[]{:S(2)}, u32[]{:S(2)}) collective-permute-start(bf16[2,8,16,128]{3,2,1,0:T(8,128)(2,1)S(1)} %get-tuple-element.29), channel_id=1, source_target_pairs={{0,4},{1,5},{2,6},{3,7},{4,0},{5,1},{6,2},{7,3},{8,12},{9,13},{10,... | collective-permute-start | bytes 196616 | tf_op jit(solution)/shard_map/ppermute | solution.py:622
  10.3 0.0 copy-start.5
  10.3 1.3 %collective-permute-start.3 = (bf16[2,8,16,128]{3,2,1,0:T(8,128)(2,1)S(1)}, bf16[2,8,16,128]{3,2,1,0:T(8,128)(2,1)S(1)}, u32[]{:S(2)}, u32[]{:S(2)}) collective-permute-start(bf16[2,8,16,128]{3,2,1,0:T(8,128)(2,1)S(1)} %get-tuple-element.30), channel_id=1, source_target_pairs={{0,6},{1,7},{2,4},{3,5},{4,2},{5,3},{6,0},{7,1},{8,14},{9,15},{10,... | collective-permute-start | bytes 196616 | tf_op jit(solution)/shard_map/ppermute | solution.py:622
  11.7 0.2 collective-permute-start.4
  11.9 0.0 copy-done.5
  11.9 0.1 lay_out_head.1
  12.0 0.0 copy-start
  12.0 1.0 %copy-done = bf16[48,27,48]{2,0,1:T(8,128)(2,1)S(1)} copy-done((bf16[48,27,48]{2,0,1:T(8,128)(2,1)S(1)}, bf16[48,27,48]{2,0,1:T(8,128)(2,1)}, u32[]{:S(2)}) %copy-start) | copy-done | bytes 124440
  12.9 0.0 copy-start.1
  12.9 0.2 prepare.1
  13.2 0.8 %copy-done.1 = bf16[48,27,48]{2,0,1:T(8,128)(2,1)S(1)} copy-done((bf16[48,27,48]{2,0,1:T(8,128)(2,1)S(1)}, bf16[48,27,48]{2,0,1:T(8,128)(2,1)}, u32[]{:S(2)}) %copy-start.1) | copy-done | bytes 124440
  13.9 0.2 second_weights.1
  14.2 0.6 %collective-permute-done.2.refs_0_ = bf16[2,8,16,128]{3,2,1,0:T(8,128)(2,1)S(1)} collective-permute-done((bf16[2,8,16,128]{3,2,1,0:T(8,128)(2,1)S(1)}, bf16[2,8,16,128]{3,2,1,0:T(8,128)(2,1)S(1)}, u32[]{:S(2)}, u32[]{:S(2)}) %collective-permute-start.2) | collective-permute-done | bytes 65568 | tf_op jit(solution)/shard_map/ppermute | solution.py:622
  14.8 1.7 %collective-permute-done.3.refs_1_ = bf16[2,8,16,128]{3,2,1,0:T(8,128)(2,1)S(1)} collective-permute-done((bf16[2,8,16,128]{3,2,1,0:T(8,128)(2,1)S(1)}, bf16[2,8,16,128]{3,2,1,0:T(8,128)(2,1)S(1)}, u32[]{:S(2)}, u32[]{:S(2)}) %collective-permute-start.3) | collective-permute-done | bytes 65568 | tf_op jit(solution)/shard_map/ppermute | solution.py:622
  16.5 0.1 collective-permute-done.4.refs_2_
  16.6 3.8 %forward_backward.1 = (f32[8,512]{1,0:T(8,128)S(1)}, f32[512,128]{1,0:T(8,128)S(1)}, f32[512,128]{1,0:T(8,128)S(1)}) custom-call(s32[1,128]{1,0:T(1,128)S(1)} %get-tuple-element.24.owners_ref, f32[8,128]{1,0:T(8,128)S(1)} %get-tuple-element.25.masks_ref, bf16[13,16,128]{2,1,0:T(8,128)(2,1)S(1)} %get-tuple-element.26.own_ref, ...), custom_call_target="tpu_custom_call" | custom-call | tf_op jit(solution)/shard_map/forward_backward/pallas_call | solution.py:692
  20.4 0.1 collective-permute-start.5
  20.5 1.5 %collective-permute-done.5.other_ref = f32[512,128]{1,0:T(8,128)S(1)} collective-permute-done((f32[512,128]{1,0:T(8,128)S(1)}, f32[512,128]{1,0:T(8,128)S(1)}, u32[]{:S(2)}, u32[]{:S(2)}) %collective-permute-start.5) | collective-permute-done | bytes 262176 | tf_op jit(solution)/shard_map/ppermute | solution.py:718
  22.0 12.2 %all_to_all.10.parts_ref = bf16[16,32,128]{2,1,0:T(8,128)(2,1)S(1)} all-to-all(bf16[16,32,128]{2,1,0:T(8,128)(2,1)S(1)} %bitcast.14), channel_id=1, replica_groups={{0,1,2,3,4,5,6,7,16,17,18,19,20,21,22,23},{8,9,10,11,12,13,14,15,24,25,..., dimensions={0} | all-to-all | bytes 262144 | tf_op jit(solution)/shard_map/all_to_all | solution.py:727
  34.2 10.6 %all_to_all.11 = bf16[16,32,128]{2,1,0:T(8,128)(2,1)S(1)} all-to-all(bf16[16,32,128]{2,1,0:T(8,128)(2,1)S(1)} %gradient_sum.3), channel_id=1, replica_groups={{0,1,2,3,4,5,6,7,16,17,18,19,20,21,22,23},{8,9,10,11,12,13,14,15,24,25,..., dimensions={0} | all-to-all | bytes 262144 | tf_op jit(solution)/shard_map/all_to_all | solution.py:727
  44.8 0.0 collective-permute-start.6
  44.8 1.3 %collective-permute-done.6.other_ref = bf16[512,128]{1,0:T(8,128)(2,1)S(1)} collective-permute-done((bf16[512,128]{1,0:T(8,128)(2,1)S(1)}, bf16[512,128]{1,0:T(8,128)(2,1)S(1)}, u32[]{:S(2)}, u32[]{:S(2)}) %collective-permute-start.6) | collective-permute-done | bytes 131104 | tf_op jit(solution)/shard_map/ppermute | solution.py:718
  46.2 1.3 %unpack_gradients.1 = (f32[27,48,48]{2,1,0:T(8,128)}, f32[27,48,48]{2,1,0:T(8,128)}, f32[3,48]{1,0:T(4,128)}, f32[3,1,512]{2,1,0:T(1,128)}) custom-call(bf16[512,128]{1,0:T(8,128)(2,1)S(1)} %bitcast.16, bf16[512,128]{1,0:T(8,128)(2,1)S(1)} %collective-permute-done.6.other_ref, f32[8,512]{1,0:T(8,128)S(1)} %get-tuple-element.39.logits_ref), custom_call_target="tpu_custom_call" | custom-call | tf_op jit(solution)/shard_map/unpack_gradients/pallas_call | solution.py:745
  (3 shorter events, 0.1 us)
Async XLA Ops:
  0.6 6.8 %collective-permute-start = (bf16[1,1,48,512]{3,2,1,0:T(8,128)(2,1)}, bf16[1,1,48,512]{3,2,1,0:T(8,128)(2,1)S(1)}, u32[]{:S(2)}, u32[]{:S(2)}) collective-permute-start(bf16[1,1,48,512]{3,2,1,0:T(8,128)(2,1)} %param.6), channel_id=1, source_target_pairs={{0,1},{1,0},{2,3},{3,2},{4,5},{5,4},{6,7},{7,6},{8,9},{9,8},{10,11... | collective-permute-start | bytes 147464 | tf_op jit(solution)/shard_map/ppermute | solution.py:622
  3.6 0.7 %copy-start.3 = (s32[1,1,3,512]{3,1,2,0:T(1,128)S(1)}, s32[1,1,3,512]{3,1,2,0:T(1,128)}, u32[]{:S(2)}) copy-start(s32[1,1,3,512]{3,1,2,0:T(1,128)} %param.11) | copy-start | bytes 18436
  3.6 3.8 %collective-permute-start.1 = (s32[1,1,3,512]{3,0,2,1:T(1,128)}, s32[1,1,3,512]{3,0,2,1:T(1,128)S(1)}, u32[]{:S(2)}, u32[]{:S(2)}) collective-permute-start(s32[1,1,3,512]{3,0,2,1:T(1,128)} %bitcast.22), channel_id=1, source_target_pairs={{0,1},{1,0},{2,3},{3,2},{4,5},{5,4},{6,7},{7,6},{8,9},{9,8},{10,11... | collective-permute-start | bytes 18440 | tf_op jit(solution)/shard_map/ppermute | solution.py:622
  3.7 0.7 %copy-start.4 = (s32[1,8]{1,0:T(1,128)S(1)}, s32[1,8]{1,0:T(1,128)}, u32[]{:S(2)}) copy-start(s32[1,8]{1,0:T(1,128)} %block_ref.5) | copy-start | bytes 100
  4.4 0.8 %copy-start.2 = (bf16[1,1,48,512]{3,2,1,0:T(8,128)(2,1)S(1)}, bf16[1,1,48,512]{3,2,1,0:T(8,128)(2,1)}, u32[]{:S(2)}) copy-start(bf16[1,1,48,512]{3,2,1,0:T(8,128)(2,1)} %param.6) | copy-start | bytes 147460
  7.6 7.1 %collective-permute-start.2 = (bf16[2,8,16,128]{3,2,1,0:T(8,128)(2,1)S(1)}, bf16[2,8,16,128]{3,2,1,0:T(8,128)(2,1)S(1)}, u32[]{:S(2)}, u32[]{:S(2)}) collective-permute-start(bf16[2,8,16,128]{3,2,1,0:T(8,128)(2,1)S(1)} %get-tuple-element.29), channel_id=1, source_target_pairs={{0,4},{1,5},{2,6},{3,7},{4,0},{5,1},{6,2},{7,3},{8,12},{9,13},{10,... | collective-permute-start | bytes 196616 | tf_op jit(solution)/shard_map/ppermute | solution.py:622
  10.3 1.6 %copy-start.5 = (bf16[3,48]{1,0:T(4,128)(2,1)S(1)}, bf16[3,48]{1,0:T(4,128)(2,1)}, u32[]{:S(2)}) copy-start(bf16[3,48]{1,0:T(4,128)(2,1)} %head_ref.1) | copy-start | bytes 868
  10.3 6.2 %collective-permute-start.3 = (bf16[2,8,16,128]{3,2,1,0:T(8,128)(2,1)S(1)}, bf16[2,8,16,128]{3,2,1,0:T(8,128)(2,1)S(1)}, u32[]{:S(2)}, u32[]{:S(2)}) collective-permute-start(bf16[2,8,16,128]{3,2,1,0:T(8,128)(2,1)S(1)} %get-tuple-element.30), channel_id=1, source_target_pairs={{0,6},{1,7},{2,4},{3,5},{4,2},{5,3},{6,0},{7,1},{8,14},{9,15},{10,... | collective-permute-start | bytes 196616 | tf_op jit(solution)/shard_map/ppermute | solution.py:622
  11.7 5.0 %collective-permute-start.4 = (bf16[2,8,16,128]{3,2,1,0:T(8,128)(2,1)S(1)}, bf16[2,8,16,128]{3,2,1,0:T(8,128)(2,1)S(1)}, u32[]{:S(2)}, u32[]{:S(2)}) collective-permute-start(bf16[2,8,16,128]{3,2,1,0:T(8,128)(2,1)S(1)} %get-tuple-element.31), channel_id=1, source_target_pairs={{0,2},{1,3},{2,0},{3,1},{4,6},{5,7},{6,4},{7,5},{8,10},{9,11},{10,... | collective-permute-start | bytes 196616 | tf_op jit(solution)/shard_map/ppermute | solution.py:622
  12.0 1.0 %copy-start = (bf16[48,27,48]{2,0,1:T(8,128)(2,1)S(1)}, bf16[48,27,48]{2,0,1:T(8,128)(2,1)}, u32[]{:S(2)}) copy-start(bf16[48,27,48]{2,0,1:T(8,128)(2,1)} %param.8) | copy-start | bytes 373252
  12.9 1.0 %copy-start.1 = (bf16[48,27,48]{2,0,1:T(8,128)(2,1)S(1)}, bf16[48,27,48]{2,0,1:T(8,128)(2,1)}, u32[]{:S(2)}) copy-start(bf16[48,27,48]{2,0,1:T(8,128)(2,1)} %param.9) | copy-start | bytes 373252
  20.4 1.6 %collective-permute-start.5 = (f32[512,128]{1,0:T(8,128)S(1)}, f32[512,128]{1,0:T(8,128)S(1)}, u32[]{:S(2)}, u32[]{:S(2)}) collective-permute-start(f32[512,128]{1,0:T(8,128)S(1)} %get-tuple-element.38), channel_id=1, source_target_pairs={{0,8},{8,0},{16,24},{24,16},{1,9},{9,1},{17,25},{25,17},{2,10},{10... | collective-permute-start | bytes 786440 | tf_op jit(solution)/shard_map/ppermute | solution.py:718
  44.8 1.3 %collective-permute-start.6 = (bf16[512,128]{1,0:T(8,128)(2,1)S(1)}, bf16[512,128]{1,0:T(8,128)(2,1)S(1)}, u32[]{:S(2)}, u32[]{:S(2)}) collective-permute-start(bf16[512,128]{1,0:T(8,128)(2,1)S(1)} %bitcast.15), channel_id=1, source_target_pairs={{0,8},{8,0},{16,24},{24,16},{1,9},{9,1},{17,25},{25,17},{2,10},{10... | collective-permute-start | bytes 393224 | tf_op jit(solution)/shard_map/ppermute | solution.py:718

commit v5 on v4

--- a/solution.py
+++ b/solution.py
@@ -565,19 +565,30 @@
     )
 
     first_core = (lax.axis_index("dp") & 1) == 0
-    head_part = jnp.concatenate([head_part, jnp.zeros((24, 16), jnp.float32)], axis=0)
-    nothing = jnp.zeros((72, 16), jnp.float32)
+
+    def halves(part):
+        blocks = [part[24 * n : 24 * (n + 1)] for n in range(6)]
+        return [jnp.concatenate(blocks[side::2], axis=0) for side in range(2)]
+
+    pieces = [
+        halves(part[:, plane_cols(q)]) for part in (first_part, second_part) for q in range(3)
+    ]
     ends = []
-    for part, extra in ((first_part, nothing), (second_part, head_part)):
-        tail = jnp.concatenate([part[0:72, 384:], part[72:144, 384:], extra, nothing], axis=1)
+    for side, first, second in zip(
+        range(2), halves(first_part[:, 384:]), halves(second_part[:, 384:])
+    ):
+        head = jnp.concatenate(
+            [head_part[24 * side : 24 * (side + 1)], jnp.zeros((48, 16), jnp.float32)], axis=0
+        )
+        nothing = jnp.zeros((72, 16), jnp.float32)
+        tail = jnp.concatenate([first, second, head, nothing], axis=1)
         ends.append(jnp.concatenate([tail, jnp.zeros((8, LANES), jnp.float32)], axis=0))
-    pieces = [(first_part[:, plane_cols(q)], second_part[:, plane_cols(q)]) for q in range(3)]
     row = 0
-    for first, second in pieces + [tuple(ends)]:
-        rows = slice(row, row + first.shape[0])
-        keep_ref[rows, :] = jnp.where(first_core, first, second)
-        send_ref[rows, :] = jnp.where(first_core, second, first)
-        row += first.shape[0]
+    for low_half, high_half in pieces + [ends]:
+        rows = slice(row, row + low_half.shape[0])
+        keep_ref[rows, :] = jnp.where(first_core, low_half, high_half)
+        send_ref[rows, :] = jnp.where(first_core, high_half, low_half)
+        row += low_half.shape[0]
 
 
 def add_kernel(mine_ref, other_ref, out_ref):
@@ -593,21 +604,38 @@
         out_ref[s] = total
 
 
-def unpack_kernel(mine_ref, other_ref, logits_ref, first_ref, second_ref, head_ref, out_ref):
-    out_ref[:, 0, :] = logits_ref[0:3, :]
-    first_core = (lax.axis_index("dp") & 1) == 0
-    mine, other = mine_ref[...], other_ref[...]
-    for k, out in ((0, first_ref), (1, second_ref)):
-        half = jnp.where(first_core, other if k else mine, mine if k else other)
-        half = half.astype(jnp.float32)
-        tail = jnp.concatenate([half[432:504, 0:C], half[432:504, C : 2 * C]], axis=0)
-        tiles = [half[144 * q : 144 * (q + 1), :] for q in range(3)]
-        whole = jnp.concatenate(tiles + [tail], axis=1)
+def unpack_half(side, rows_ref, outs, whole_ref, sems):
+    rows = rows_ref[...].astype(jnp.float32)
+    copies = []
+    for m, out in enumerate(outs):
+        tiles = [rows[72 * (3 * m + q) : 72 * (3 * m + q + 1)] for q in range(3)]
+        whole = jnp.concatenate(tiles + [rows[432:504, C * m : C * (m + 1)]], axis=1)
         for a in range(3):
             for t in range(9):
-                out[9 * a + t] = whole[C * a : C * (a + 1), C * t : C * (t + 1)]
-        if k:
-            head_ref[...] = half[432 : 432 + C, 96:112].T[0:3]
+                whole_ref[m, 9 * a + t] = whole[24 * a : 24 * (a + 1), C * t : C * (t + 1)]
+        channels = pl.ds(pl.multiple_of(24 * side, 8), 24)
+        copy = pltpu.make_async_copy(whole_ref.at[m], out.at[:, channels, :], sems.at[m])
+        copy.start()
+        copies.append(copy)
+    for copy in copies:
+        copy.wait()
+
+
+def unpack_own_kernel(mine_ref, logits_ref, first_ref, second_ref, out_ref, whole_ref, sems):
+    out_ref[:, 0, :] = logits_ref[0:3, :]
+    core = lax.axis_index("dp") & 1
+    unpack_half(core, mine_ref, (first_ref, second_ref), whole_ref, sems)
+
+
+def unpack_other_kernel(
+    mine_ref, other_ref, _first, _second, first_ref, second_ref, head_ref, whole_ref, sems
+):
+    core = lax.axis_index("dp") & 1
+    mine, other = (ref[432:504, :].astype(jnp.float32)[0:24, 96:112] for ref in (mine_ref, other_ref))
+    low_half = jnp.where(core == 0, mine, other)
+    high_half = jnp.where(core == 0, other, mine)
+    head_ref[...] = jnp.concatenate([low_half, high_half], axis=0).T[0:3]
+    unpack_half(1 - core, other_ref, (first_ref, second_ref), whole_ref, sems)
 
 
 def on_device_flat(features, device_block, conv_first, conv_second, head_weight, targets):
@@ -742,19 +770,30 @@
     pieces = shape((peers, HALF // peers, LANES), bf16)
     total = exchange(step(sum_kernel, pieces, exchange(term.reshape(pieces.shape))))
     total = total.reshape(HALF, LANES)
-    grad_first, grad_second, grad_head, logits = pl.pallas_call(
-        unpack_kernel,
-        out_shape=(
-            shape((27, C, C), f32),
-            shape((27, C, C), f32),
-            shape((3, C), f32),
-            shape((3, 1, CELLS), f32),
-        ),
-        in_specs=[vmem] * 3,
-        out_specs=(vmem,) * 4,
+    other = swap_cores(total)
+    gradient = shape((27, C, C), f32)
+    anywhere = pl.BlockSpec(memory_space=pl.ANY)
+    scratch = [pltpu.VMEM((2, 27, 24, C), f32), pltpu.SemaphoreType.DMA((2,))]
+    grad_first, grad_second, logits = pl.pallas_call(
+        unpack_own_kernel,
+        out_shape=(gradient, gradient, shape((3, 1, CELLS), f32)),
+        in_specs=[vmem] * 2,
+        out_specs=(anywhere, anywhere, vmem),
+        scratch_shapes=scratch,
         compiler_params=small,
-        name="unpack_gradients",
-    )(total, swap_cores(total), logits)
+        cost_estimate=pl.CostEstimate(flops=1_000_000, bytes_accessed=2_000_000, transcendentals=0),
+        name="unpack_own",
+    )(total, logits)
+    grad_first, grad_second, grad_head = pl.pallas_call(
+        unpack_other_kernel,
+        out_shape=(gradient, gradient, shape((3, C), f32)),
+        in_specs=[vmem, vmem, anywhere, anywhere],
+        out_specs=(anywhere, anywhere, vmem),
+        input_output_aliases={2: 0, 3: 1},
+        scratch_shapes=scratch,
+        compiler_params=small,
+        name="unpack_other",
+    )(total, other, grad_first, grad_second)
     return (
         logits.transpose(1, 0, 2)[None],
         grad_first.transpose(1, 0, 2),

time: 47.8 us -> 48.4 us (1.013)
  Pallas kernels: 5.92 us -> 7.73 us
  waiting for transfers between devices: 7.46 us -> 6.12 us
    pallas_call x1 -> x2, Pallas kernels: 1.28 us -> 3.13 us  [the longest x1 1.57 us: on_device_flat(): pl.pallas_call(unpack_other_kernel, out_shape=(gradient, gradient, shape(...]
    ppermute x2, waiting for transfers between devices: 2.87 us -> 1.52 us  [swap_cores(): return lax.ppermute(values, 'dp', [(d, d ^ 1) for d in range(dp_count)])]
  transfers between devices with their start and end apart: 7 -> 7, of which waited for: 6 -> 5; matrix products, arithmetic and copies ran while one was open for 0% -> 0% of each run, Pallas kernels for 1% -> 5%
where the time goes in v5:
time: 48.4 us; the launch traced here: 48 us
  blocking collectives  22.8 us (47%)
  Pallas kernels  7.73 us (16%)
  starting transfers between devices  7.4 us (15%)
  waiting for transfers between devices  6.12 us (13%)
  local copies, waits for them, and re-layouts  3.19 us (7%)
  between operations  0.71 us (1%)
    all_to_all x2, blocking collectives, exchange(): lax.all_to_all(values, ('dp', 'space'), 0, 0, axis_index_groups=groups, t...  22.8 us
    ppermute x5, starting transfers between devices, swap(): lax.ppermute(values, 'space', [(s, s ^ mask) for s in range(space_count)])  7.33 us
    ppermute x5, waiting for transfers between devices, swap(): lax.ppermute(values, 'space', [(s, s ^ mask) for s in range(space_count)])  4.6 us
    pallas_call x1, Pallas kernels, on_device_flat(): pl.pallas_call(functools.partial(crop_kernel, scale), out_shape=(shape((8...  3.71 us
    unnamed x12, local copies, waits for them, and re-layouts  3.19 us
    pallas_call x1, Pallas kernels, on_device_flat(): pl.pallas_call(unpack_other_kernel, out_shape=(gradient, gradient, shape(...  1.57 us
    pallas_call x1, Pallas kernels, on_device_flat(): pl.pallas_call(unpack_own_kernel, out_shape=(gradient, gradient, shape((3...  1.56 us
    ppermute x2, waiting for transfers between devices, swap_cores(): return lax.ppermute(values, 'dp', [(d, d ^ 1) for d in range(dp_count)])  1.52 us
  transfers between devices with their start and end apart: 7, of which 5 were waited for; matrix products, arithmetic and copies ran while one was open for 0% of the time, Pallas kernels for 5%

profile of v5, /device:TPU:0, one launch (start us, length us, event | category | flops | bytes accessed | tf_op | source)
XLA Modules:
  0.0 48.0 jit_solution(4266570518734786879)
XLA Ops:
  0.6 3.0 %collective-permute-start = (bf16[1,1,48,512]{3,2,1,0:T(8,128)(2,1)}, bf16[1,1,48,512]{3,2,1,0:T(8,128)(2,1)S(1)}, u32[]{:S(2)}, u32[]{:S(2)}) collective-permute-start(bf16[1,1,48,512]{3,2,1,0:T(8,128)(2,1)} %param.6), channel_id=1, source_target_pairs={{0,1},{1,0},{2,3},{3,2},{4,5},{5,4},{6,7},{7,6},{8,9},{9,8},{10,11... | collective-permute-start | bytes 147464 | tf_op jit(solution)/shard_map/ppermute | solution.py:650
  3.6 0.0 copy-start.3
  3.6 0.1 collective-permute-start.1
  3.7 0.0 copy-start.4
  3.7 0.6 %copy-done.3 = s32[1,1,3,512]{3,1,2,0:T(1,128)S(1)} copy-done((s32[1,1,3,512]{3,1,2,0:T(1,128)S(1)}, s32[1,1,3,512]{3,1,2,0:T(1,128)}, u32[]{:S(2)}) %copy-start.3) | copy-done | bytes 6168
  4.3 0.1 copy-done.4
  4.4 0.0 copy-start.2
  4.4 0.8 %copy-done.2 = bf16[1,1,48,512]{3,2,1,0:T(8,128)(2,1)S(1)} copy-done((bf16[1,1,48,512]{3,2,1,0:T(8,128)(2,1)S(1)}, bf16[1,1,48,512]{3,2,1,0:T(8,128)(2,1)}, u32[]{:S(2)}) %copy-start.2) | copy-done | bytes 49176
  5.2 0.2 pack_own.1
  5.3 2.1 %collective-permute-done.1 = s32[1,1,3,512]{3,0,2,1:T(1,128)S(1)} collective-permute-done((s32[1,1,3,512]{3,0,2,1:T(1,128)}, s32[1,1,3,512]{3,0,2,1:T(1,128)S(1)}, u32[]{:S(2)}, u32[]{:S(2)}) %collective-permute-start.1) | collective-permute-done | bytes 6176 | tf_op jit(solution)/shard_map/ppermute | solution.py:650
  7.5 0.0 collective-permute-done
  7.5 0.2 pack_mate.1
  7.6 2.7 %collective-permute-start.2 = (bf16[2,8,16,128]{3,2,1,0:T(8,128)(2,1)S(1)}, bf16[2,8,16,128]{3,2,1,0:T(8,128)(2,1)S(1)}, u32[]{:S(2)}, u32[]{:S(2)}) collective-permute-start(bf16[2,8,16,128]{3,2,1,0:T(8,128)(2,1)S(1)} %get-tuple-element.31), channel_id=1, source_target_pairs={{0,4},{1,5},{2,6},{3,7},{4,0},{5,1},{6,2},{7,3},{8,12},{9,13},{10,... | collective-permute-start | bytes 196616 | tf_op jit(solution)/shard_map/ppermute | solution.py:650
  10.3 0.0 copy-start.5
  10.3 1.3 %collective-permute-start.3 = (bf16[2,8,16,128]{3,2,1,0:T(8,128)(2,1)S(1)}, bf16[2,8,16,128]{3,2,1,0:T(8,128)(2,1)S(1)}, u32[]{:S(2)}, u32[]{:S(2)}) collective-permute-start(bf16[2,8,16,128]{3,2,1,0:T(8,128)(2,1)S(1)} %get-tuple-element.32), channel_id=1, source_target_pairs={{0,6},{1,7},{2,4},{3,5},{4,2},{5,3},{6,0},{7,1},{8,14},{9,15},{10,... | collective-permute-start | bytes 196616 | tf_op jit(solution)/shard_map/ppermute | solution.py:650
  11.7 0.2 collective-permute-start.4
  11.9 0.0 copy-done.5
  11.9 0.1 lay_out_head.1
  12.0 0.0 copy-start
  12.0 1.0 %copy-done = bf16[48,27,48]{2,0,1:T(8,128)(2,1)S(1)} copy-done((bf16[48,27,48]{2,0,1:T(8,128)(2,1)S(1)}, bf16[48,27,48]{2,0,1:T(8,128)(2,1)}, u32[]{:S(2)}) %copy-start) | copy-done | bytes 124440
  12.9 0.0 copy-start.1
  12.9 0.2 prepare.1
  13.2 0.8 %copy-done.1 = bf16[48,27,48]{2,0,1:T(8,128)(2,1)S(1)} copy-done((bf16[48,27,48]{2,0,1:T(8,128)(2,1)S(1)}, bf16[48,27,48]{2,0,1:T(8,128)(2,1)}, u32[]{:S(2)}) %copy-start.1) | copy-done | bytes 124440
  13.9 0.2 second_weights.1
  14.2 0.6 %collective-permute-done.2.refs_0_ = bf16[2,8,16,128]{3,2,1,0:T(8,128)(2,1)S(1)} collective-permute-done((bf16[2,8,16,128]{3,2,1,0:T(8,128)(2,1)S(1)}, bf16[2,8,16,128]{3,2,1,0:T(8,128)(2,1)S(1)}, u32[]{:S(2)}, u32[]{:S(2)}) %collective-permute-start.2) | collective-permute-done | bytes 65568 | tf_op jit(solution)/shard_map/ppermute | solution.py:650
  14.8 1.7 %collective-permute-done.3.refs_1_ = bf16[2,8,16,128]{3,2,1,0:T(8,128)(2,1)S(1)} collective-permute-done((bf16[2,8,16,128]{3,2,1,0:T(8,128)(2,1)S(1)}, bf16[2,8,16,128]{3,2,1,0:T(8,128)(2,1)S(1)}, u32[]{:S(2)}, u32[]{:S(2)}) %collective-permute-start.3) | collective-permute-done | bytes 65568 | tf_op jit(solution)/shard_map/ppermute | solution.py:650
  16.5 0.1 collective-permute-done.4.refs_2_
  16.6 3.7 %forward_backward.1 = (f32[8,512]{1,0:T(8,128)S(1)}, f32[512,128]{1,0:T(8,128)S(1)}, f32[512,128]{1,0:T(8,128)S(1)}) custom-call(s32[1,128]{1,0:T(1,128)S(1)} %get-tuple-element.26.owners_ref, f32[8,128]{1,0:T(8,128)S(1)} %get-tuple-element.27.masks_ref, bf16[13,16,128]{2,1,0:T(8,128)(2,1)S(1)} %get-tuple-element.28.own_ref, ...), custom_call_target="tpu_custom_call" | custom-call | tf_op jit(solution)/shard_map/forward_backward/pallas_call | solution.py:720
  20.3 0.1 collective-permute-start.5
  20.4 1.5 %collective-permute-done.5.other_ref = f32[512,128]{1,0:T(8,128)S(1)} collective-permute-done((f32[512,128]{1,0:T(8,128)S(1)}, f32[512,128]{1,0:T(8,128)S(1)}, u32[]{:S(2)}, u32[]{:S(2)}) %collective-permute-start.5) | collective-permute-done | bytes 262176 | tf_op jit(solution)/shard_map/ppermute | solution.py:746
  22.0 12.2 %all_to_all.10.parts_ref = bf16[16,32,128]{2,1,0:T(8,128)(2,1)S(1)} all-to-all(bf16[16,32,128]{2,1,0:T(8,128)(2,1)S(1)} %bitcast.17), channel_id=1, replica_groups={{0,1,2,3,4,5,6,7,16,17,18,19,20,21,22,23},{8,9,10,11,12,13,14,15,24,25,..., dimensions={0} | all-to-all | bytes 262144 | tf_op jit(solution)/shard_map/all_to_all | solution.py:755
  34.2 10.6 %all_to_all.11 = bf16[16,32,128]{2,1,0:T(8,128)(2,1)S(1)} all-to-all(bf16[16,32,128]{2,1,0:T(8,128)(2,1)S(1)} %gradient_sum.3), channel_id=1, replica_groups={{0,1,2,3,4,5,6,7,16,17,18,19,20,21,22,23},{8,9,10,11,12,13,14,15,24,25,..., dimensions={0} | all-to-all | bytes 262144 | tf_op jit(solution)/shard_map/all_to_all | solution.py:755
  44.8 0.0 collective-permute-start.6
  44.8 1.6 %unpack_own.1 = (f32[27,48,48]{2,1,0:T(8,128)}, f32[27,48,48]{2,1,0:T(8,128)}, f32[3,1,512]{2,1,0:T(1,128)}) custom-call(bf16[512,128]{1,0:T(8,128)(2,1)S(1)} %bitcast.15, f32[8,512]{1,0:T(8,128)S(1)} %get-tuple-element.41.logits_ref), custom_call_target="tpu_custom_call" | custom-call | flops 1000000 | bytes 2000000 | tf_op jit(solution)/shard_map/unpack_own/pallas_call | solution.py:777
  46.4 0.0 collective-permute-done.6.other_ref
  46.4 1.6 %unpack_other.1 = (f32[27,48,48]{2,1,0:T(8,128)}, f32[27,48,48]{2,1,0:T(8,128)}, f32[3,48]{1,0:T(4,128)}) custom-call(bf16[512,128]{1,0:T(8,128)(2,1)S(1)} %bitcast.16, bf16[512,128]{1,0:T(8,128)(2,1)S(1)} %collective-permute-done.6.other_ref, f32[27,48,48]{2,1,0:T(8,128)} %get-tuple-element.43._first, ...), custom_call_target="tpu_custom_call", output_to_operand_aliasing={{0}: (2, {}), {1}: (3, {})} | custom-call | tf_op jit(solution)/shard_map/unpack_other/pallas_call | solution.py:787
  (3 shorter events, 0.1 us)
Async XLA Ops:
  0.6 6.8 %collective-permute-start = (bf16[1,1,48,512]{3,2,1,0:T(8,128)(2,1)}, bf16[1,1,48,512]{3,2,1,0:T(8,128)(2,1)S(1)}, u32[]{:S(2)}, u32[]{:S(2)}) collective-permute-start(bf16[1,1,48,512]{3,2,1,0:T(8,128)(2,1)} %param.6), channel_id=1, source_target_pairs={{0,1},{1,0},{2,3},{3,2},{4,5},{5,4},{6,7},{7,6},{8,9},{9,8},{10,11... | collective-permute-start | bytes 147464 | tf_op jit(solution)/shard_map/ppermute | solution.py:650
  3.6 0.7 %copy-start.3 = (s32[1,1,3,512]{3,1,2,0:T(1,128)S(1)}, s32[1,1,3,512]{3,1,2,0:T(1,128)}, u32[]{:S(2)}) copy-start(s32[1,1,3,512]{3,1,2,0:T(1,128)} %param.11) | copy-start | bytes 18436
  3.6 3.8 %collective-permute-start.1 = (s32[1,1,3,512]{3,0,2,1:T(1,128)}, s32[1,1,3,512]{3,0,2,1:T(1,128)S(1)}, u32[]{:S(2)}, u32[]{:S(2)}) collective-permute-start(s32[1,1,3,512]{3,0,2,1:T(1,128)} %bitcast.23), channel_id=1, source_target_pairs={{0,1},{1,0},{2,3},{3,2},{4,5},{5,4},{6,7},{7,6},{8,9},{9,8},{10,11... | collective-permute-start | bytes 18440 | tf_op jit(solution)/shard_map/ppermute | solution.py:650
  3.7 0.7 %copy-start.4 = (s32[1,8]{1,0:T(1,128)S(1)}, s32[1,8]{1,0:T(1,128)}, u32[]{:S(2)}) copy-start(s32[1,8]{1,0:T(1,128)} %block_ref.5) | copy-start | bytes 100
  4.4 0.8 %copy-start.2 = (bf16[1,1,48,512]{3,2,1,0:T(8,128)(2,1)S(1)}, bf16[1,1,48,512]{3,2,1,0:T(8,128)(2,1)}, u32[]{:S(2)}) copy-start(bf16[1,1,48,512]{3,2,1,0:T(8,128)(2,1)} %param.6) | copy-start | bytes 147460
  7.6 7.1 %collective-permute-start.2 = (bf16[2,8,16,128]{3,2,1,0:T(8,128)(2,1)S(1)}, bf16[2,8,16,128]{3,2,1,0:T(8,128)(2,1)S(1)}, u32[]{:S(2)}, u32[]{:S(2)}) collective-permute-start(bf16[2,8,16,128]{3,2,1,0:T(8,128)(2,1)S(1)} %get-tuple-element.31), channel_id=1, source_target_pairs={{0,4},{1,5},{2,6},{3,7},{4,0},{5,1},{6,2},{7,3},{8,12},{9,13},{10,... | collective-permute-start | bytes 196616 | tf_op jit(solution)/shard_map/ppermute | solution.py:650
  10.3 1.6 %copy-start.5 = (bf16[3,48]{1,0:T(4,128)(2,1)S(1)}, bf16[3,48]{1,0:T(4,128)(2,1)}, u32[]{:S(2)}) copy-start(bf16[3,48]{1,0:T(4,128)(2,1)} %head_ref.1) | copy-start | bytes 868
  10.3 6.2 %collective-permute-start.3 = (bf16[2,8,16,128]{3,2,1,0:T(8,128)(2,1)S(1)}, bf16[2,8,16,128]{3,2,1,0:T(8,128)(2,1)S(1)}, u32[]{:S(2)}, u32[]{:S(2)}) collective-permute-start(bf16[2,8,16,128]{3,2,1,0:T(8,128)(2,1)S(1)} %get-tuple-element.32), channel_id=1, source_target_pairs={{0,6},{1,7},{2,4},{3,5},{4,2},{5,3},{6,0},{7,1},{8,14},{9,15},{10,... | collective-permute-start | bytes 196616 | tf_op jit(solution)/shard_map/ppermute | solution.py:650
  11.7 5.0 %collective-permute-start.4 = (bf16[2,8,16,128]{3,2,1,0:T(8,128)(2,1)S(1)}, bf16[2,8,16,128]{3,2,1,0:T(8,128)(2,1)S(1)}, u32[]{:S(2)}, u32[]{:S(2)}) collective-permute-start(bf16[2,8,16,128]{3,2,1,0:T(8,128)(2,1)S(1)} %get-tuple-element.33), channel_id=1, source_target_pairs={{0,2},{1,3},{2,0},{3,1},{4,6},{5,7},{6,4},{7,5},{8,10},{9,11},{10,... | collective-permute-start | bytes 196616 | tf_op jit(solution)/shard_map/ppermute | solution.py:650
  12.0 1.0 %copy-start = (bf16[48,27,48]{2,0,1:T(8,128)(2,1)S(1)}, bf16[48,27,48]{2,0,1:T(8,128)(2,1)}, u32[]{:S(2)}) copy-start(bf16[48,27,48]{2,0,1:T(8,128)(2,1)} %param.8) | copy-start | bytes 373252
  12.9 1.0 %copy-start.1 = (bf16[48,27,48]{2,0,1:T(8,128)(2,1)S(1)}, bf16[48,27,48]{2,0,1:T(8,128)(2,1)}, u32[]{:S(2)}) copy-start(bf16[48,27,48]{2,0,1:T(8,128)(2,1)} %param.9) | copy-start | bytes 373252
  20.3 1.6 %collective-permute-start.5 = (f32[512,128]{1,0:T(8,128)S(1)}, f32[512,128]{1,0:T(8,128)S(1)}, u32[]{:S(2)}, u32[]{:S(2)}) collective-permute-start(f32[512,128]{1,0:T(8,128)S(1)} %get-tuple-element.40), channel_id=1, source_target_pairs={{0,8},{8,0},{16,24},{24,16},{1,9},{9,1},{17,25},{25,17},{2,10},{10... | collective-permute-start | bytes 786440 | tf_op jit(solution)/shard_map/ppermute | solution.py:746
  44.8 1.6 %collective-permute-start.6 = (bf16[512,128]{1,0:T(8,128)(2,1)S(1)}, bf16[512,128]{1,0:T(8,128)(2,1)S(1)}, u32[]{:S(2)}, u32[]{:S(2)}) collective-permute-start(bf16[512,128]{1,0:T(8,128)(2,1)S(1)} %bitcast.14), channel_id=1, source_target_pairs={{0,8},{8,0},{16,24},{24,16},{1,9},{9,1},{17,25},{25,17},{2,10},{10... | collective-permute-start | bytes 393224 | tf_op jit(solution)/shard_map/ppermute | solution.py:746

commit v6 on v4

--- a/solution.py
+++ b/solution.py
@@ -254,9 +254,8 @@
     out_ref[...] = lanes(16)
 
 
-def pack_own_kernel(
-    block_ref, features_ref, targets_ref, lane_ref, own_ref, slabs_ref, cases_ref
-):
+def pack_own_kernel(block_ref, features_ref, targets_ref, lane_ref, own_ref, *refs):
+    *slab_refs, cases_ref = refs
     blocks = listed_blocks(block_ref, lax.axis_index("space"))
     tiles, rows = block_tiles(features_ref, targets_ref)
     for ct in range(3):
@@ -264,18 +263,17 @@
             own_ref[4 * ct + q] = tiles[ct][q]
     own_ref[12] = jnp.concatenate(rows, axis=0).astype(jnp.bfloat16)
     write_cases(tiles, rows, cases_ref, lane_ref[...])
-    for n, k in enumerate(PARTNERS):
-        slabs_ref[n] = cases_ref[case_of(blocks[0], blocks[k])]
-
-
-def pack_mate_kernel(block_ref, features_ref, targets_ref, slabs_ref, mate_ref, *refs):
-    *pair_refs, cases_ref = refs
+    for k, ref in zip(PARTNERS, slab_refs):
+        ref[...] = cases_ref[case_of(blocks[0], blocks[k])]
+
+
+def pack_mate_kernel(block_ref, features_ref, targets_ref, mate_ref, *refs):
+    *slab_refs, cases_ref = refs
     blocks = listed_blocks(block_ref, lax.axis_index("space"))
     write_cases(*block_tiles(features_ref, targets_ref), cases_ref, lanes(16))
     mate_ref[...] = cases_ref[case_of(blocks[1], blocks[0])]
-    for n, (k, ref) in enumerate(zip(PARTNERS, pair_refs)):
-        ref[0] = slabs_ref[n]
-        ref[1] = cases_ref[case_of(blocks[1], blocks[k])]
+    for k, ref in zip(PARTNERS, slab_refs):
+        ref[...] = cases_ref[case_of(blocks[1], blocks[k])]
 
 
 def stacked_taps(ref):
@@ -333,7 +331,7 @@
 
 
 def crop_kernel(scale, owners_ref, masks_ref, own_ref, mate_ref, *refs):
-    crop_body(scale, owners_ref, masks_ref, own_ref, mate_ref, refs[:3], *refs[3:])
+    crop_body(scale, owners_ref, masks_ref, own_ref, mate_ref, refs[:6], *refs[6:])
 
 
 def crop_body(
@@ -342,7 +340,7 @@
     masks_ref,
     own_ref,
     mate_ref,
-    pairs,
+    slabs,
     w1_ref,
     w2_ref,
     w2t_ref,
@@ -365,9 +363,9 @@
     back_ref,
 ):
     gathered_ref[1] = mate_ref[...]
-    for k, pair in zip(PARTNERS, pairs):
+    for n, k in enumerate(PARTNERS):
         for j in range(2):
-            gathered_ref[k + j] = pair[j]
+            gathered_ref[k + j] = slabs[3 * j + n][...]
     owners = owners_ref[...]
     owner = [owners[0, q] for q in range(9)]
 
@@ -466,8 +464,8 @@
         pre = summed(plane, 1)
         negative = jnp.exp(jnp.minimum(pre, 0.0))
         if 4 <= plane < 12:
-            slope1_ref[:, plane_cols(plane - 4)] = jnp.where(pre > 0, 1.0, negative)
-        hidden = jnp.where(pre > 0, pre, negative - 1.0) * masks[bx]
+            slope1_ref[:, plane_cols(plane - 4)] = negative
+        hidden = (jnp.maximum(pre, 0.0) + (negative - 1.0)) * masks[bx]
         hidden = hidden.astype(bf16)
         for c in (-1, 0, 1):
             if c == 0:
@@ -488,8 +486,8 @@
         bx = (plane + 6) // 8
         pre = summed(plane, 2)
         negative = jnp.exp(jnp.minimum(pre, 0.0))
-        slope2_ref[:, plane_cols(plane)] = jnp.where(pre > 0, 1.0, negative) * masks[bx]
-        hidden = jnp.where(pre > 0, pre, negative - 1.0) * masks[bx]
+        slope2_ref[:, plane_cols(plane)] = negative * masks[bx]
+        hidden = (jnp.maximum(pre, 0.0) + (negative - 1.0)) * masks[bx]
         hid2_ref[:, plane_cols(plane)] = hidden.astype(jnp.bfloat16)
 
     logits = matmul(h_ref[...], hid2_ref[...])
@@ -639,30 +637,28 @@
         cost_estimate=pl.CostEstimate(flops=0, bytes_accessed=2_000_000, transcendentals=0),
         name="lane_indices",
     )()
-    own, own_slabs = pl.pallas_call(
+    slab = shape((8, 16, LANES), bf16)
+    own, *own_slabs = pl.pallas_call(
         pack_own_kernel,
-        out_shape=(shape((13, 16, LANES), bf16), shape((3, 8, 16, LANES), bf16)),
+        out_shape=(shape((13, 16, LANES), bf16), slab, slab, slab),
         in_specs=[vmem] * 4,
-        out_specs=(vmem,) * 2,
+        out_specs=(vmem,) * 4,
         scratch_shapes=[pltpu.VMEM((4, 8, 16, LANES), bf16)],
         compiler_params=small,
         cost_estimate=pl.CostEstimate(flops=1_000_000, bytes_accessed=2_000_000, transcendentals=0),
         name="pack_own",
     )(device_block, features[0, 0], targets[0].transpose(1, 0, 2), lane)
-    mate_slab, *pairs = pl.pallas_call(
+    slabs = [swap(own_slab, mask) for own_slab, mask in zip(own_slabs, PARTNERS)]
+    mate_slab, *mate_slabs = pl.pallas_call(
         pack_mate_kernel,
-        out_shape=(
-            shape((8, 16, LANES), bf16),
-            *[shape((2, 8, 16, LANES), bf16) for _ in PARTNERS],
-        ),
-        in_specs=[vmem] * 4,
+        out_shape=(slab,) * 4,
+        in_specs=[vmem] * 3,
         out_specs=(vmem,) * 4,
         scratch_shapes=[pltpu.VMEM((4, 8, 16, LANES), bf16)],
         compiler_params=small,
-        cost_estimate=pl.CostEstimate(flops=1_000_000, bytes_accessed=2_000_000, transcendentals=0),
         name="pack_mate",
-    )(device_block, mate_features[0, 0], mate_targets[0].transpose(1, 0, 2), own_slabs)
-    pairs = [swap(pair, mask) for pair, mask in zip(pairs, PARTNERS)]
+    )(device_block, mate_features[0, 0], mate_targets[0].transpose(1, 0, 2))
+    slabs += [swap(mate_part, mask) for mate_part, mask in zip(mate_slabs, PARTNERS)]
 
     w1, owners, masks = pl.pallas_call(
         prepare_kernel,
@@ -692,7 +688,7 @@
     logits, keep, send = pl.pallas_call(
         functools.partial(crop_kernel, scale),
         out_shape=(shape((8, CELLS), f32), shape((HALF, LANES), f32), shape((HALF, LANES), f32)),
-        in_specs=[vmem] * 12,
+        in_specs=[vmem] * 15,
         out_specs=(vmem,) * 3,
         scratch_shapes=[
             pltpu.VMEM((space_count, 8, 16, LANES), bf16),
@@ -710,7 +706,7 @@
         ],
         compiler_params=pltpu.CompilerParams(vmem_limit_bytes=20 * 1024 * 1024),
         name="forward_backward",
-    )(owners, masks, own, mate_slab, *pairs, w1, w2, w2t, head, head_t)
+    )(owners, masks, own, mate_slab, *slabs, w1, w2, w2t, head, head_t)
 
     dp_count = lax.axis_size("dp")
 

time: 47.8 us -> 50.7 us (1.061)
  starting transfers between devices: 7.4 us -> 11.9 us
  waiting for transfers between devices: 7.46 us -> 6 us
    ppermute x5 -> x8, starting transfers between devices: 7.33 us -> 11.8 us  [swap(): lax.ppermute(values, 'space', [(s, s ^ mask) for s in range(space_count)])]
    ppermute x5 -> x8, waiting for transfers between devices: 4.6 us -> 3.13 us  [swap(): lax.ppermute(values, 'space', [(s, s ^ mask) for s in range(space_count)])]
  transfers between devices with their start and end apart: 7 -> 10, of which waited for: 6 -> 5; matrix products, arithmetic and copies ran while one was open for 0% -> 0% of each run, Pallas kernels for 1% -> 2%
where the time goes in v6:
time: 50.7 us; the launch traced here: 50.4 us
  blocking collectives  22.7 us (45%)
  starting transfers between devices  11.9 us (23%)
  waiting for transfers between devices  6 us (12%)
  Pallas kernels  5.93 us (12%)
  local copies, waits for them, and re-layouts  3.19 us (6%)
  between operations  0.74 us (1%)
    all_to_all x2, blocking collectives, exchange(): lax.all_to_all(values, ('dp', 'space'), 0, 0, axis_index_groups=groups, t...  22.7 us
    ppermute x8, starting transfers between devices, swap(): lax.ppermute(values, 'space', [(s, s ^ mask) for s in range(space_count)])  11.8 us
    pallas_call x1, Pallas kernels, on_device_flat(): pl.pallas_call(functools.partial(crop_kernel, scale), out_shape=(shape((8...  3.76 us
    unnamed x12, local copies, waits for them, and re-layouts  3.19 us
    ppermute x8, waiting for transfers between devices, swap(): lax.ppermute(values, 'space', [(s, s ^ mask) for s in range(space_count)])  3.13 us
    ppermute x2, waiting for transfers between devices, swap_cores(): return lax.ppermute(values, 'dp', [(d, d ^ 1) for d in range(dp_count)])  2.87 us
    pallas_call x1, Pallas kernels, on_device_flat(): pl.pallas_call(unpack_kernel, out_shape=(shape((27, C, C), f32), shape((2...  1.28 us
  transfers between devices with their start and end apart: 10, of which 5 were waited for; matrix products, arithmetic and copies ran while one was open for 0% of the time, Pallas kernels for 2%

profile of v6, /device:TPU:0, one launch (start us, length us, event | category | flops | bytes accessed | tf_op | source)
XLA Modules:
  0.0 50.4 jit_solution(3379984705263308839)
XLA Ops:
  0.6 0.0 copy-start.3
  0.6 3.0 %collective-permute-start = (bf16[1,1,48,512]{3,2,1,0:T(8,128)(2,1)}, bf16[1,1,48,512]{3,2,1,0:T(8,128)(2,1)S(1)}, u32[]{:S(2)}, u32[]{:S(2)}) collective-permute-start(bf16[1,1,48,512]{3,2,1,0:T(8,128)(2,1)} %param.6), channel_id=1, source_target_pairs={{0,1},{1,0},{2,3},{3,2},{4,5},{5,4},{6,7},{7,6},{8,9},{9,8},{10,11... | collective-permute-start | bytes 147464 | tf_op jit(solution)/shard_map/ppermute | solution.py:620
  3.6 0.0 copy-start.4
  3.6 0.0 copy-done.3
  3.7 0.7 %copy-done.4 = s32[1,8]{1,0:T(1,128)S(1)} copy-done((s32[1,8]{1,0:T(1,128)S(1)}, s32[1,8]{1,0:T(1,128)}, u32[]{:S(2)}) %copy-start.4) | copy-done | bytes 56
  4.3 0.0 copy-start.2
  4.3 0.8 %copy-done.2 = bf16[1,1,48,512]{3,2,1,0:T(8,128)(2,1)S(1)} copy-done((bf16[1,1,48,512]{3,2,1,0:T(8,128)(2,1)S(1)}, bf16[1,1,48,512]{3,2,1,0:T(8,128)(2,1)}, u32[]{:S(2)}) %copy-start.2) | copy-done | bytes 49176
  5.1 0.2 pack_own.1
  5.3 2.7 %collective-permute-start.2 = (bf16[8,16,128]{2,1,0:T(8,128)(2,1)S(1)}, bf16[8,16,128]{2,1,0:T(8,128)(2,1)S(1)}, u32[]{:S(2)}, u32[]{:S(2)}) collective-permute-start(bf16[8,16,128]{2,1,0:T(8,128)(2,1)S(1)} %get-tuple-element.30), channel_id=1, source_target_pairs={{0,4},{1,5},{2,6},{3,7},{4,0},{5,1},{6,2},{7,3},{8,12},{9,13},{10,... | collective-permute-start | bytes 98312 | tf_op jit(solution)/shard_map/ppermute | solution.py:620
  7.9 0.5 %collective-permute-start.1 = (s32[1,1,3,512]{3,0,2,1:T(1,128)S(1)}, s32[1,1,3,512]{3,0,2,1:T(1,128)S(1)}, u32[]{:S(2)}, u32[]{:S(2)}) collective-permute-start(s32[1,1,3,512]{3,0,2,1:T(1,128)S(1)} %bitcast.23), channel_id=1, source_target_pairs={{0,1},{1,0},{2,3},{3,2},{4,5},{5,4},{6,7},{7,6},{8,9},{9,8},{10,11... | collective-permute-start | bytes 18440 | tf_op jit(solution)/shard_map/ppermute | solution.py:620
  8.5 1.3 %collective-permute-start.3 = (bf16[8,16,128]{2,1,0:T(8,128)(2,1)S(1)}, bf16[8,16,128]{2,1,0:T(8,128)(2,1)S(1)}, u32[]{:S(2)}, u32[]{:S(2)}) collective-permute-start(bf16[8,16,128]{2,1,0:T(8,128)(2,1)S(1)} %get-tuple-element.31), channel_id=1, source_target_pairs={{0,6},{1,7},{2,4},{3,5},{4,2},{5,3},{6,0},{7,1},{8,14},{9,15},{10,... | collective-permute-start | bytes 98312 | tf_op jit(solution)/shard_map/ppermute | solution.py:620
  9.8 0.2 collective-permute-start.4
  10.0 1.5 %collective-permute-done.1 = s32[1,1,3,512]{3,0,2,1:T(1,128)S(1)} collective-permute-done((s32[1,1,3,512]{3,0,2,1:T(1,128)S(1)}, s32[1,1,3,512]{3,0,2,1:T(1,128)S(1)}, u32[]{:S(2)}, u32[]{:S(2)}) %collective-permute-start.1) | collective-permute-done | bytes 6176 | tf_op jit(solution)/shard_map/ppermute | solution.py:620
  11.5 0.0 collective-permute-done
  11.6 0.2 pack_mate.1
  11.7 1.4 %collective-permute-start.5 = (bf16[8,16,128]{2,1,0:T(8,128)(2,1)S(1)}, bf16[8,16,128]{2,1,0:T(8,128)(2,1)S(1)}, u32[]{:S(2)}, u32[]{:S(2)}) collective-permute-start(bf16[8,16,128]{2,1,0:T(8,128)(2,1)S(1)} %get-tuple-element.33), channel_id=1, source_target_pairs={{0,4},{1,5},{2,6},{3,7},{4,0},{5,1},{6,2},{7,3},{8,12},{9,13},{10,... | collective-permute-start | bytes 98312 | tf_op jit(solution)/shard_map/ppermute | solution.py:620
  13.1 0.0 copy-start.5
  13.1 2.6 %collective-permute-start.6 = (bf16[8,16,128]{2,1,0:T(8,128)(2,1)S(1)}, bf16[8,16,128]{2,1,0:T(8,128)(2,1)S(1)}, u32[]{:S(2)}, u32[]{:S(2)}) collective-permute-start(bf16[8,16,128]{2,1,0:T(8,128)(2,1)S(1)} %get-tuple-element.34), channel_id=1, source_target_pairs={{0,6},{1,7},{2,4},{3,5},{4,2},{5,3},{6,0},{7,1},{8,14},{9,15},{10,... | collective-permute-start | bytes 98312 | tf_op jit(solution)/shard_map/ppermute | solution.py:620
  15.7 0.0 collective-permute-done.2.refs_0_
  15.7 0.0 collective-permute-start.7
  15.7 0.0 copy-done.5
  15.7 0.1 lay_out_head.1
  15.8 0.0 copy-start
  15.8 1.0 %copy-done = bf16[48,27,48]{2,0,1:T(8,128)(2,1)S(1)} copy-done((bf16[48,27,48]{2,0,1:T(8,128)(2,1)S(1)}, bf16[48,27,48]{2,0,1:T(8,128)(2,1)}, u32[]{:S(2)}) %copy-start) | copy-done | bytes 124440
  16.8 0.0 copy-start.1
  16.8 0.2 prepare.1
  17.0 0.8 %copy-done.1 = bf16[48,27,48]{2,0,1:T(8,128)(2,1)S(1)} copy-done((bf16[48,27,48]{2,0,1:T(8,128)(2,1)S(1)}, bf16[48,27,48]{2,0,1:T(8,128)(2,1)}, u32[]{:S(2)}) %copy-start.1) | copy-done | bytes 124440
  17.8 0.2 second_weights.1
  18.0 0.0 collective-permute-done.3.refs_1_
  18.0 0.0 collective-permute-done.4.refs_2_
  18.0 0.0 collective-permute-done.5.refs_3_
  18.0 0.8 %collective-permute-done.6.refs_4_ = bf16[8,16,128]{2,1,0:T(8,128)(2,1)S(1)} collective-permute-done((bf16[8,16,128]{2,1,0:T(8,128)(2,1)S(1)}, bf16[8,16,128]{2,1,0:T(8,128)(2,1)S(1)}, u32[]{:S(2)}, u32[]{:S(2)}) %collective-permute-start.6) | collective-permute-done | bytes 32800 | tf_op jit(solution)/shard_map/ppermute | solution.py:620
  18.8 0.8 %collective-permute-done.7.refs_5_ = bf16[8,16,128]{2,1,0:T(8,128)(2,1)S(1)} collective-permute-done((bf16[8,16,128]{2,1,0:T(8,128)(2,1)S(1)}, bf16[8,16,128]{2,1,0:T(8,128)(2,1)S(1)}, u32[]{:S(2)}, u32[]{:S(2)}) %collective-permute-start.7) | collective-permute-done | bytes 32800 | tf_op jit(solution)/shard_map/ppermute | solution.py:620
  19.6 3.8 %forward_backward.1 = (f32[8,512]{1,0:T(8,128)S(1)}, f32[512,128]{1,0:T(8,128)S(1)}, f32[512,128]{1,0:T(8,128)S(1)}) custom-call(s32[1,128]{1,0:T(1,128)S(1)} %get-tuple-element.26.owners_ref, f32[8,128]{1,0:T(8,128)S(1)} %get-tuple-element.27.masks_ref, bf16[13,16,128]{2,1,0:T(8,128)(2,1)S(1)} %get-tuple-element.28.own_ref, ...), custom_call_target="tpu_custom_call" | custom-call | tf_op jit(solution)/shard_map/forward_backward/pallas_call | solution.py:688
  23.4 0.1 collective-permute-start.8
  23.5 1.5 %collective-permute-done.8.other_ref = f32[512,128]{1,0:T(8,128)S(1)} collective-permute-done((f32[512,128]{1,0:T(8,128)S(1)}, f32[512,128]{1,0:T(8,128)S(1)}, u32[]{:S(2)}, u32[]{:S(2)}) %collective-permute-start.8) | collective-permute-done | bytes 262176 | tf_op jit(solution)/shard_map/ppermute | solution.py:714
  25.0 12.1 %all_to_all.10.parts_ref = bf16[16,32,128]{2,1,0:T(8,128)(2,1)S(1)} all-to-all(bf16[16,32,128]{2,1,0:T(8,128)(2,1)S(1)} %bitcast.14), channel_id=1, replica_groups={{0,1,2,3,4,5,6,7,16,17,18,19,20,21,22,23},{8,9,10,11,12,13,14,15,24,25,..., dimensions={0} | all-to-all | bytes 262144 | tf_op jit(solution)/shard_map/all_to_all | solution.py:723
  37.1 10.6 %all_to_all.11 = bf16[16,32,128]{2,1,0:T(8,128)(2,1)S(1)} all-to-all(bf16[16,32,128]{2,1,0:T(8,128)(2,1)S(1)} %gradient_sum.3), channel_id=1, replica_groups={{0,1,2,3,4,5,6,7,16,17,18,19,20,21,22,23},{8,9,10,11,12,13,14,15,24,25,..., dimensions={0} | all-to-all | bytes 262144 | tf_op jit(solution)/shard_map/all_to_all | solution.py:723
  47.8 0.0 collective-permute-start.9
  47.8 1.3 %collective-permute-done.9.other_ref = bf16[512,128]{1,0:T(8,128)(2,1)S(1)} collective-permute-done((bf16[512,128]{1,0:T(8,128)(2,1)S(1)}, bf16[512,128]{1,0:T(8,128)(2,1)S(1)}, u32[]{:S(2)}, u32[]{:S(2)}) %collective-permute-start.9) | collective-permute-done | bytes 131104 | tf_op jit(solution)/shard_map/ppermute | solution.py:714
  49.1 1.3 %unpack_gradients.1 = (f32[27,48,48]{2,1,0:T(8,128)}, f32[27,48,48]{2,1,0:T(8,128)}, f32[3,48]{1,0:T(4,128)}, f32[3,1,512]{2,1,0:T(1,128)}) custom-call(bf16[512,128]{1,0:T(8,128)(2,1)S(1)} %bitcast.16, bf16[512,128]{1,0:T(8,128)(2,1)S(1)} %collective-permute-done.9.other_ref, f32[8,512]{1,0:T(8,128)S(1)} %get-tuple-element.43.logits_ref), custom_call_target="tpu_custom_call" | custom-call | tf_op jit(solution)/shard_map/unpack_gradients/pallas_call | solution.py:741
  (3 shorter events, 0.1 us)
Async XLA Ops:
  0.6 3.0 %copy-start.3 = (s32[1,1,3,512]{3,1,2,0:T(1,128)S(1)}, s32[1,1,3,512]{3,1,2,0:T(1,128)}, u32[]{:S(2)}) copy-start(s32[1,1,3,512]{3,1,2,0:T(1,128)} %param.11) | copy-start | bytes 18436
  0.6 10.9 %collective-permute-start = (bf16[1,1,48,512]{3,2,1,0:T(8,128)(2,1)}, bf16[1,1,48,512]{3,2,1,0:T(8,128)(2,1)S(1)}, u32[]{:S(2)}, u32[]{:S(2)}) collective-permute-start(bf16[1,1,48,512]{3,2,1,0:T(8,128)(2,1)} %param.6), channel_id=1, source_target_pairs={{0,1},{1,0},{2,3},{3,2},{4,5},{5,4},{6,7},{7,6},{8,9},{9,8},{10,11... | collective-permute-start | bytes 147464 | tf_op jit(solution)/shard_map/ppermute | solution.py:620
  3.6 0.7 %copy-start.4 = (s32[1,8]{1,0:T(1,128)S(1)}, s32[1,8]{1,0:T(1,128)}, u32[]{:S(2)}) copy-start(s32[1,8]{1,0:T(1,128)} %block_ref.5) | copy-start | bytes 100
  4.3 0.8 %copy-start.2 = (bf16[1,1,48,512]{3,2,1,0:T(8,128)(2,1)S(1)}, bf16[1,1,48,512]{3,2,1,0:T(8,128)(2,1)}, u32[]{:S(2)}) copy-start(bf16[1,1,48,512]{3,2,1,0:T(8,128)(2,1)} %param.6) | copy-start | bytes 147460
  5.3 10.5 %collective-permute-start.2 = (bf16[8,16,128]{2,1,0:T(8,128)(2,1)S(1)}, bf16[8,16,128]{2,1,0:T(8,128)(2,1)S(1)}, u32[]{:S(2)}, u32[]{:S(2)}) collective-permute-start(bf16[8,16,128]{2,1,0:T(8,128)(2,1)S(1)} %get-tuple-element.30), channel_id=1, source_target_pairs={{0,4},{1,5},{2,6},{3,7},{4,0},{5,1},{6,2},{7,3},{8,12},{9,13},{10,... | collective-permute-start | bytes 98312 | tf_op jit(solution)/shard_map/ppermute | solution.py:620
  7.9 3.6 %collective-permute-start.1 = (s32[1,1,3,512]{3,0,2,1:T(1,128)S(1)}, s32[1,1,3,512]{3,0,2,1:T(1,128)S(1)}, u32[]{:S(2)}, u32[]{:S(2)}) collective-permute-start(s32[1,1,3,512]{3,0,2,1:T(1,128)S(1)} %bitcast.23), channel_id=1, source_target_pairs={{0,1},{1,0},{2,3},{3,2},{4,5},{5,4},{6,7},{7,6},{8,9},{9,8},{10,11... | collective-permute-start | bytes 18440 | tf_op jit(solution)/shard_map/ppermute | solution.py:620
  8.5 9.6 %collective-permute-start.3 = (bf16[8,16,128]{2,1,0:T(8,128)(2,1)S(1)}, bf16[8,16,128]{2,1,0:T(8,128)(2,1)S(1)}, u32[]{:S(2)}, u32[]{:S(2)}) collective-permute-start(bf16[8,16,128]{2,1,0:T(8,128)(2,1)S(1)} %get-tuple-element.31), channel_id=1, source_target_pairs={{0,6},{1,7},{2,4},{3,5},{4,2},{5,3},{6,0},{7,1},{8,14},{9,15},{10,... | collective-permute-start | bytes 98312 | tf_op jit(solution)/shard_map/ppermute | solution.py:620
  9.8 8.2 %collective-permute-start.4 = (bf16[8,16,128]{2,1,0:T(8,128)(2,1)S(1)}, bf16[8,16,128]{2,1,0:T(8,128)(2,1)S(1)}, u32[]{:S(2)}, u32[]{:S(2)}) collective-permute-start(bf16[8,16,128]{2,1,0:T(8,128)(2,1)S(1)} %get-tuple-element.32), channel_id=1, source_target_pairs={{0,2},{1,3},{2,0},{3,1},{4,6},{5,7},{6,4},{7,5},{8,10},{9,11},{10,... | collective-permute-start | bytes 98312 | tf_op jit(solution)/shard_map/ppermute | solution.py:620
  11.7 6.3 %collective-permute-start.5 = (bf16[8,16,128]{2,1,0:T(8,128)(2,1)S(1)}, bf16[8,16,128]{2,1,0:T(8,128)(2,1)S(1)}, u32[]{:S(2)}, u32[]{:S(2)}) collective-permute-start(bf16[8,16,128]{2,1,0:T(8,128)(2,1)S(1)} %get-tuple-element.33), channel_id=1, source_target_pairs={{0,4},{1,5},{2,6},{3,7},{4,0},{5,1},{6,2},{7,3},{8,12},{9,13},{10,... | collective-permute-start | bytes 98312 | tf_op jit(solution)/shard_map/ppermute | solution.py:620
  13.1 2.7 %copy-start.5 = (bf16[3,48]{1,0:T(4,128)(2,1)S(1)}, bf16[3,48]{1,0:T(4,128)(2,1)}, u32[]{:S(2)}) copy-start(bf16[3,48]{1,0:T(4,128)(2,1)} %head_ref.1) | copy-start | bytes 868
  13.1 5.7 %collective-permute-start.6 = (bf16[8,16,128]{2,1,0:T(8,128)(2,1)S(1)}, bf16[8,16,128]{2,1,0:T(8,128)(2,1)S(1)}, u32[]{:S(2)}, u32[]{:S(2)}) collective-permute-start(bf16[8,16,128]{2,1,0:T(8,128)(2,1)S(1)} %get-tuple-element.34), channel_id=1, source_target_pairs={{0,6},{1,7},{2,4},{3,5},{4,2},{5,3},{6,0},{7,1},{8,14},{9,15},{10,... | collective-permute-start | bytes 98312 | tf_op jit(solution)/shard_map/ppermute | solution.py:620
  15.7 3.9 %collective-permute-start.7 = (bf16[8,16,128]{2,1,0:T(8,128)(2,1)S(1)}, bf16[8,16,128]{2,1,0:T(8,128)(2,1)S(1)}, u32[]{:S(2)}, u32[]{:S(2)}) collective-permute-start(bf16[8,16,128]{2,1,0:T(8,128)(2,1)S(1)} %get-tuple-element.35), channel_id=1, source_target_pairs={{0,2},{1,3},{2,0},{3,1},{4,6},{5,7},{6,4},{7,5},{8,10},{9,11},{10,... | collective-permute-start | bytes 98312 | tf_op jit(solution)/shard_map/ppermute | solution.py:620
  15.8 1.0 %copy-start = (bf16[48,27,48]{2,0,1:T(8,128)(2,1)S(1)}, bf16[48,27,48]{2,0,1:T(8,128)(2,1)}, u32[]{:S(2)}) copy-start(bf16[48,27,48]{2,0,1:T(8,128)(2,1)} %param.8) | copy-start | bytes 373252
  16.8 1.0 %copy-start.1 = (bf16[48,27,48]{2,0,1:T(8,128)(2,1)S(1)}, bf16[48,27,48]{2,0,1:T(8,128)(2,1)}, u32[]{:S(2)}) copy-start(bf16[48,27,48]{2,0,1:T(8,128)(2,1)} %param.9) | copy-start | bytes 373252
  23.4 1.6 %collective-permute-start.8 = (f32[512,128]{1,0:T(8,128)S(1)}, f32[512,128]{1,0:T(8,128)S(1)}, u32[]{:S(2)}, u32[]{:S(2)}) collective-permute-start(f32[512,128]{1,0:T(8,128)S(1)} %get-tuple-element.42), channel_id=1, source_target_pairs={{0,8},{8,0},{16,24},{24,16},{1,9},{9,1},{17,25},{25,17},{2,10},{10... | collective-permute-start | bytes 786440 | tf_op jit(solution)/shard_map/ppermute | solution.py:714
  47.8 1.3 %collective-permute-start.9 = (bf16[512,128]{1,0:T(8,128)(2,1)S(1)}, bf16[512,128]{1,0:T(8,128)(2,1)S(1)}, u32[]{:S(2)}, u32[]{:S(2)}) collective-permute-start(bf16[512,128]{1,0:T(8,128)(2,1)S(1)} %bitcast.15), channel_id=1, source_target_pairs={{0,8},{8,0},{16,24},{24,16},{1,9},{9,1},{17,25},{25,17},{2,10},{10... | collective-permute-start | bytes 393224 | tf_op jit(solution)/shard_map/ppermute | solution.py:714

commit v7 on v4

--- a/solution.py
+++ b/solution.py
@@ -457,8 +457,8 @@
             + product_ref[2 * C : 3 * C, plane_cols(plane + 2 * stride)]
         )
 
-    for n in range(9):
-        cols = slice(256 * n, 256 * (n + 1))
+    for n in range(3):
+        cols = slice(768 * n, 768 * (n + 1))
         product_ref[:, cols] = matmul(w1_ref[...], x9_ref[:, cols])
 
     for plane in range(16):
@@ -466,8 +466,8 @@
         pre = summed(plane, 1)
         negative = jnp.exp(jnp.minimum(pre, 0.0))
         if 4 <= plane < 12:
-            slope1_ref[:, plane_cols(plane - 4)] = jnp.where(pre > 0, 1.0, negative)
-        hidden = jnp.where(pre > 0, pre, negative - 1.0) * masks[bx]
+            slope1_ref[:, plane_cols(plane - 4)] = negative
+        hidden = (jnp.maximum(pre, 0.0) + (negative - 1.0)) * masks[bx]
         hidden = hidden.astype(bf16)
         for c in (-1, 0, 1):
             if c == 0:
@@ -480,16 +480,16 @@
                 row = (3 * (b + 1) + c + 1) * C
                 h9_ref[row : row + C, plane_cols(plane)] = roll(source, -step) if step else source
 
-    for n in range(8):
-        cols = slice(256 * n, 256 * (n + 1))
+    for n in range(4):
+        cols = slice(512 * n, 512 * (n + 1))
         product_ref[:, cols] = matmul(w2_ref[...], h9_ref[:, cols])
 
     for plane in range(12):
         bx = (plane + 6) // 8
         pre = summed(plane, 2)
         negative = jnp.exp(jnp.minimum(pre, 0.0))
-        slope2_ref[:, plane_cols(plane)] = jnp.where(pre > 0, 1.0, negative) * masks[bx]
-        hidden = jnp.where(pre > 0, pre, negative - 1.0) * masks[bx]
+        slope2_ref[:, plane_cols(plane)] = negative * masks[bx]
+        hidden = (jnp.maximum(pre, 0.0) + (negative - 1.0)) * masks[bx]
         hid2_ref[:, plane_cols(plane)] = hidden.astype(jnp.bfloat16)
 
     logits = matmul(h_ref[...], hid2_ref[...])
@@ -538,8 +538,8 @@
     for a in range(3):
         for x in range(8):
             shifted_ref[C * a : C * (a + 1), plane_cols(x)] = grad2_ref[:, plane_cols(x + 4 - 2 * a)]
-    for n in range(4):
-        cols = slice(256 * n, 256 * (n + 1))
+    for n in range(2):
+        cols = slice(512 * n, 512 * (n + 1))
         back_ref[:, cols] = matmul(w2t_ref[...], shifted_ref[:, cols])
     grad1 = []
     for x in range(8):

time: 47.8 us -> 47.8 us (level)
  no operation moved by 1% of the time
where the time goes in v7:
time: 47.8 us; the launch traced here: 47.5 us
  blocking collectives  22.8 us (48%)
  waiting for transfers between devices  7.46 us (16%)
  starting transfers between devices  7.4 us (15%)
  Pallas kernels  5.93 us (12%)
  local copies, waits for them, and re-layouts  3.19 us (7%)
  between operations  0.7 us (1%)
    all_to_all x2, blocking collectives, exchange(): lax.all_to_all(values, ('dp', 'space'), 0, 0, axis_index_groups=groups, t...  22.8 us
    ppermute x5, starting transfers between devices, swap(): lax.ppermute(values, 'space', [(s, s ^ mask) for s in range(space_count)])  7.33 us
    ppermute x5, waiting for transfers between devices, swap(): lax.ppermute(values, 'space', [(s, s ^ mask) for s in range(space_count)])  4.6 us
    pallas_call x1, Pallas kernels, on_device_flat(): pl.pallas_call(functools.partial(crop_kernel, scale), out_shape=(shape((8...  3.76 us
    unnamed x12, local copies, waits for them, and re-layouts  3.19 us
    ppermute x2, waiting for transfers between devices, swap_cores(): return lax.ppermute(values, 'dp', [(d, d ^ 1) for d in range(dp_count)])  2.87 us
    pallas_call x1, Pallas kernels, on_device_flat(): pl.pallas_call(unpack_kernel, out_shape=(shape((27, C, C), f32), shape((2...  1.28 us
  transfers between devices with their start and end apart: 7, of which 6 were waited for; matrix products, arithmetic and copies ran while one was open for 0% of the time, Pallas kernels for 1%

profile of v7, /device:TPU:0, one launch (start us, length us, event | category | flops | bytes accessed | tf_op | source)
XLA Modules:
  0.0 47.5 jit_solution(10393885757781987462)
XLA Ops:
  0.6 3.0 %collective-permute-start = (bf16[1,1,48,512]{3,2,1,0:T(8,128)(2,1)}, bf16[1,1,48,512]{3,2,1,0:T(8,128)(2,1)S(1)}, u32[]{:S(2)}, u32[]{:S(2)}) collective-permute-start(bf16[1,1,48,512]{3,2,1,0:T(8,128)(2,1)} %param.6), channel_id=1, source_target_pairs={{0,1},{1,0},{2,3},{3,2},{4,5},{5,4},{6,7},{7,6},{8,9},{9,8},{10,11... | collective-permute-start | bytes 147464 | tf_op jit(solution)/shard_map/ppermute | solution.py:622
  3.6 0.0 copy-start.3
  3.6 0.1 collective-permute-start.1
  3.7 0.0 copy-start.4
  3.7 0.6 %copy-done.3 = s32[1,1,3,512]{3,1,2,0:T(1,128)S(1)} copy-done((s32[1,1,3,512]{3,1,2,0:T(1,128)S(1)}, s32[1,1,3,512]{3,1,2,0:T(1,128)}, u32[]{:S(2)}) %copy-start.3) | copy-done | bytes 6168
  4.3 0.1 copy-done.4
  4.4 0.0 copy-start.2
  4.4 0.8 %copy-done.2 = bf16[1,1,48,512]{3,2,1,0:T(8,128)(2,1)S(1)} copy-done((bf16[1,1,48,512]{3,2,1,0:T(8,128)(2,1)S(1)}, bf16[1,1,48,512]{3,2,1,0:T(8,128)(2,1)}, u32[]{:S(2)}) %copy-start.2) | copy-done | bytes 49176
  5.2 0.2 pack_own.1
  5.3 2.1 %collective-permute-done.1 = s32[1,1,3,512]{3,0,2,1:T(1,128)S(1)} collective-permute-done((s32[1,1,3,512]{3,0,2,1:T(1,128)}, s32[1,1,3,512]{3,0,2,1:T(1,128)S(1)}, u32[]{:S(2)}, u32[]{:S(2)}) %collective-permute-start.1) | collective-permute-done | bytes 6176 | tf_op jit(solution)/shard_map/ppermute | solution.py:622
  7.5 0.0 collective-permute-done
  7.5 0.2 pack_mate.1
  7.6 2.7 %collective-permute-start.2 = (bf16[2,8,16,128]{3,2,1,0:T(8,128)(2,1)S(1)}, bf16[2,8,16,128]{3,2,1,0:T(8,128)(2,1)S(1)}, u32[]{:S(2)}, u32[]{:S(2)}) collective-permute-start(bf16[2,8,16,128]{3,2,1,0:T(8,128)(2,1)S(1)} %get-tuple-element.29), channel_id=1, source_target_pairs={{0,4},{1,5},{2,6},{3,7},{4,0},{5,1},{6,2},{7,3},{8,12},{9,13},{10,... | collective-permute-start | bytes 196616 | tf_op jit(solution)/shard_map/ppermute | solution.py:622
  10.3 0.0 copy-start.5
  10.3 1.3 %collective-permute-start.3 = (bf16[2,8,16,128]{3,2,1,0:T(8,128)(2,1)S(1)}, bf16[2,8,16,128]{3,2,1,0:T(8,128)(2,1)S(1)}, u32[]{:S(2)}, u32[]{:S(2)}) collective-permute-start(bf16[2,8,16,128]{3,2,1,0:T(8,128)(2,1)S(1)} %get-tuple-element.30), channel_id=1, source_target_pairs={{0,6},{1,7},{2,4},{3,5},{4,2},{5,3},{6,0},{7,1},{8,14},{9,15},{10,... | collective-permute-start | bytes 196616 | tf_op jit(solution)/shard_map/ppermute | solution.py:622
  11.7 0.2 collective-permute-start.4
  11.9 0.0 copy-done.5
  11.9 0.1 lay_out_head.1
  12.0 0.0 copy-start
  12.0 1.0 %copy-done = bf16[48,27,48]{2,0,1:T(8,128)(2,1)S(1)} copy-done((bf16[48,27,48]{2,0,1:T(8,128)(2,1)S(1)}, bf16[48,27,48]{2,0,1:T(8,128)(2,1)}, u32[]{:S(2)}) %copy-start) | copy-done | bytes 124440
  12.9 0.0 copy-start.1
  12.9 0.2 prepare.1
  13.2 0.8 %copy-done.1 = bf16[48,27,48]{2,0,1:T(8,128)(2,1)S(1)} copy-done((bf16[48,27,48]{2,0,1:T(8,128)(2,1)S(1)}, bf16[48,27,48]{2,0,1:T(8,128)(2,1)}, u32[]{:S(2)}) %copy-start.1) | copy-done | bytes 124440
  13.9 0.2 second_weights.1
  14.2 0.6 %collective-permute-done.2.refs_0_ = bf16[2,8,16,128]{3,2,1,0:T(8,128)(2,1)S(1)} collective-permute-done((bf16[2,8,16,128]{3,2,1,0:T(8,128)(2,1)S(1)}, bf16[2,8,16,128]{3,2,1,0:T(8,128)(2,1)S(1)}, u32[]{:S(2)}, u32[]{:S(2)}) %collective-permute-start.2) | collective-permute-done | bytes 65568 | tf_op jit(solution)/shard_map/ppermute | solution.py:622
  14.8 1.7 %collective-permute-done.3.refs_1_ = bf16[2,8,16,128]{3,2,1,0:T(8,128)(2,1)S(1)} collective-permute-done((bf16[2,8,16,128]{3,2,1,0:T(8,128)(2,1)S(1)}, bf16[2,8,16,128]{3,2,1,0:T(8,128)(2,1)S(1)}, u32[]{:S(2)}, u32[]{:S(2)}) %collective-permute-start.3) | collective-permute-done | bytes 65568 | tf_op jit(solution)/shard_map/ppermute | solution.py:622
  16.5 0.1 collective-permute-done.4.refs_2_
  16.6 3.8 %forward_backward.1 = (f32[8,512]{1,0:T(8,128)S(1)}, f32[512,128]{1,0:T(8,128)S(1)}, f32[512,128]{1,0:T(8,128)S(1)}) custom-call(s32[1,128]{1,0:T(1,128)S(1)} %get-tuple-element.24.owners_ref, f32[8,128]{1,0:T(8,128)S(1)} %get-tuple-element.25.masks_ref, bf16[13,16,128]{2,1,0:T(8,128)(2,1)S(1)} %get-tuple-element.26.own_ref, ...), custom_call_target="tpu_custom_call" | custom-call | tf_op jit(solution)/shard_map/forward_backward/pallas_call | solution.py:692
  20.4 0.1 collective-permute-start.5
  20.5 1.5 %collective-permute-done.5.other_ref = f32[512,128]{1,0:T(8,128)S(1)} collective-permute-done((f32[512,128]{1,0:T(8,128)S(1)}, f32[512,128]{1,0:T(8,128)S(1)}, u32[]{:S(2)}, u32[]{:S(2)}) %collective-permute-start.5) | collective-permute-done | bytes 262176 | tf_op jit(solution)/shard_map/ppermute | solution.py:718
  22.0 12.2 %all_to_all.10.parts_ref = bf16[16,32,128]{2,1,0:T(8,128)(2,1)S(1)} all-to-all(bf16[16,32,128]{2,1,0:T(8,128)(2,1)S(1)} %bitcast.14), channel_id=1, replica_groups={{0,1,2,3,4,5,6,7,16,17,18,19,20,21,22,23},{8,9,10,11,12,13,14,15,24,25,..., dimensions={0} | all-to-all | bytes 262144 | tf_op jit(solution)/shard_map/all_to_all | solution.py:727
  34.2 10.6 %all_to_all.11 = bf16[16,32,128]{2,1,0:T(8,128)(2,1)S(1)} all-to-all(bf16[16,32,128]{2,1,0:T(8,128)(2,1)S(1)} %gradient_sum.3), channel_id=1, replica_groups={{0,1,2,3,4,5,6,7,16,17,18,19,20,21,22,23},{8,9,10,11,12,13,14,15,24,25,..., dimensions={0} | all-to-all | bytes 262144 | tf_op jit(solution)/shard_map/all_to_all | solution.py:727
  44.8 0.0 collective-permute-start.6
  44.8 1.3 %collective-permute-done.6.other_ref = bf16[512,128]{1,0:T(8,128)(2,1)S(1)} collective-permute-done((bf16[512,128]{1,0:T(8,128)(2,1)S(1)}, bf16[512,128]{1,0:T(8,128)(2,1)S(1)}, u32[]{:S(2)}, u32[]{:S(2)}) %collective-permute-start.6) | collective-permute-done | bytes 131104 | tf_op jit(solution)/shard_map/ppermute | solution.py:718
  46.2 1.3 %unpack_gradients.1 = (f32[27,48,48]{2,1,0:T(8,128)}, f32[27,48,48]{2,1,0:T(8,128)}, f32[3,48]{1,0:T(4,128)}, f32[3,1,512]{2,1,0:T(1,128)}) custom-call(bf16[512,128]{1,0:T(8,128)(2,1)S(1)} %bitcast.16, bf16[512,128]{1,0:T(8,128)(2,1)S(1)} %collective-permute-done.6.other_ref, f32[8,512]{1,0:T(8,128)S(1)} %get-tuple-element.39.logits_ref), custom_call_target="tpu_custom_call" | custom-call | tf_op jit(solution)/shard_map/unpack_gradients/pallas_call | solution.py:745
  (3 shorter events, 0.1 us)
Async XLA Ops:
  0.6 6.8 %collective-permute-start = (bf16[1,1,48,512]{3,2,1,0:T(8,128)(2,1)}, bf16[1,1,48,512]{3,2,1,0:T(8,128)(2,1)S(1)}, u32[]{:S(2)}, u32[]{:S(2)}) collective-permute-start(bf16[1,1,48,512]{3,2,1,0:T(8,128)(2,1)} %param.6), channel_id=1, source_target_pairs={{0,1},{1,0},{2,3},{3,2},{4,5},{5,4},{6,7},{7,6},{8,9},{9,8},{10,11... | collective-permute-start | bytes 147464 | tf_op jit(solution)/shard_map/ppermute | solution.py:622
  3.6 0.7 %copy-start.3 = (s32[1,1,3,512]{3,1,2,0:T(1,128)S(1)}, s32[1,1,3,512]{3,1,2,0:T(1,128)}, u32[]{:S(2)}) copy-start(s32[1,1,3,512]{3,1,2,0:T(1,128)} %param.11) | copy-start | bytes 18436
  3.6 3.8 %collective-permute-start.1 = (s32[1,1,3,512]{3,0,2,1:T(1,128)}, s32[1,1,3,512]{3,0,2,1:T(1,128)S(1)}, u32[]{:S(2)}, u32[]{:S(2)}) collective-permute-start(s32[1,1,3,512]{3,0,2,1:T(1,128)} %bitcast.22), channel_id=1, source_target_pairs={{0,1},{1,0},{2,3},{3,2},{4,5},{5,4},{6,7},{7,6},{8,9},{9,8},{10,11... | collective-permute-start | bytes 18440 | tf_op jit(solution)/shard_map/ppermute | solution.py:622
  3.7 0.7 %copy-start.4 = (s32[1,8]{1,0:T(1,128)S(1)}, s32[1,8]{1,0:T(1,128)}, u32[]{:S(2)}) copy-start(s32[1,8]{1,0:T(1,128)} %block_ref.5) | copy-start | bytes 100
  4.4 0.8 %copy-start.2 = (bf16[1,1,48,512]{3,2,1,0:T(8,128)(2,1)S(1)}, bf16[1,1,48,512]{3,2,1,0:T(8,128)(2,1)}, u32[]{:S(2)}) copy-start(bf16[1,1,48,512]{3,2,1,0:T(8,128)(2,1)} %param.6) | copy-start | bytes 147460
  7.6 7.1 %collective-permute-start.2 = (bf16[2,8,16,128]{3,2,1,0:T(8,128)(2,1)S(1)}, bf16[2,8,16,128]{3,2,1,0:T(8,128)(2,1)S(1)}, u32[]{:S(2)}, u32[]{:S(2)}) collective-permute-start(bf16[2,8,16,128]{3,2,1,0:T(8,128)(2,1)S(1)} %get-tuple-element.29), channel_id=1, source_target_pairs={{0,4},{1,5},{2,6},{3,7},{4,0},{5,1},{6,2},{7,3},{8,12},{9,13},{10,... | collective-permute-start | bytes 196616 | tf_op jit(solution)/shard_map/ppermute | solution.py:622
  10.3 1.6 %copy-start.5 = (bf16[3,48]{1,0:T(4,128)(2,1)S(1)}, bf16[3,48]{1,0:T(4,128)(2,1)}, u32[]{:S(2)}) copy-start(bf16[3,48]{1,0:T(4,128)(2,1)} %head_ref.1) | copy-start | bytes 868
  10.3 6.2 %collective-permute-start.3 = (bf16[2,8,16,128]{3,2,1,0:T(8,128)(2,1)S(1)}, bf16[2,8,16,128]{3,2,1,0:T(8,128)(2,1)S(1)}, u32[]{:S(2)}, u32[]{:S(2)}) collective-permute-start(bf16[2,8,16,128]{3,2,1,0:T(8,128)(2,1)S(1)} %get-tuple-element.30), channel_id=1, source_target_pairs={{0,6},{1,7},{2,4},{3,5},{4,2},{5,3},{6,0},{7,1},{8,14},{9,15},{10,... | collective-permute-start | bytes 196616 | tf_op jit(solution)/shard_map/ppermute | solution.py:622
  11.7 5.0 %collective-permute-start.4 = (bf16[2,8,16,128]{3,2,1,0:T(8,128)(2,1)S(1)}, bf16[2,8,16,128]{3,2,1,0:T(8,128)(2,1)S(1)}, u32[]{:S(2)}, u32[]{:S(2)}) collective-permute-start(bf16[2,8,16,128]{3,2,1,0:T(8,128)(2,1)S(1)} %get-tuple-element.31), channel_id=1, source_target_pairs={{0,2},{1,3},{2,0},{3,1},{4,6},{5,7},{6,4},{7,5},{8,10},{9,11},{10,... | collective-permute-start | bytes 196616 | tf_op jit(solution)/shard_map/ppermute | solution.py:622
  12.0 1.0 %copy-start = (bf16[48,27,48]{2,0,1:T(8,128)(2,1)S(1)}, bf16[48,27,48]{2,0,1:T(8,128)(2,1)}, u32[]{:S(2)}) copy-start(bf16[48,27,48]{2,0,1:T(8,128)(2,1)} %param.8) | copy-start | bytes 373252
  12.9 1.0 %copy-start.1 = (bf16[48,27,48]{2,0,1:T(8,128)(2,1)S(1)}, bf16[48,27,48]{2,0,1:T(8,128)(2,1)}, u32[]{:S(2)}) copy-start(bf16[48,27,48]{2,0,1:T(8,128)(2,1)} %param.9) | copy-start | bytes 373252
  20.4 1.6 %collective-permute-start.5 = (f32[512,128]{1,0:T(8,128)S(1)}, f32[512,128]{1,0:T(8,128)S(1)}, u32[]{:S(2)}, u32[]{:S(2)}) collective-permute-start(f32[512,128]{1,0:T(8,128)S(1)} %get-tuple-element.38), channel_id=1, source_target_pairs={{0,8},{8,0},{16,24},{24,16},{1,9},{9,1},{17,25},{25,17},{2,10},{10... | collective-permute-start | bytes 786440 | tf_op jit(solution)/shard_map/ppermute | solution.py:718
  44.8 1.3 %collective-permute-start.6 = (bf16[512,128]{1,0:T(8,128)(2,1)S(1)}, bf16[512,128]{1,0:T(8,128)(2,1)S(1)}, u32[]{:S(2)}, u32[]{:S(2)}) collective-permute-start(bf16[512,128]{1,0:T(8,128)(2,1)S(1)} %bitcast.15), channel_id=1, source_target_pairs={{0,8},{8,0},{16,24},{24,16},{1,9},{9,1},{17,25},{25,17},{2,10},{10... | collective-permute-start | bytes 393224 | tf_op jit(solution)/shard_map/ppermute | solution.py:718

commit v8 on v7

--- a/solution.py
+++ b/solution.py
@@ -533,7 +533,7 @@
             shifted_ref[C * a : C * (a + 1), plane_cols(x + 2 * a)] = (
                 grad2_ref[:, plane_cols(x + 2)] * own_bf16
             )
-    second_part = matmul_lanes(shifted_ref[...], h9_ref[:, 2 * LANES : 14 * LANES])
+    second_part = matmul_lanes(h9_ref[:, 2 * LANES : 14 * LANES], shifted_ref[...]).T
 
     for a in range(3):
         for x in range(8):
@@ -561,8 +561,8 @@
         for x in range(8):
             shifted_ref[C * a : C * (a + 1), plane_cols(x + a)] = grad1[x]
     first_part = matmul_lanes(
-        shifted_ref[:, 0 : 10 * LANES], x9_ref[:, 4 * LANES : 14 * LANES]
-    )
+        x9_ref[:, 4 * LANES : 14 * LANES], shifted_ref[:, 0 : 10 * LANES]
+    ).T
 
     first_core = (lax.axis_index("dp") & 1) == 0
     head_part = jnp.concatenate([head_part, jnp.zeros((24, 16), jnp.float32)], axis=0)

time: 47.8 us -> 48.4 us (1.013)
  Pallas kernels: 5.93 us -> 6.52 us
    pallas_call x1, Pallas kernels: 3.76 us -> 4.35 us  [on_device_flat(): pl.pallas_call(functools.partial(crop_kernel, scale), out_shape=(shape((8...]
where the time goes in v8:
time: 48.4 us; the launch traced here: 48.1 us
  blocking collectives  22.8 us (47%)
  waiting for transfers between devices  7.46 us (15%)
  starting transfers between devices  7.4 us (15%)
  Pallas kernels  6.52 us (13%)
  local copies, waits for them, and re-layouts  3.19 us (7%)
  between operations  0.7 us (1%)
    all_to_all x2, blocking collectives, exchange(): lax.all_to_all(values, ('dp', 'space'), 0, 0, axis_index_groups=groups, t...  22.8 us
    ppermute x5, starting transfers between devices, swap(): lax.ppermute(values, 'space', [(s, s ^ mask) for s in range(space_count)])  7.33 us
    ppermute x5, waiting for transfers between devices, swap(): lax.ppermute(values, 'space', [(s, s ^ mask) for s in range(space_count)])  4.6 us
    pallas_call x1, Pallas kernels, on_device_flat(): pl.pallas_call(functools.partial(crop_kernel, scale), out_shape=(shape((8...  4.35 us
    unnamed x12, local copies, waits for them, and re-layouts  3.19 us
    ppermute x2, waiting for transfers between devices, swap_cores(): return lax.ppermute(values, 'dp', [(d, d ^ 1) for d in range(dp_count)])  2.87 us
    pallas_call x1, Pallas kernels, on_device_flat(): pl.pallas_call(unpack_kernel, out_shape=(shape((27, C, C), f32), shape((2...  1.28 us
  transfers between devices with their start and end apart: 7, of which 6 were waited for; matrix products, arithmetic and copies ran while one was open for 0% of the time, Pallas kernels for 1%

profile of v8, /device:TPU:0, one launch (start us, length us, event | category | flops | bytes accessed | tf_op | source)
XLA Modules:
  0.0 48.1 jit_solution(4957126276257464053)
XLA Ops:
  0.6 3.0 %collective-permute-start = (bf16[1,1,48,512]{3,2,1,0:T(8,128)(2,1)}, bf16[1,1,48,512]{3,2,1,0:T(8,128)(2,1)S(1)}, u32[]{:S(2)}, u32[]{:S(2)}) collective-permute-start(bf16[1,1,48,512]{3,2,1,0:T(8,128)(2,1)} %param.6), channel_id=1, source_target_pairs={{0,1},{1,0},{2,3},{3,2},{4,5},{5,4},{6,7},{7,6},{8,9},{9,8},{10,11... | collective-permute-start | bytes 147464 | tf_op jit(solution)/shard_map/ppermute | solution.py:622
  3.6 0.0 copy-start.3
  3.6 0.1 collective-permute-start.1
  3.7 0.0 copy-start.4
  3.7 0.6 %copy-done.3 = s32[1,1,3,512]{3,1,2,0:T(1,128)S(1)} copy-done((s32[1,1,3,512]{3,1,2,0:T(1,128)S(1)}, s32[1,1,3,512]{3,1,2,0:T(1,128)}, u32[]{:S(2)}) %copy-start.3) | copy-done | bytes 6168
  4.3 0.1 copy-done.4
  4.4 0.0 copy-start.2
  4.4 0.8 %copy-done.2 = bf16[1,1,48,512]{3,2,1,0:T(8,128)(2,1)S(1)} copy-done((bf16[1,1,48,512]{3,2,1,0:T(8,128)(2,1)S(1)}, bf16[1,1,48,512]{3,2,1,0:T(8,128)(2,1)}, u32[]{:S(2)}) %copy-start.2) | copy-done | bytes 49176
  5.2 0.2 pack_own.1
  5.3 2.1 %collective-permute-done.1 = s32[1,1,3,512]{3,0,2,1:T(1,128)S(1)} collective-permute-done((s32[1,1,3,512]{3,0,2,1:T(1,128)}, s32[1,1,3,512]{3,0,2,1:T(1,128)S(1)}, u32[]{:S(2)}, u32[]{:S(2)}) %collective-permute-start.1) | collective-permute-done | bytes 6176 | tf_op jit(solution)/shard_map/ppermute | solution.py:622
  7.5 0.0 collective-permute-done
  7.5 0.2 pack_mate.1
  7.6 2.7 %collective-permute-start.2 = (bf16[2,8,16,128]{3,2,1,0:T(8,128)(2,1)S(1)}, bf16[2,8,16,128]{3,2,1,0:T(8,128)(2,1)S(1)}, u32[]{:S(2)}, u32[]{:S(2)}) collective-permute-start(bf16[2,8,16,128]{3,2,1,0:T(8,128)(2,1)S(1)} %get-tuple-element.29), channel_id=1, source_target_pairs={{0,4},{1,5},{2,6},{3,7},{4,0},{5,1},{6,2},{7,3},{8,12},{9,13},{10,... | collective-permute-start | bytes 196616 | tf_op jit(solution)/shard_map/ppermute | solution.py:622
  10.3 0.0 copy-start.5
  10.3 1.3 %collective-permute-start.3 = (bf16[2,8,16,128]{3,2,1,0:T(8,128)(2,1)S(1)}, bf16[2,8,16,128]{3,2,1,0:T(8,128)(2,1)S(1)}, u32[]{:S(2)}, u32[]{:S(2)}) collective-permute-start(bf16[2,8,16,128]{3,2,1,0:T(8,128)(2,1)S(1)} %get-tuple-element.30), channel_id=1, source_target_pairs={{0,6},{1,7},{2,4},{3,5},{4,2},{5,3},{6,0},{7,1},{8,14},{9,15},{10,... | collective-permute-start | bytes 196616 | tf_op jit(solution)/shard_map/ppermute | solution.py:622
  11.7 0.2 collective-permute-start.4
  11.9 0.0 copy-done.5
  11.9 0.1 lay_out_head.1
  12.0 0.0 copy-start
  12.0 1.0 %copy-done = bf16[48,27,48]{2,0,1:T(8,128)(2,1)S(1)} copy-done((bf16[48,27,48]{2,0,1:T(8,128)(2,1)S(1)}, bf16[48,27,48]{2,0,1:T(8,128)(2,1)}, u32[]{:S(2)}) %copy-start) | copy-done | bytes 124440
  12.9 0.0 copy-start.1
  12.9 0.2 prepare.1
  13.2 0.8 %copy-done.1 = bf16[48,27,48]{2,0,1:T(8,128)(2,1)S(1)} copy-done((bf16[48,27,48]{2,0,1:T(8,128)(2,1)S(1)}, bf16[48,27,48]{2,0,1:T(8,128)(2,1)}, u32[]{:S(2)}) %copy-start.1) | copy-done | bytes 124440
  13.9 0.2 second_weights.1
  14.2 0.6 %collective-permute-done.2.refs_0_ = bf16[2,8,16,128]{3,2,1,0:T(8,128)(2,1)S(1)} collective-permute-done((bf16[2,8,16,128]{3,2,1,0:T(8,128)(2,1)S(1)}, bf16[2,8,16,128]{3,2,1,0:T(8,128)(2,1)S(1)}, u32[]{:S(2)}, u32[]{:S(2)}) %collective-permute-start.2) | collective-permute-done | bytes 65568 | tf_op jit(solution)/shard_map/ppermute | solution.py:622
  14.8 1.7 %collective-permute-done.3.refs_1_ = bf16[2,8,16,128]{3,2,1,0:T(8,128)(2,1)S(1)} collective-permute-done((bf16[2,8,16,128]{3,2,1,0:T(8,128)(2,1)S(1)}, bf16[2,8,16,128]{3,2,1,0:T(8,128)(2,1)S(1)}, u32[]{:S(2)}, u32[]{:S(2)}) %collective-permute-start.3) | collective-permute-done | bytes 65568 | tf_op jit(solution)/shard_map/ppermute | solution.py:622
  16.5 0.1 collective-permute-done.4.refs_2_
  16.6 4.4 %forward_backward.1 = (f32[8,512]{1,0:T(8,128)S(1)}, f32[512,128]{1,0:T(8,128)S(1)}, f32[512,128]{1,0:T(8,128)S(1)}) custom-call(s32[1,128]{1,0:T(1,128)S(1)} %get-tuple-element.24.owners_ref, f32[8,128]{1,0:T(8,128)S(1)} %get-tuple-element.25.masks_ref, bf16[13,16,128]{2,1,0:T(8,128)(2,1)S(1)} %get-tuple-element.26.own_ref, ...), custom_call_target="tpu_custom_call" | custom-call | tf_op jit(solution)/shard_map/forward_backward/pallas_call | solution.py:692
  21.0 0.1 collective-permute-start.5
  21.1 1.5 %collective-permute-done.5.other_ref = f32[512,128]{1,0:T(8,128)S(1)} collective-permute-done((f32[512,128]{1,0:T(8,128)S(1)}, f32[512,128]{1,0:T(8,128)S(1)}, u32[]{:S(2)}, u32[]{:S(2)}) %collective-permute-start.5) | collective-permute-done | bytes 262176 | tf_op jit(solution)/shard_map/ppermute | solution.py:718
  22.6 12.2 %all_to_all.10.parts_ref = bf16[16,32,128]{2,1,0:T(8,128)(2,1)S(1)} all-to-all(bf16[16,32,128]{2,1,0:T(8,128)(2,1)S(1)} %bitcast.14), channel_id=1, replica_groups={{0,1,2,3,4,5,6,7,16,17,18,19,20,21,22,23},{8,9,10,11,12,13,14,15,24,25,..., dimensions={0} | all-to-all | bytes 262144 | tf_op jit(solution)/shard_map/all_to_all | solution.py:727
  34.8 10.6 %all_to_all.11 = bf16[16,32,128]{2,1,0:T(8,128)(2,1)S(1)} all-to-all(bf16[16,32,128]{2,1,0:T(8,128)(2,1)S(1)} %gradient_sum.3), channel_id=1, replica_groups={{0,1,2,3,4,5,6,7,16,17,18,19,20,21,22,23},{8,9,10,11,12,13,14,15,24,25,..., dimensions={0} | all-to-all | bytes 262144 | tf_op jit(solution)/shard_map/all_to_all | solution.py:727
  45.4 0.0 collective-permute-start.6
  45.4 1.3 %collective-permute-done.6.other_ref = bf16[512,128]{1,0:T(8,128)(2,1)S(1)} collective-permute-done((bf16[512,128]{1,0:T(8,128)(2,1)S(1)}, bf16[512,128]{1,0:T(8,128)(2,1)S(1)}, u32[]{:S(2)}, u32[]{:S(2)}) %collective-permute-start.6) | collective-permute-done | bytes 131104 | tf_op jit(solution)/shard_map/ppermute | solution.py:718
  46.8 1.3 %unpack_gradients.1 = (f32[27,48,48]{2,1,0:T(8,128)}, f32[27,48,48]{2,1,0:T(8,128)}, f32[3,48]{1,0:T(4,128)}, f32[3,1,512]{2,1,0:T(1,128)}) custom-call(bf16[512,128]{1,0:T(8,128)(2,1)S(1)} %bitcast.16, bf16[512,128]{1,0:T(8,128)(2,1)S(1)} %collective-permute-done.6.other_ref, f32[8,512]{1,0:T(8,128)S(1)} %get-tuple-element.39.logits_ref), custom_call_target="tpu_custom_call" | custom-call | tf_op jit(solution)/shard_map/unpack_gradients/pallas_call | solution.py:745
  (3 shorter events, 0.1 us)
Async XLA Ops:
  0.6 6.8 %collective-permute-start = (bf16[1,1,48,512]{3,2,1,0:T(8,128)(2,1)}, bf16[1,1,48,512]{3,2,1,0:T(8,128)(2,1)S(1)}, u32[]{:S(2)}, u32[]{:S(2)}) collective-permute-start(bf16[1,1,48,512]{3,2,1,0:T(8,128)(2,1)} %param.6), channel_id=1, source_target_pairs={{0,1},{1,0},{2,3},{3,2},{4,5},{5,4},{6,7},{7,6},{8,9},{9,8},{10,11... | collective-permute-start | bytes 147464 | tf_op jit(solution)/shard_map/ppermute | solution.py:622
  3.6 0.7 %copy-start.3 = (s32[1,1,3,512]{3,1,2,0:T(1,128)S(1)}, s32[1,1,3,512]{3,1,2,0:T(1,128)}, u32[]{:S(2)}) copy-start(s32[1,1,3,512]{3,1,2,0:T(1,128)} %param.11) | copy-start | bytes 18436
  3.6 3.8 %collective-permute-start.1 = (s32[1,1,3,512]{3,0,2,1:T(1,128)}, s32[1,1,3,512]{3,0,2,1:T(1,128)S(1)}, u32[]{:S(2)}, u32[]{:S(2)}) collective-permute-start(s32[1,1,3,512]{3,0,2,1:T(1,128)} %bitcast.22), channel_id=1, source_target_pairs={{0,1},{1,0},{2,3},{3,2},{4,5},{5,4},{6,7},{7,6},{8,9},{9,8},{10,11... | collective-permute-start | bytes 18440 | tf_op jit(solution)/shard_map/ppermute | solution.py:622
  3.7 0.7 %copy-start.4 = (s32[1,8]{1,0:T(1,128)S(1)}, s32[1,8]{1,0:T(1,128)}, u32[]{:S(2)}) copy-start(s32[1,8]{1,0:T(1,128)} %block_ref.5) | copy-start | bytes 100
  4.4 0.8 %copy-start.2 = (bf16[1,1,48,512]{3,2,1,0:T(8,128)(2,1)S(1)}, bf16[1,1,48,512]{3,2,1,0:T(8,128)(2,1)}, u32[]{:S(2)}) copy-start(bf16[1,1,48,512]{3,2,1,0:T(8,128)(2,1)} %param.6) | copy-start | bytes 147460
  7.6 7.1 %collective-permute-start.2 = (bf16[2,8,16,128]{3,2,1,0:T(8,128)(2,1)S(1)}, bf16[2,8,16,128]{3,2,1,0:T(8,128)(2,1)S(1)}, u32[]{:S(2)}, u32[]{:S(2)}) collective-permute-start(bf16[2,8,16,128]{3,2,1,0:T(8,128)(2,1)S(1)} %get-tuple-element.29), channel_id=1, source_target_pairs={{0,4},{1,5},{2,6},{3,7},{4,0},{5,1},{6,2},{7,3},{8,12},{9,13},{10,... | collective-permute-start | bytes 196616 | tf_op jit(solution)/shard_map/ppermute | solution.py:622
  10.3 1.6 %copy-start.5 = (bf16[3,48]{1,0:T(4,128)(2,1)S(1)}, bf16[3,48]{1,0:T(4,128)(2,1)}, u32[]{:S(2)}) copy-start(bf16[3,48]{1,0:T(4,128)(2,1)} %head_ref.1) | copy-start | bytes 868
  10.3 6.2 %collective-permute-start.3 = (bf16[2,8,16,128]{3,2,1,0:T(8,128)(2,1)S(1)}, bf16[2,8,16,128]{3,2,1,0:T(8,128)(2,1)S(1)}, u32[]{:S(2)}, u32[]{:S(2)}) collective-permute-start(bf16[2,8,16,128]{3,2,1,0:T(8,128)(2,1)S(1)} %get-tuple-element.30), channel_id=1, source_target_pairs={{0,6},{1,7},{2,4},{3,5},{4,2},{5,3},{6,0},{7,1},{8,14},{9,15},{10,... | collective-permute-start | bytes 196616 | tf_op jit(solution)/shard_map/ppermute | solution.py:622
  11.7 5.0 %collective-permute-start.4 = (bf16[2,8,16,128]{3,2,1,0:T(8,128)(2,1)S(1)}, bf16[2,8,16,128]{3,2,1,0:T(8,128)(2,1)S(1)}, u32[]{:S(2)}, u32[]{:S(2)}) collective-permute-start(bf16[2,8,16,128]{3,2,1,0:T(8,128)(2,1)S(1)} %get-tuple-element.31), channel_id=1, source_target_pairs={{0,2},{1,3},{2,0},{3,1},{4,6},{5,7},{6,4},{7,5},{8,10},{9,11},{10,... | collective-permute-start | bytes 196616 | tf_op jit(solution)/shard_map/ppermute | solution.py:622
  12.0 1.0 %copy-start = (bf16[48,27,48]{2,0,1:T(8,128)(2,1)S(1)}, bf16[48,27,48]{2,0,1:T(8,128)(2,1)}, u32[]{:S(2)}) copy-start(bf16[48,27,48]{2,0,1:T(8,128)(2,1)} %param.8) | copy-start | bytes 373252
  12.9 1.0 %copy-start.1 = (bf16[48,27,48]{2,0,1:T(8,128)(2,1)S(1)}, bf16[48,27,48]{2,0,1:T(8,128)(2,1)}, u32[]{:S(2)}) copy-start(bf16[48,27,48]{2,0,1:T(8,128)(2,1)} %param.9) | copy-start | bytes 373252
  21.0 1.6 %collective-permute-start.5 = (f32[512,128]{1,0:T(8,128)S(1)}, f32[512,128]{1,0:T(8,128)S(1)}, u32[]{:S(2)}, u32[]{:S(2)}) collective-permute-start(f32[512,128]{1,0:T(8,128)S(1)} %get-tuple-element.38), channel_id=1, source_target_pairs={{0,8},{8,0},{16,24},{24,16},{1,9},{9,1},{17,25},{25,17},{2,10},{10... | collective-permute-start | bytes 786440 | tf_op jit(solution)/shard_map/ppermute | solution.py:718
  45.4 1.3 %collective-permute-start.6 = (bf16[512,128]{1,0:T(8,128)(2,1)S(1)}, bf16[512,128]{1,0:T(8,128)(2,1)S(1)}, u32[]{:S(2)}, u32[]{:S(2)}) collective-permute-start(bf16[512,128]{1,0:T(8,128)(2,1)S(1)} %bitcast.15), channel_id=1, source_target_pairs={{0,8},{8,0},{16,24},{24,16},{1,9},{9,1},{17,25},{25,17},{2,10},{10... | collective-permute-start | bytes 393224 | tf_op jit(solution)/shard_map/ppermute | solution.py:718

commit v9 on v7

--- a/solution.py
+++ b/solution.py
@@ -193,7 +193,7 @@
     return (target >> 2) - (source >> 2), (target & 3) - (source & 3)
 
 
-PARTNERS = (4, 6, 2)
+PARTNERS = (4, 2, 6)
 
 
 def block_tiles(features_ref, targets_ref):

time: 47.8 us -> 47.7 us (level)
  blocking collectives: 22.8 us -> 21.4 us
  waiting for transfers between devices: 7.46 us -> 8.56 us
    all_to_all x2, blocking collectives: 22.8 us -> 21.4 us  [exchange(): lax.all_to_all(values, ('dp', 'space'), 0, 0, axis_index_groups=groups, t...]
    ppermute x5, waiting for transfers between devices: 4.6 us -> 5.69 us  [swap(): lax.ppermute(values, 'space', [(s, s ^ mask) for s in range(space_count)])]
  transfers between devices with their start and end apart: 7 -> 7, of which waited for: 6 -> 5; matrix products, arithmetic and copies ran while one was open for 0% -> 0% of each run, Pallas kernels for 1% -> 1%
where the time goes in v9:
time: 47.7 us; the launch traced here: 47.4 us
  blocking collectives  21.4 us (45%)
  waiting for transfers between devices  8.56 us (18%)
  starting transfers between devices  7.62 us (16%)
  Pallas kernels  5.92 us (12%)
  local copies, waits for them, and re-layouts  3.19 us (7%)
  between operations  0.71 us (1%)
    all_to_all x2, blocking collectives, exchange(): lax.all_to_all(values, ('dp', 'space'), 0, 0, axis_index_groups=groups, t...  21.4 us
    ppermute x5, starting transfers between devices, swap(): lax.ppermute(values, 'space', [(s, s ^ mask) for s in range(space_count)])  7.54 us
    ppermute x5, waiting for transfers between devices, swap(): lax.ppermute(values, 'space', [(s, s ^ mask) for s in range(space_count)])  5.69 us
    pallas_call x1, Pallas kernels, on_device_flat(): pl.pallas_call(functools.partial(crop_kernel, scale), out_shape=(shape((8...  3.75 us
    unnamed x12, local copies, waits for them, and re-layouts  3.19 us
    ppermute x2, waiting for transfers between devices, swap_cores(): return lax.ppermute(values, 'dp', [(d, d ^ 1) for d in range(dp_count)])  2.87 us
    pallas_call x1, Pallas kernels, on_device_flat(): pl.pallas_call(unpack_kernel, out_shape=(shape((27, C, C), f32), shape((2...  1.28 us
  transfers between devices with their start and end apart: 7, of which 5 were waited for; matrix products, arithmetic and copies ran while one was open for 0% of the time, Pallas kernels for 1%

profile of v9, /device:TPU:0, one launch (start us, length us, event | category | flops | bytes accessed | tf_op | source)
XLA Modules:
  0.0 47.4 jit_solution(6648394989764343444)
XLA Ops:
  0.6 3.0 %collective-permute-start = (bf16[1,1,48,512]{3,2,1,0:T(8,128)(2,1)}, bf16[1,1,48,512]{3,2,1,0:T(8,128)(2,1)S(1)}, u32[]{:S(2)}, u32[]{:S(2)}) collective-permute-start(bf16[1,1,48,512]{3,2,1,0:T(8,128)(2,1)} %param.6), channel_id=1, source_target_pairs={{0,1},{1,0},{2,3},{3,2},{4,5},{5,4},{6,7},{7,6},{8,9},{9,8},{10,11... | collective-permute-start | bytes 147464 | tf_op jit(solution)/shard_map/ppermute | solution.py:622
  3.6 0.0 copy-start.3
  3.6 0.1 collective-permute-start.1
  3.7 0.0 copy-start.4
  3.7 0.6 %copy-done.3 = s32[1,1,3,512]{3,1,2,0:T(1,128)S(1)} copy-done((s32[1,1,3,512]{3,1,2,0:T(1,128)S(1)}, s32[1,1,3,512]{3,1,2,0:T(1,128)}, u32[]{:S(2)}) %copy-start.3) | copy-done | bytes 6168
  4.3 0.1 copy-done.4
  4.4 0.0 copy-start.2
  4.4 0.8 %copy-done.2 = bf16[1,1,48,512]{3,2,1,0:T(8,128)(2,1)S(1)} copy-done((bf16[1,1,48,512]{3,2,1,0:T(8,128)(2,1)S(1)}, bf16[1,1,48,512]{3,2,1,0:T(8,128)(2,1)}, u32[]{:S(2)}) %copy-start.2) | copy-done | bytes 49176
  5.2 0.2 pack_own.1
  5.3 2.1 %collective-permute-done.1 = s32[1,1,3,512]{3,0,2,1:T(1,128)S(1)} collective-permute-done((s32[1,1,3,512]{3,0,2,1:T(1,128)}, s32[1,1,3,512]{3,0,2,1:T(1,128)S(1)}, u32[]{:S(2)}, u32[]{:S(2)}) %collective-permute-start.1) | collective-permute-done | bytes 6176 | tf_op jit(solution)/shard_map/ppermute | solution.py:622
  7.5 0.0 collective-permute-done
  7.5 0.2 pack_mate.1
  7.6 2.7 %collective-permute-start.2 = (bf16[2,8,16,128]{3,2,1,0:T(8,128)(2,1)S(1)}, bf16[2,8,16,128]{3,2,1,0:T(8,128)(2,1)S(1)}, u32[]{:S(2)}, u32[]{:S(2)}) collective-permute-start(bf16[2,8,16,128]{3,2,1,0:T(8,128)(2,1)S(1)} %get-tuple-element.29), channel_id=1, source_target_pairs={{0,4},{1,5},{2,6},{3,7},{4,0},{5,1},{6,2},{7,3},{8,12},{9,13},{10,... | collective-permute-start | bytes 196616 | tf_op jit(solution)/shard_map/ppermute | solution.py:622
  10.3 0.0 copy-start.5
  10.3 1.6 %collective-permute-start.3 = (bf16[2,8,16,128]{3,2,1,0:T(8,128)(2,1)S(1)}, bf16[2,8,16,128]{3,2,1,0:T(8,128)(2,1)S(1)}, u32[]{:S(2)}, u32[]{:S(2)}) collective-permute-start(bf16[2,8,16,128]{3,2,1,0:T(8,128)(2,1)S(1)} %get-tuple-element.30), channel_id=1, source_target_pairs={{0,2},{1,3},{2,0},{3,1},{4,6},{5,7},{6,4},{7,5},{8,10},{9,11},{10,... | collective-permute-start | bytes 196616 | tf_op jit(solution)/shard_map/ppermute | solution.py:622
  11.9 0.2 collective-permute-start.4
  12.1 0.0 copy-done.5
  12.1 0.1 lay_out_head.1
  12.2 0.0 copy-start
  12.2 1.0 %copy-done = bf16[48,27,48]{2,0,1:T(8,128)(2,1)S(1)} copy-done((bf16[48,27,48]{2,0,1:T(8,128)(2,1)S(1)}, bf16[48,27,48]{2,0,1:T(8,128)(2,1)}, u32[]{:S(2)}) %copy-start) | copy-done | bytes 124440
  13.2 0.0 copy-start.1
  13.2 0.2 prepare.1
  13.4 0.8 %copy-done.1 = bf16[48,27,48]{2,0,1:T(8,128)(2,1)S(1)} copy-done((bf16[48,27,48]{2,0,1:T(8,128)(2,1)S(1)}, bf16[48,27,48]{2,0,1:T(8,128)(2,1)}, u32[]{:S(2)}) %copy-start.1) | copy-done | bytes 124440
  14.1 0.2 second_weights.1
  14.4 0.0 collective-permute-done.2.refs_0_
  14.4 0.2 collective-permute-done.3.refs_1_
  14.6 3.3 %collective-permute-done.4.refs_2_ = bf16[2,8,16,128]{3,2,1,0:T(8,128)(2,1)S(1)} collective-permute-done((bf16[2,8,16,128]{3,2,1,0:T(8,128)(2,1)S(1)}, bf16[2,8,16,128]{3,2,1,0:T(8,128)(2,1)S(1)}, u32[]{:S(2)}, u32[]{:S(2)}) %collective-permute-start.4) | collective-permute-done | bytes 65568 | tf_op jit(solution)/shard_map/ppermute | solution.py:622
  17.9 3.8 %forward_backward.1 = (f32[8,512]{1,0:T(8,128)S(1)}, f32[512,128]{1,0:T(8,128)S(1)}, f32[512,128]{1,0:T(8,128)S(1)}) custom-call(s32[1,128]{1,0:T(1,128)S(1)} %get-tuple-element.24.owners_ref, f32[8,128]{1,0:T(8,128)S(1)} %get-tuple-element.25.masks_ref, bf16[13,16,128]{2,1,0:T(8,128)(2,1)S(1)} %get-tuple-element.26.own_ref, ...), custom_call_target="tpu_custom_call" | custom-call | tf_op jit(solution)/shard_map/forward_backward/pallas_call | solution.py:692
  21.7 0.1 collective-permute-start.5
  21.8 1.5 %collective-permute-done.5.other_ref = f32[512,128]{1,0:T(8,128)S(1)} collective-permute-done((f32[512,128]{1,0:T(8,128)S(1)}, f32[512,128]{1,0:T(8,128)S(1)}, u32[]{:S(2)}, u32[]{:S(2)}) %collective-permute-start.5) | collective-permute-done | bytes 262176 | tf_op jit(solution)/shard_map/ppermute | solution.py:718
  23.3 10.7 %all_to_all.10.parts_ref = bf16[16,32,128]{2,1,0:T(8,128)(2,1)S(1)} all-to-all(bf16[16,32,128]{2,1,0:T(8,128)(2,1)S(1)} %bitcast.14), channel_id=1, replica_groups={{0,1,2,3,4,5,6,7,16,17,18,19,20,21,22,23},{8,9,10,11,12,13,14,15,24,25,..., dimensions={0} | all-to-all | bytes 262144 | tf_op jit(solution)/shard_map/all_to_all | solution.py:727
  34.1 10.6 %all_to_all.11 = bf16[16,32,128]{2,1,0:T(8,128)(2,1)S(1)} all-to-all(bf16[16,32,128]{2,1,0:T(8,128)(2,1)S(1)} %gradient_sum.3), channel_id=1, replica_groups={{0,1,2,3,4,5,6,7,16,17,18,19,20,21,22,23},{8,9,10,11,12,13,14,15,24,25,..., dimensions={0} | all-to-all | bytes 262144 | tf_op jit(solution)/shard_map/all_to_all | solution.py:727
  44.7 0.0 collective-permute-start.6
  44.7 1.3 %collective-permute-done.6.other_ref = bf16[512,128]{1,0:T(8,128)(2,1)S(1)} collective-permute-done((bf16[512,128]{1,0:T(8,128)(2,1)S(1)}, bf16[512,128]{1,0:T(8,128)(2,1)S(1)}, u32[]{:S(2)}, u32[]{:S(2)}) %collective-permute-start.6) | collective-permute-done | bytes 131104 | tf_op jit(solution)/shard_map/ppermute | solution.py:718
  46.1 1.3 %unpack_gradients.1 = (f32[27,48,48]{2,1,0:T(8,128)}, f32[27,48,48]{2,1,0:T(8,128)}, f32[3,48]{1,0:T(4,128)}, f32[3,1,512]{2,1,0:T(1,128)}) custom-call(bf16[512,128]{1,0:T(8,128)(2,1)S(1)} %bitcast.16, bf16[512,128]{1,0:T(8,128)(2,1)S(1)} %collective-permute-done.6.other_ref, f32[8,512]{1,0:T(8,128)S(1)} %get-tuple-element.39.logits_ref), custom_call_target="tpu_custom_call" | custom-call | tf_op jit(solution)/shard_map/unpack_gradients/pallas_call | solution.py:745
  (3 shorter events, 0.1 us)
Async XLA Ops:
  0.6 6.8 %collective-permute-start = (bf16[1,1,48,512]{3,2,1,0:T(8,128)(2,1)}, bf16[1,1,48,512]{3,2,1,0:T(8,128)(2,1)S(1)}, u32[]{:S(2)}, u32[]{:S(2)}) collective-permute-start(bf16[1,1,48,512]{3,2,1,0:T(8,128)(2,1)} %param.6), channel_id=1, source_target_pairs={{0,1},{1,0},{2,3},{3,2},{4,5},{5,4},{6,7},{7,6},{8,9},{9,8},{10,11... | collective-permute-start | bytes 147464 | tf_op jit(solution)/shard_map/ppermute | solution.py:622
  3.6 0.7 %copy-start.3 = (s32[1,1,3,512]{3,1,2,0:T(1,128)S(1)}, s32[1,1,3,512]{3,1,2,0:T(1,128)}, u32[]{:S(2)}) copy-start(s32[1,1,3,512]{3,1,2,0:T(1,128)} %param.11) | copy-start | bytes 18436
  3.6 3.8 %collective-permute-start.1 = (s32[1,1,3,512]{3,0,2,1:T(1,128)}, s32[1,1,3,512]{3,0,2,1:T(1,128)S(1)}, u32[]{:S(2)}, u32[]{:S(2)}) collective-permute-start(s32[1,1,3,512]{3,0,2,1:T(1,128)} %bitcast.22), channel_id=1, source_target_pairs={{0,1},{1,0},{2,3},{3,2},{4,5},{5,4},{6,7},{7,6},{8,9},{9,8},{10,11... | collective-permute-start | bytes 18440 | tf_op jit(solution)/shard_map/ppermute | solution.py:622
  3.7 0.7 %copy-start.4 = (s32[1,8]{1,0:T(1,128)S(1)}, s32[1,8]{1,0:T(1,128)}, u32[]{:S(2)}) copy-start(s32[1,8]{1,0:T(1,128)} %block_ref.5) | copy-start | bytes 100
  4.4 0.8 %copy-start.2 = (bf16[1,1,48,512]{3,2,1,0:T(8,128)(2,1)S(1)}, bf16[1,1,48,512]{3,2,1,0:T(8,128)(2,1)}, u32[]{:S(2)}) copy-start(bf16[1,1,48,512]{3,2,1,0:T(8,128)(2,1)} %param.6) | copy-start | bytes 147460
  7.6 6.7 %collective-permute-start.2 = (bf16[2,8,16,128]{3,2,1,0:T(8,128)(2,1)S(1)}, bf16[2,8,16,128]{3,2,1,0:T(8,128)(2,1)S(1)}, u32[]{:S(2)}, u32[]{:S(2)}) collective-permute-start(bf16[2,8,16,128]{3,2,1,0:T(8,128)(2,1)S(1)} %get-tuple-element.29), channel_id=1, source_target_pairs={{0,4},{1,5},{2,6},{3,7},{4,0},{5,1},{6,2},{7,3},{8,12},{9,13},{10,... | collective-permute-start | bytes 196616 | tf_op jit(solution)/shard_map/ppermute | solution.py:622
  10.3 1.8 %copy-start.5 = (bf16[3,48]{1,0:T(4,128)(2,1)S(1)}, bf16[3,48]{1,0:T(4,128)(2,1)}, u32[]{:S(2)}) copy-start(bf16[3,48]{1,0:T(4,128)(2,1)} %head_ref.1) | copy-start | bytes 868
  10.3 4.3 %collective-permute-start.3 = (bf16[2,8,16,128]{3,2,1,0:T(8,128)(2,1)S(1)}, bf16[2,8,16,128]{3,2,1,0:T(8,128)(2,1)S(1)}, u32[]{:S(2)}, u32[]{:S(2)}) collective-permute-start(bf16[2,8,16,128]{3,2,1,0:T(8,128)(2,1)S(1)} %get-tuple-element.30), channel_id=1, source_target_pairs={{0,2},{1,3},{2,0},{3,1},{4,6},{5,7},{6,4},{7,5},{8,10},{9,11},{10,... | collective-permute-start | bytes 196616 | tf_op jit(solution)/shard_map/ppermute | solution.py:622
  11.9 6.1 %collective-permute-start.4 = (bf16[2,8,16,128]{3,2,1,0:T(8,128)(2,1)S(1)}, bf16[2,8,16,128]{3,2,1,0:T(8,128)(2,1)S(1)}, u32[]{:S(2)}, u32[]{:S(2)}) collective-permute-start(bf16[2,8,16,128]{3,2,1,0:T(8,128)(2,1)S(1)} %get-tuple-element.31), channel_id=1, source_target_pairs={{0,6},{1,7},{2,4},{3,5},{4,2},{5,3},{6,0},{7,1},{8,14},{9,15},{10,... | collective-permute-start | bytes 196616 | tf_op jit(solution)/shard_map/ppermute | solution.py:622
  12.2 1.0 %copy-start = (bf16[48,27,48]{2,0,1:T(8,128)(2,1)S(1)}, bf16[48,27,48]{2,0,1:T(8,128)(2,1)}, u32[]{:S(2)}) copy-start(bf16[48,27,48]{2,0,1:T(8,128)(2,1)} %param.8) | copy-start | bytes 373252
  13.2 1.0 %copy-start.1 = (bf16[48,27,48]{2,0,1:T(8,128)(2,1)S(1)}, bf16[48,27,48]{2,0,1:T(8,128)(2,1)}, u32[]{:S(2)}) copy-start(bf16[48,27,48]{2,0,1:T(8,128)(2,1)} %param.9) | copy-start | bytes 373252
  21.7 1.6 %collective-permute-start.5 = (f32[512,128]{1,0:T(8,128)S(1)}, f32[512,128]{1,0:T(8,128)S(1)}, u32[]{:S(2)}, u32[]{:S(2)}) collective-permute-start(f32[512,128]{1,0:T(8,128)S(1)} %get-tuple-element.38), channel_id=1, source_target_pairs={{0,8},{8,0},{16,24},{24,16},{1,9},{9,1},{17,25},{25,17},{2,10},{10... | collective-permute-start | bytes 786440 | tf_op jit(solution)/shard_map/ppermute | solution.py:718
  44.7 1.3 %collective-permute-start.6 = (bf16[512,128]{1,0:T(8,128)(2,1)S(1)}, bf16[512,128]{1,0:T(8,128)(2,1)S(1)}, u32[]{:S(2)}, u32[]{:S(2)}) collective-permute-start(bf16[512,128]{1,0:T(8,128)(2,1)S(1)} %bitcast.15), channel_id=1, source_target_pairs={{0,8},{8,0},{16,24},{24,16},{1,9},{9,1},{17,25},{25,17},{2,10},{10... | collective-permute-start | bytes 393224 | tf_op jit(solution)/shard_map/ppermute | solution.py:718

commit v10 on v7

--- a/solution.py
+++ b/solution.py
@@ -457,9 +457,11 @@
             + product_ref[2 * C : 3 * C, plane_cols(plane + 2 * stride)]
         )
 
-    for n in range(3):
-        cols = slice(768 * n, 768 * (n + 1))
-        product_ref[:, cols] = matmul(w1_ref[...], x9_ref[:, cols])
+    for top, bottom, start, stop in (
+        (0, 2, 0, 2), (0, 3, 2, 6), (0, 3, 6, 10), (0, 3, 10, 16), (1, 3, 16, 18)
+    ):
+        rows, cols = slice(C * top, C * bottom), slice(LANES * start, LANES * stop)
+        product_ref[rows, cols] = matmul(w1_ref[rows, :], x9_ref[:, cols])
 
     for plane in range(16):
         bx = (plane + 4) // 8
@@ -480,9 +482,11 @@
                 row = (3 * (b + 1) + c + 1) * C
                 h9_ref[row : row + C, plane_cols(plane)] = roll(source, -step) if step else source
 
-    for n in range(4):
-        cols = slice(512 * n, 512 * (n + 1))
-        product_ref[:, cols] = matmul(w2_ref[...], h9_ref[:, cols])
+    for top, bottom, start, stop in (
+        (0, 1, 0, 2), (0, 2, 2, 4), (0, 3, 4, 8), (0, 3, 8, 12), (1, 3, 12, 14), (2, 3, 14, 16)
+    ):
+        rows, cols = slice(C * top, C * bottom), slice(LANES * start, LANES * stop)
+        product_ref[rows, cols] = matmul(w2_ref[rows, :], h9_ref[:, cols])
 
     for plane in range(12):
         bx = (plane + 6) // 8

time: 47.8 us -> 47.7 us (level)
  no operation moved by 1% of the time
where the time goes in v10:
time: 47.7 us; the launch traced here: 47.4 us
  blocking collectives  22.8 us (48%)
  waiting for transfers between devices  7.46 us (16%)
  starting transfers between devices  7.4 us (16%)
  Pallas kernels  5.81 us (12%)
  local copies, waits for them, and re-layouts  3.19 us (7%)
  between operations  0.7 us (1%)
    all_to_all x2, blocking collectives, exchange(): lax.all_to_all(values, ('dp', 'space'), 0, 0, axis_index_groups=groups, t...  22.8 us
    ppermute x5, starting transfers between devices, swap(): lax.ppermute(values, 'space', [(s, s ^ mask) for s in range(space_count)])  7.33 us
    ppermute x5, waiting for transfers between devices, swap(): lax.ppermute(values, 'space', [(s, s ^ mask) for s in range(space_count)])  4.6 us
    pallas_call x1, Pallas kernels, on_device_flat(): pl.pallas_call(functools.partial(crop_kernel, scale), out_shape=(shape((8...  3.64 us
    unnamed x12, local copies, waits for them, and re-layouts  3.19 us
    ppermute x2, waiting for transfers between devices, swap_cores(): return lax.ppermute(values, 'dp', [(d, d ^ 1) for d in range(dp_count)])  2.87 us
    pallas_call x1, Pallas kernels, on_device_flat(): pl.pallas_call(unpack_kernel, out_shape=(shape((27, C, C), f32), shape((2...  1.28 us
  transfers between devices with their start and end apart: 7, of which 6 were waited for; matrix products, arithmetic and copies ran while one was open for 0% of the time, Pallas kernels for 1%

profile of v10, /device:TPU:0, one launch (start us, length us, event | category | flops | bytes accessed | tf_op | source)
XLA Modules:
  0.0 47.4 jit_solution(16422226288689638126)
XLA Ops:
  0.6 3.0 %collective-permute-start = (bf16[1,1,48,512]{3,2,1,0:T(8,128)(2,1)}, bf16[1,1,48,512]{3,2,1,0:T(8,128)(2,1)S(1)}, u32[]{:S(2)}, u32[]{:S(2)}) collective-permute-start(bf16[1,1,48,512]{3,2,1,0:T(8,128)(2,1)} %param.6), channel_id=1, source_target_pairs={{0,1},{1,0},{2,3},{3,2},{4,5},{5,4},{6,7},{7,6},{8,9},{9,8},{10,11... | collective-permute-start | bytes 147464 | tf_op jit(solution)/shard_map/ppermute | solution.py:626
  3.6 0.0 copy-start.3
  3.6 0.1 collective-permute-start.1
  3.7 0.0 copy-start.4
  3.7 0.6 %copy-done.3 = s32[1,1,3,512]{3,1,2,0:T(1,128)S(1)} copy-done((s32[1,1,3,512]{3,1,2,0:T(1,128)S(1)}, s32[1,1,3,512]{3,1,2,0:T(1,128)}, u32[]{:S(2)}) %copy-start.3) | copy-done | bytes 6168
  4.3 0.1 copy-done.4
  4.4 0.0 copy-start.2
  4.4 0.8 %copy-done.2 = bf16[1,1,48,512]{3,2,1,0:T(8,128)(2,1)S(1)} copy-done((bf16[1,1,48,512]{3,2,1,0:T(8,128)(2,1)S(1)}, bf16[1,1,48,512]{3,2,1,0:T(8,128)(2,1)}, u32[]{:S(2)}) %copy-start.2) | copy-done | bytes 49176
  5.2 0.2 pack_own.1
  5.3 2.1 %collective-permute-done.1 = s32[1,1,3,512]{3,0,2,1:T(1,128)S(1)} collective-permute-done((s32[1,1,3,512]{3,0,2,1:T(1,128)}, s32[1,1,3,512]{3,0,2,1:T(1,128)S(1)}, u32[]{:S(2)}, u32[]{:S(2)}) %collective-permute-start.1) | collective-permute-done | bytes 6176 | tf_op jit(solution)/shard_map/ppermute | solution.py:626
  7.5 0.0 collective-permute-done
  7.5 0.2 pack_mate.1
  7.6 2.7 %collective-permute-start.2 = (bf16[2,8,16,128]{3,2,1,0:T(8,128)(2,1)S(1)}, bf16[2,8,16,128]{3,2,1,0:T(8,128)(2,1)S(1)}, u32[]{:S(2)}, u32[]{:S(2)}) collective-permute-start(bf16[2,8,16,128]{3,2,1,0:T(8,128)(2,1)S(1)} %get-tuple-element.29), channel_id=1, source_target_pairs={{0,4},{1,5},{2,6},{3,7},{4,0},{5,1},{6,2},{7,3},{8,12},{9,13},{10,... | collective-permute-start | bytes 196616 | tf_op jit(solution)/shard_map/ppermute | solution.py:626
  10.3 0.0 copy-start.5
  10.3 1.3 %collective-permute-start.3 = (bf16[2,8,16,128]{3,2,1,0:T(8,128)(2,1)S(1)}, bf16[2,8,16,128]{3,2,1,0:T(8,128)(2,1)S(1)}, u32[]{:S(2)}, u32[]{:S(2)}) collective-permute-start(bf16[2,8,16,128]{3,2,1,0:T(8,128)(2,1)S(1)} %get-tuple-element.30), channel_id=1, source_target_pairs={{0,6},{1,7},{2,4},{3,5},{4,2},{5,3},{6,0},{7,1},{8,14},{9,15},{10,... | collective-permute-start | bytes 196616 | tf_op jit(solution)/shard_map/ppermute | solution.py:626
  11.7 0.2 collective-permute-start.4
  11.9 0.0 copy-done.5
  11.9 0.1 lay_out_head.1
  12.0 0.0 copy-start
  12.0 1.0 %copy-done = bf16[48,27,48]{2,0,1:T(8,128)(2,1)S(1)} copy-done((bf16[48,27,48]{2,0,1:T(8,128)(2,1)S(1)}, bf16[48,27,48]{2,0,1:T(8,128)(2,1)}, u32[]{:S(2)}) %copy-start) | copy-done | bytes 124440
  12.9 0.0 copy-start.1
  12.9 0.2 prepare.1
  13.2 0.8 %copy-done.1 = bf16[48,27,48]{2,0,1:T(8,128)(2,1)S(1)} copy-done((bf16[48,27,48]{2,0,1:T(8,128)(2,1)S(1)}, bf16[48,27,48]{2,0,1:T(8,128)(2,1)}, u32[]{:S(2)}) %copy-start.1) | copy-done | bytes 124440
  13.9 0.2 second_weights.1
  14.2 0.6 %collective-permute-done.2.refs_0_ = bf16[2,8,16,128]{3,2,1,0:T(8,128)(2,1)S(1)} collective-permute-done((bf16[2,8,16,128]{3,2,1,0:T(8,128)(2,1)S(1)}, bf16[2,8,16,128]{3,2,1,0:T(8,128)(2,1)S(1)}, u32[]{:S(2)}, u32[]{:S(2)}) %collective-permute-start.2) | collective-permute-done | bytes 65568 | tf_op jit(solution)/shard_map/ppermute | solution.py:626
  14.8 1.7 %collective-permute-done.3.refs_1_ = bf16[2,8,16,128]{3,2,1,0:T(8,128)(2,1)S(1)} collective-permute-done((bf16[2,8,16,128]{3,2,1,0:T(8,128)(2,1)S(1)}, bf16[2,8,16,128]{3,2,1,0:T(8,128)(2,1)S(1)}, u32[]{:S(2)}, u32[]{:S(2)}) %collective-permute-start.3) | collective-permute-done | bytes 65568 | tf_op jit(solution)/shard_map/ppermute | solution.py:626
  16.5 0.1 collective-permute-done.4.refs_2_
  16.6 3.6 %forward_backward.1 = (f32[8,512]{1,0:T(8,128)S(1)}, f32[512,128]{1,0:T(8,128)S(1)}, f32[512,128]{1,0:T(8,128)S(1)}) custom-call(s32[1,128]{1,0:T(1,128)S(1)} %get-tuple-element.24.owners_ref, f32[8,128]{1,0:T(8,128)S(1)} %get-tuple-element.25.masks_ref, bf16[13,16,128]{2,1,0:T(8,128)(2,1)S(1)} %get-tuple-element.26.own_ref, ...), custom_call_target="tpu_custom_call" | custom-call | tf_op jit(solution)/shard_map/forward_backward/pallas_call | solution.py:696
  20.3 0.1 collective-permute-start.5
  20.4 1.5 %collective-permute-done.5.other_ref = f32[512,128]{1,0:T(8,128)S(1)} collective-permute-done((f32[512,128]{1,0:T(8,128)S(1)}, f32[512,128]{1,0:T(8,128)S(1)}, u32[]{:S(2)}, u32[]{:S(2)}) %collective-permute-start.5) | collective-permute-done | bytes 262176 | tf_op jit(solution)/shard_map/ppermute | solution.py:722
  21.9 12.2 %all_to_all.10.parts_ref = bf16[16,32,128]{2,1,0:T(8,128)(2,1)S(1)} all-to-all(bf16[16,32,128]{2,1,0:T(8,128)(2,1)S(1)} %bitcast.14), channel_id=1, replica_groups={{0,1,2,3,4,5,6,7,16,17,18,19,20,21,22,23},{8,9,10,11,12,13,14,15,24,25,..., dimensions={0} | all-to-all | bytes 262144 | tf_op jit(solution)/shard_map/all_to_all | solution.py:731
  34.1 10.6 %all_to_all.11 = bf16[16,32,128]{2,1,0:T(8,128)(2,1)S(1)} all-to-all(bf16[16,32,128]{2,1,0:T(8,128)(2,1)S(1)} %gradient_sum.3), channel_id=1, replica_groups={{0,1,2,3,4,5,6,7,16,17,18,19,20,21,22,23},{8,9,10,11,12,13,14,15,24,25,..., dimensions={0} | all-to-all | bytes 262144 | tf_op jit(solution)/shard_map/all_to_all | solution.py:731
  44.7 0.0 collective-permute-start.6
  44.7 1.3 %collective-permute-done.6.other_ref = bf16[512,128]{1,0:T(8,128)(2,1)S(1)} collective-permute-done((bf16[512,128]{1,0:T(8,128)(2,1)S(1)}, bf16[512,128]{1,0:T(8,128)(2,1)S(1)}, u32[]{:S(2)}, u32[]{:S(2)}) %collective-permute-start.6) | collective-permute-done | bytes 131104 | tf_op jit(solution)/shard_map/ppermute | solution.py:722
  46.1 1.3 %unpack_gradients.1 = (f32[27,48,48]{2,1,0:T(8,128)}, f32[27,48,48]{2,1,0:T(8,128)}, f32[3,48]{1,0:T(4,128)}, f32[3,1,512]{2,1,0:T(1,128)}) custom-call(bf16[512,128]{1,0:T(8,128)(2,1)S(1)} %bitcast.16, bf16[512,128]{1,0:T(8,128)(2,1)S(1)} %collective-permute-done.6.other_ref, f32[8,512]{1,0:T(8,128)S(1)} %get-tuple-element.39.logits_ref), custom_call_target="tpu_custom_call" | custom-call | tf_op jit(solution)/shard_map/unpack_gradients/pallas_call | solution.py:749
  (3 shorter events, 0.1 us)
Async XLA Ops:
  0.6 6.8 %collective-permute-start = (bf16[1,1,48,512]{3,2,1,0:T(8,128)(2,1)}, bf16[1,1,48,512]{3,2,1,0:T(8,128)(2,1)S(1)}, u32[]{:S(2)}, u32[]{:S(2)}) collective-permute-start(bf16[1,1,48,512]{3,2,1,0:T(8,128)(2,1)} %param.6), channel_id=1, source_target_pairs={{0,1},{1,0},{2,3},{3,2},{4,5},{5,4},{6,7},{7,6},{8,9},{9,8},{10,11... | collective-permute-start | bytes 147464 | tf_op jit(solution)/shard_map/ppermute | solution.py:626
  3.6 0.7 %copy-start.3 = (s32[1,1,3,512]{3,1,2,0:T(1,128)S(1)}, s32[1,1,3,512]{3,1,2,0:T(1,128)}, u32[]{:S(2)}) copy-start(s32[1,1,3,512]{3,1,2,0:T(1,128)} %param.11) | copy-start | bytes 18436
  3.6 3.8 %collective-permute-start.1 = (s32[1,1,3,512]{3,0,2,1:T(1,128)}, s32[1,1,3,512]{3,0,2,1:T(1,128)S(1)}, u32[]{:S(2)}, u32[]{:S(2)}) collective-permute-start(s32[1,1,3,512]{3,0,2,1:T(1,128)} %bitcast.22), channel_id=1, source_target_pairs={{0,1},{1,0},{2,3},{3,2},{4,5},{5,4},{6,7},{7,6},{8,9},{9,8},{10,11... | collective-permute-start | bytes 18440 | tf_op jit(solution)/shard_map/ppermute | solution.py:626
  3.7 0.7 %copy-start.4 = (s32[1,8]{1,0:T(1,128)S(1)}, s32[1,8]{1,0:T(1,128)}, u32[]{:S(2)}) copy-start(s32[1,8]{1,0:T(1,128)} %block_ref.5) | copy-start | bytes 100
  4.4 0.8 %copy-start.2 = (bf16[1,1,48,512]{3,2,1,0:T(8,128)(2,1)S(1)}, bf16[1,1,48,512]{3,2,1,0:T(8,128)(2,1)}, u32[]{:S(2)}) copy-start(bf16[1,1,48,512]{3,2,1,0:T(8,128)(2,1)} %param.6) | copy-start | bytes 147460
  7.6 7.1 %collective-permute-start.2 = (bf16[2,8,16,128]{3,2,1,0:T(8,128)(2,1)S(1)}, bf16[2,8,16,128]{3,2,1,0:T(8,128)(2,1)S(1)}, u32[]{:S(2)}, u32[]{:S(2)}) collective-permute-start(bf16[2,8,16,128]{3,2,1,0:T(8,128)(2,1)S(1)} %get-tuple-element.29), channel_id=1, source_target_pairs={{0,4},{1,5},{2,6},{3,7},{4,0},{5,1},{6,2},{7,3},{8,12},{9,13},{10,... | collective-permute-start | bytes 196616 | tf_op jit(solution)/shard_map/ppermute | solution.py:626
  10.3 1.6 %copy-start.5 = (bf16[3,48]{1,0:T(4,128)(2,1)S(1)}, bf16[3,48]{1,0:T(4,128)(2,1)}, u32[]{:S(2)}) copy-start(bf16[3,48]{1,0:T(4,128)(2,1)} %head_ref.1) | copy-start | bytes 868
  10.3 6.2 %collective-permute-start.3 = (bf16[2,8,16,128]{3,2,1,0:T(8,128)(2,1)S(1)}, bf16[2,8,16,128]{3,2,1,0:T(8,128)(2,1)S(1)}, u32[]{:S(2)}, u32[]{:S(2)}) collective-permute-start(bf16[2,8,16,128]{3,2,1,0:T(8,128)(2,1)S(1)} %get-tuple-element.30), channel_id=1, source_target_pairs={{0,6},{1,7},{2,4},{3,5},{4,2},{5,3},{6,0},{7,1},{8,14},{9,15},{10,... | collective-permute-start | bytes 196616 | tf_op jit(solution)/shard_map/ppermute | solution.py:626
  11.7 5.0 %collective-permute-start.4 = (bf16[2,8,16,128]{3,2,1,0:T(8,128)(2,1)S(1)}, bf16[2,8,16,128]{3,2,1,0:T(8,128)(2,1)S(1)}, u32[]{:S(2)}, u32[]{:S(2)}) collective-permute-start(bf16[2,8,16,128]{3,2,1,0:T(8,128)(2,1)S(1)} %get-tuple-element.31), channel_id=1, source_target_pairs={{0,2},{1,3},{2,0},{3,1},{4,6},{5,7},{6,4},{7,5},{8,10},{9,11},{10,... | collective-permute-start | bytes 196616 | tf_op jit(solution)/shard_map/ppermute | solution.py:626
  12.0 1.0 %copy-start = (bf16[48,27,48]{2,0,1:T(8,128)(2,1)S(1)}, bf16[48,27,48]{2,0,1:T(8,128)(2,1)}, u32[]{:S(2)}) copy-start(bf16[48,27,48]{2,0,1:T(8,128)(2,1)} %param.8) | copy-start | bytes 373252
  12.9 1.0 %copy-start.1 = (bf16[48,27,48]{2,0,1:T(8,128)(2,1)S(1)}, bf16[48,27,48]{2,0,1:T(8,128)(2,1)}, u32[]{:S(2)}) copy-start(bf16[48,27,48]{2,0,1:T(8,128)(2,1)} %param.9) | copy-start | bytes 373252
  20.3 1.6 %collective-permute-start.5 = (f32[512,128]{1,0:T(8,128)S(1)}, f32[512,128]{1,0:T(8,128)S(1)}, u32[]{:S(2)}, u32[]{:S(2)}) collective-permute-start(f32[512,128]{1,0:T(8,128)S(1)} %get-tuple-element.38), channel_id=1, source_target_pairs={{0,8},{8,0},{16,24},{24,16},{1,9},{9,1},{17,25},{25,17},{2,10},{10... | collective-permute-start | bytes 786440 | tf_op jit(solution)/shard_map/ppermute | solution.py:722
  44.7 1.3 %collective-permute-start.6 = (bf16[512,128]{1,0:T(8,128)(2,1)S(1)}, bf16[512,128]{1,0:T(8,128)(2,1)S(1)}, u32[]{:S(2)}, u32[]{:S(2)}) collective-permute-start(bf16[512,128]{1,0:T(8,128)(2,1)S(1)} %bitcast.15), channel_id=1, source_target_pairs={{0,8},{8,0},{16,24},{24,16},{1,9},{9,1},{17,25},{25,17},{2,10},{10... | collective-permute-start | bytes 393224 | tf_op jit(solution)/shard_map/ppermute | solution.py:722

commit v11 on v10

--- a/solution.py
+++ b/solution.py
@@ -193,7 +193,7 @@
     return (target >> 2) - (source >> 2), (target & 3) - (source & 3)
 
 
-PARTNERS = (4, 6, 2)
+PARTNERS = (6, 4, 2)
 
 
 def block_tiles(features_ref, targets_ref):

time: 47.7 us -> 47.5 us (level)
  transfers between devices with their start and end apart: 7 -> 7, of which waited for: 6 -> 4; matrix products, arithmetic and copies ran while one was open for 0% -> 0% of each run, Pallas kernels for 1% -> 1%
where the time goes in v11:
time: 47.5 us; the launch traced here: 47.2 us
  blocking collectives  22.6 us (48%)
  starting transfers between devices  7.62 us (16%)
  waiting for transfers between devices  7.2 us (15%)
  Pallas kernels  5.82 us (12%)
  local copies, waits for them, and re-layouts  3.19 us (7%)
  between operations  0.71 us (1%)
    all_to_all x2, blocking collectives, exchange(): lax.all_to_all(values, ('dp', 'space'), 0, 0, axis_index_groups=groups, t...  22.6 us
    ppermute x5, starting transfers between devices, swap(): lax.ppermute(values, 'space', [(s, s ^ mask) for s in range(space_count)])  7.54 us
    ppermute x5, waiting for transfers between devices, swap(): lax.ppermute(values, 'space', [(s, s ^ mask) for s in range(space_count)])  4.34 us
    pallas_call x1, Pallas kernels, on_device_flat(): pl.pallas_call(functools.partial(crop_kernel, scale), out_shape=(shape((8...  3.64 us
    unnamed x12, local copies, waits for them, and re-layouts  3.19 us
    ppermute x2, waiting for transfers between devices, swap_cores(): return lax.ppermute(values, 'dp', [(d, d ^ 1) for d in range(dp_count)])  2.87 us
    pallas_call x1, Pallas kernels, on_device_flat(): pl.pallas_call(unpack_kernel, out_shape=(shape((27, C, C), f32), shape((2...  1.28 us
  transfers between devices with their start and end apart: 7, of which 4 were waited for; matrix products, arithmetic and copies ran while one was open for 0% of the time, Pallas kernels for 1%

profile of v11, /device:TPU:0, one launch (start us, length us, event | category | flops | bytes accessed | tf_op | source)
XLA Modules:
  0.0 47.2 jit_solution(3505327624490012218)
XLA Ops:
  0.6 3.0 %collective-permute-start = (bf16[1,1,48,512]{3,2,1,0:T(8,128)(2,1)}, bf16[1,1,48,512]{3,2,1,0:T(8,128)(2,1)S(1)}, u32[]{:S(2)}, u32[]{:S(2)}) collective-permute-start(bf16[1,1,48,512]{3,2,1,0:T(8,128)(2,1)} %param.6), channel_id=1, source_target_pairs={{0,1},{1,0},{2,3},{3,2},{4,5},{5,4},{6,7},{7,6},{8,9},{9,8},{10,11... | collective-permute-start | bytes 147464 | tf_op jit(solution)/shard_map/ppermute | solution.py:626
  3.6 0.0 copy-start.3
  3.6 0.1 collective-permute-start.1
  3.7 0.0 copy-start.4
  3.7 0.6 %copy-done.3 = s32[1,1,3,512]{3,1,2,0:T(1,128)S(1)} copy-done((s32[1,1,3,512]{3,1,2,0:T(1,128)S(1)}, s32[1,1,3,512]{3,1,2,0:T(1,128)}, u32[]{:S(2)}) %copy-start.3) | copy-done | bytes 6168
  4.3 0.1 copy-done.4
  4.4 0.0 copy-start.2
  4.4 0.8 %copy-done.2 = bf16[1,1,48,512]{3,2,1,0:T(8,128)(2,1)S(1)} copy-done((bf16[1,1,48,512]{3,2,1,0:T(8,128)(2,1)S(1)}, bf16[1,1,48,512]{3,2,1,0:T(8,128)(2,1)}, u32[]{:S(2)}) %copy-start.2) | copy-done | bytes 49176
  5.2 0.2 pack_own.1
  5.3 2.1 %collective-permute-done.1 = s32[1,1,3,512]{3,0,2,1:T(1,128)S(1)} collective-permute-done((s32[1,1,3,512]{3,0,2,1:T(1,128)}, s32[1,1,3,512]{3,0,2,1:T(1,128)S(1)}, u32[]{:S(2)}, u32[]{:S(2)}) %collective-permute-start.1) | collective-permute-done | bytes 6176 | tf_op jit(solution)/shard_map/ppermute | solution.py:626
  7.5 0.0 collective-permute-done
  7.5 0.2 pack_mate.1
  7.6 3.7 %collective-permute-start.2 = (bf16[2,8,16,128]{3,2,1,0:T(8,128)(2,1)S(1)}, bf16[2,8,16,128]{3,2,1,0:T(8,128)(2,1)S(1)}, u32[]{:S(2)}, u32[]{:S(2)}) collective-permute-start(bf16[2,8,16,128]{3,2,1,0:T(8,128)(2,1)S(1)} %get-tuple-element.29), channel_id=1, source_target_pairs={{0,6},{1,7},{2,4},{3,5},{4,2},{5,3},{6,0},{7,1},{8,14},{9,15},{10,... | collective-permute-start | bytes 196616 | tf_op jit(solution)/shard_map/ppermute | solution.py:626
  11.3 0.0 copy-start.5
  11.3 0.0 collective-permute-start.3
  11.3 0.8 %collective-permute-start.4 = (bf16[2,8,16,128]{3,2,1,0:T(8,128)(2,1)S(1)}, bf16[2,8,16,128]{3,2,1,0:T(8,128)(2,1)S(1)}, u32[]{:S(2)}, u32[]{:S(2)}) collective-permute-start(bf16[2,8,16,128]{3,2,1,0:T(8,128)(2,1)S(1)} %get-tuple-element.31), channel_id=1, source_target_pairs={{0,2},{1,3},{2,0},{3,1},{4,6},{5,7},{6,4},{7,5},{8,10},{9,11},{10,... | collective-permute-start | bytes 196616 | tf_op jit(solution)/shard_map/ppermute | solution.py:626
  12.1 0.0 copy-done.5
  12.1 0.1 lay_out_head.1
  12.2 0.0 copy-start
  12.2 1.0 %copy-done = bf16[48,27,48]{2,0,1:T(8,128)(2,1)S(1)} copy-done((bf16[48,27,48]{2,0,1:T(8,128)(2,1)S(1)}, bf16[48,27,48]{2,0,1:T(8,128)(2,1)}, u32[]{:S(2)}) %copy-start) | copy-done | bytes 124440
  13.2 0.0 copy-start.1
  13.2 0.2 prepare.1
  13.4 0.8 %copy-done.1 = bf16[48,27,48]{2,0,1:T(8,128)(2,1)S(1)} copy-done((bf16[48,27,48]{2,0,1:T(8,128)(2,1)S(1)}, bf16[48,27,48]{2,0,1:T(8,128)(2,1)}, u32[]{:S(2)}) %copy-start.1) | copy-done | bytes 124440
  14.1 0.2 second_weights.1
  14.4 0.0 collective-permute-done.2.refs_0_
  14.4 2.2 %collective-permute-done.3.refs_1_ = bf16[2,8,16,128]{3,2,1,0:T(8,128)(2,1)S(1)} collective-permute-done((bf16[2,8,16,128]{3,2,1,0:T(8,128)(2,1)S(1)}, bf16[2,8,16,128]{3,2,1,0:T(8,128)(2,1)S(1)}, u32[]{:S(2)}, u32[]{:S(2)}) %collective-permute-start.3) | collective-permute-done | bytes 65568 | tf_op jit(solution)/shard_map/ppermute | solution.py:626
  16.6 0.0 collective-permute-done.4.refs_2_
  16.6 3.6 %forward_backward.1 = (f32[8,512]{1,0:T(8,128)S(1)}, f32[512,128]{1,0:T(8,128)S(1)}, f32[512,128]{1,0:T(8,128)S(1)}) custom-call(s32[1,128]{1,0:T(1,128)S(1)} %get-tuple-element.24.owners_ref, f32[8,128]{1,0:T(8,128)S(1)} %get-tuple-element.25.masks_ref, bf16[13,16,128]{2,1,0:T(8,128)(2,1)S(1)} %get-tuple-element.26.own_ref, ...), custom_call_target="tpu_custom_call" | custom-call | tf_op jit(solution)/shard_map/forward_backward/pallas_call | solution.py:696
  20.2 0.1 collective-permute-start.5
  20.3 1.5 %collective-permute-done.5.other_ref = f32[512,128]{1,0:T(8,128)S(1)} collective-permute-done((f32[512,128]{1,0:T(8,128)S(1)}, f32[512,128]{1,0:T(8,128)S(1)}, u32[]{:S(2)}, u32[]{:S(2)}) %collective-permute-start.5) | collective-permute-done | bytes 262176 | tf_op jit(solution)/shard_map/ppermute | solution.py:722
  21.9 12.0 %all_to_all.10.parts_ref = bf16[16,32,128]{2,1,0:T(8,128)(2,1)S(1)} all-to-all(bf16[16,32,128]{2,1,0:T(8,128)(2,1)S(1)} %bitcast.14), channel_id=1, replica_groups={{0,1,2,3,4,5,6,7,16,17,18,19,20,21,22,23},{8,9,10,11,12,13,14,15,24,25,..., dimensions={0} | all-to-all | bytes 262144 | tf_op jit(solution)/shard_map/all_to_all | solution.py:731
  33.9 10.6 %all_to_all.11 = bf16[16,32,128]{2,1,0:T(8,128)(2,1)S(1)} all-to-all(bf16[16,32,128]{2,1,0:T(8,128)(2,1)S(1)} %gradient_sum.3), channel_id=1, replica_groups={{0,1,2,3,4,5,6,7,16,17,18,19,20,21,22,23},{8,9,10,11,12,13,14,15,24,25,..., dimensions={0} | all-to-all | bytes 262144 | tf_op jit(solution)/shard_map/all_to_all | solution.py:731
  44.6 0.0 collective-permute-start.6
  44.6 1.3 %collective-permute-done.6.other_ref = bf16[512,128]{1,0:T(8,128)(2,1)S(1)} collective-permute-done((bf16[512,128]{1,0:T(8,128)(2,1)S(1)}, bf16[512,128]{1,0:T(8,128)(2,1)S(1)}, u32[]{:S(2)}, u32[]{:S(2)}) %collective-permute-start.6) | collective-permute-done | bytes 131104 | tf_op jit(solution)/shard_map/ppermute | solution.py:722
  45.9 1.3 %unpack_gradients.1 = (f32[27,48,48]{2,1,0:T(8,128)}, f32[27,48,48]{2,1,0:T(8,128)}, f32[3,48]{1,0:T(4,128)}, f32[3,1,512]{2,1,0:T(1,128)}) custom-call(bf16[512,128]{1,0:T(8,128)(2,1)S(1)} %bitcast.16, bf16[512,128]{1,0:T(8,128)(2,1)S(1)} %collective-permute-done.6.other_ref, f32[8,512]{1,0:T(8,128)S(1)} %get-tuple-element.39.logits_ref), custom_call_target="tpu_custom_call" | custom-call | tf_op jit(solution)/shard_map/unpack_gradients/pallas_call | solution.py:749
  (3 shorter events, 0.1 us)
Async XLA Ops:
  0.6 6.8 %collective-permute-start = (bf16[1,1,48,512]{3,2,1,0:T(8,128)(2,1)}, bf16[1,1,48,512]{3,2,1,0:T(8,128)(2,1)S(1)}, u32[]{:S(2)}, u32[]{:S(2)}) collective-permute-start(bf16[1,1,48,512]{3,2,1,0:T(8,128)(2,1)} %param.6), channel_id=1, source_target_pairs={{0,1},{1,0},{2,3},{3,2},{4,5},{5,4},{6,7},{7,6},{8,9},{9,8},{10,11... | collective-permute-start | bytes 147464 | tf_op jit(solution)/shard_map/ppermute | solution.py:626
  3.6 0.7 %copy-start.3 = (s32[1,1,3,512]{3,1,2,0:T(1,128)S(1)}, s32[1,1,3,512]{3,1,2,0:T(1,128)}, u32[]{:S(2)}) copy-start(s32[1,1,3,512]{3,1,2,0:T(1,128)} %param.11) | copy-start | bytes 18436
  3.6 3.8 %collective-permute-start.1 = (s32[1,1,3,512]{3,0,2,1:T(1,128)}, s32[1,1,3,512]{3,0,2,1:T(1,128)S(1)}, u32[]{:S(2)}, u32[]{:S(2)}) collective-permute-start(s32[1,1,3,512]{3,0,2,1:T(1,128)} %bitcast.22), channel_id=1, source_target_pairs={{0,1},{1,0},{2,3},{3,2},{4,5},{5,4},{6,7},{7,6},{8,9},{9,8},{10,11... | collective-permute-start | bytes 18440 | tf_op jit(solution)/shard_map/ppermute | solution.py:626
  3.7 0.7 %copy-start.4 = (s32[1,8]{1,0:T(1,128)S(1)}, s32[1,8]{1,0:T(1,128)}, u32[]{:S(2)}) copy-start(s32[1,8]{1,0:T(1,128)} %block_ref.5) | copy-start | bytes 100
  4.4 0.8 %copy-start.2 = (bf16[1,1,48,512]{3,2,1,0:T(8,128)(2,1)S(1)}, bf16[1,1,48,512]{3,2,1,0:T(8,128)(2,1)}, u32[]{:S(2)}) copy-start(bf16[1,1,48,512]{3,2,1,0:T(8,128)(2,1)} %param.6) | copy-start | bytes 147460
  7.6 6.7 %collective-permute-start.2 = (bf16[2,8,16,128]{3,2,1,0:T(8,128)(2,1)S(1)}, bf16[2,8,16,128]{3,2,1,0:T(8,128)(2,1)S(1)}, u32[]{:S(2)}, u32[]{:S(2)}) collective-permute-start(bf16[2,8,16,128]{3,2,1,0:T(8,128)(2,1)S(1)} %get-tuple-element.29), channel_id=1, source_target_pairs={{0,6},{1,7},{2,4},{3,5},{4,2},{5,3},{6,0},{7,1},{8,14},{9,15},{10,... | collective-permute-start | bytes 196616 | tf_op jit(solution)/shard_map/ppermute | solution.py:626
  11.3 0.8 %copy-start.5 = (bf16[3,48]{1,0:T(4,128)(2,1)S(1)}, bf16[3,48]{1,0:T(4,128)(2,1)}, u32[]{:S(2)}) copy-start(bf16[3,48]{1,0:T(4,128)(2,1)} %head_ref.1) | copy-start | bytes 868
  11.3 5.3 %collective-permute-start.3 = (bf16[2,8,16,128]{3,2,1,0:T(8,128)(2,1)S(1)}, bf16[2,8,16,128]{3,2,1,0:T(8,128)(2,1)S(1)}, u32[]{:S(2)}, u32[]{:S(2)}) collective-permute-start(bf16[2,8,16,128]{3,2,1,0:T(8,128)(2,1)S(1)} %get-tuple-element.30), channel_id=1, source_target_pairs={{0,4},{1,5},{2,6},{3,7},{4,0},{5,1},{6,2},{7,3},{8,12},{9,13},{10,... | collective-permute-start | bytes 196616 | tf_op jit(solution)/shard_map/ppermute | solution.py:626
  11.3 5.3 %collective-permute-start.4 = (bf16[2,8,16,128]{3,2,1,0:T(8,128)(2,1)S(1)}, bf16[2,8,16,128]{3,2,1,0:T(8,128)(2,1)S(1)}, u32[]{:S(2)}, u32[]{:S(2)}) collective-permute-start(bf16[2,8,16,128]{3,2,1,0:T(8,128)(2,1)S(1)} %get-tuple-element.31), channel_id=1, source_target_pairs={{0,2},{1,3},{2,0},{3,1},{4,6},{5,7},{6,4},{7,5},{8,10},{9,11},{10,... | collective-permute-start | bytes 196616 | tf_op jit(solution)/shard_map/ppermute | solution.py:626
  12.2 1.0 %copy-start = (bf16[48,27,48]{2,0,1:T(8,128)(2,1)S(1)}, bf16[48,27,48]{2,0,1:T(8,128)(2,1)}, u32[]{:S(2)}) copy-start(bf16[48,27,48]{2,0,1:T(8,128)(2,1)} %param.8) | copy-start | bytes 373252
  13.2 1.0 %copy-start.1 = (bf16[48,27,48]{2,0,1:T(8,128)(2,1)S(1)}, bf16[48,27,48]{2,0,1:T(8,128)(2,1)}, u32[]{:S(2)}) copy-start(bf16[48,27,48]{2,0,1:T(8,128)(2,1)} %param.9) | copy-start | bytes 373252
  20.2 1.6 %collective-permute-start.5 = (f32[512,128]{1,0:T(8,128)S(1)}, f32[512,128]{1,0:T(8,128)S(1)}, u32[]{:S(2)}, u32[]{:S(2)}) collective-permute-start(f32[512,128]{1,0:T(8,128)S(1)} %get-tuple-element.38), channel_id=1, source_target_pairs={{0,8},{8,0},{16,24},{24,16},{1,9},{9,1},{17,25},{25,17},{2,10},{10... | collective-permute-start | bytes 786440 | tf_op jit(solution)/shard_map/ppermute | solution.py:722
  44.6 1.3 %collective-permute-start.6 = (bf16[512,128]{1,0:T(8,128)(2,1)S(1)}, bf16[512,128]{1,0:T(8,128)(2,1)S(1)}, u32[]{:S(2)}, u32[]{:S(2)}) collective-permute-start(bf16[512,128]{1,0:T(8,128)(2,1)S(1)} %bitcast.15), channel_id=1, source_target_pairs={{0,8},{8,0},{16,24},{24,16},{1,9},{9,1},{17,25},{25,17},{2,10},{10... | collective-permute-start | bytes 393224 | tf_op jit(solution)/shard_map/ppermute | solution.py:722
